TPU v7x, 32 devices: a whole 2x2x4 slice. The times are simulated.
32 devices in a mesh: dp: 8 (over z, y), fsdp: 4 (over x, core).
Axes of the slice: x: 2, y: 2, z: 4, core: 2. Of those that a mesh axis runs over, the one named last changes fastest.
Arguments:
- inputs: bfloat16 [4, 4096, 768], P(None, ('dp', 'fsdp')), may hold values from -6 to 6
- segments: int32 [4, 4096], P(None, 'dp'), may hold values from 0 to 1, as said below
- norm1_gain: bfloat16 [768], P(('dp', 'fsdp')), may hold values from 0.5 to 1.5
- norm1_bias: bfloat16 [768], P(('dp', 'fsdp')), may hold values from -0.59765625 to 0.59765625
- qkv_weight: bfloat16 [768, 2304], P(('dp', 'fsdp')), may hold values from -0.21875 to 0.21875
- query_bias: bfloat16 [768], P(('dp', 'fsdp')), may hold values from -0.59765625 to 0.59765625
- value_bias: bfloat16 [768], P(('dp', 'fsdp')), may hold values from -0.1796875 to 0.1796875
- out_weight: bfloat16 [768, 768], P(('dp', 'fsdp')), may hold values from -3.5 to 3.5
- out_bias: bfloat16 [768], P(('dp', 'fsdp')), may hold values from -0.59765625 to 0.59765625
- norm2_gain: bfloat16 [768], P(('dp', 'fsdp')), may hold values from 0.5 to 1.5
- norm2_bias: bfloat16 [768], P(('dp', 'fsdp')), may hold values from -0.59765625 to 0.59765625
- up_weight: bfloat16 [768, 3072], P(('dp', 'fsdp')), may hold values from -0.21875 to 0.21875
- up_bias: bfloat16 [3072], P(('dp', 'fsdp')), may hold values from -0.59765625 to 0.59765625
- down_weight: bfloat16 [3072, 768], P(('dp', 'fsdp')), may hold values from -0.109375 to 0.109375
- down_bias: bfloat16 [768], P(('dp', 'fsdp')), may hold values from -0.59765625 to 0.59765625
- cotangent: bfloat16 [4, 4096, 768], P(None, ('dp', 'fsdp')), may hold values from -6 to 6
Outputs:
- output: bfloat16 [4, 4096, 768], P(None, ('dp', 'fsdp'))
- input_grad: float32 [4, 4096, 768], P(None, ('dp', 'fsdp'))
- grad_norm1_gain: float32 [768], P(('dp', 'fsdp'))
- grad_norm1_bias: float32 [768], P(('dp', 'fsdp'))
- grad_qkv_weight: float32 [768, 2304], P(('dp', 'fsdp'))
- grad_query_bias: float32 [768], P(('dp', 'fsdp'))
- grad_value_bias: float32 [768], P(('dp', 'fsdp'))
- grad_out_weight: float32 [768, 768], P(('dp', 'fsdp'))
- grad_out_bias: float32 [768], P(('dp', 'fsdp'))
- grad_norm2_gain: float32 [768], P(('dp', 'fsdp'))
- grad_norm2_bias: float32 [768], P(('dp', 'fsdp'))
- grad_up_weight: float32 [768, 3072], P(('dp', 'fsdp'))
- grad_up_bias: float32 [3072], P(('dp', 'fsdp'))
- grad_down_weight: float32 [3072, 768], P(('dp', 'fsdp'))
- grad_down_bias: float32 [768], P(('dp', 'fsdp'))
Inputs may be any that keep to these rules, and one draw needn't show every extreme that they name: `segments`: in each micro-batch each index of dp holds two clips numbered 0 and 1. List the group's 512 tokens by their row within a device first and their index of fsdp second: clip 0 comes first, then clip 1. Clip 0 ends after 512 // 2 tokens of this list, moved by at most 32 either way, so that every clip has tokens on every device of fsdp.
All inputs are finite; a program needn't handle non-finite values.
Results may differ from a plain program's by a relative error of at most 0.013.
Values may be sent and summed in bfloat16 or wider, within the bound.
No kernel may reach another device: no remote copies, remote signals or barrier semaphores. Data moves between devices by JAX's collectives and lax.ppermute only.
A program may use at most 256 MiB of HBM per device.

v0:
```python
import math

import jax
import jax.numpy as jnp
from jax import lax
from jax.sharding import PartitionSpec as P

HEADS = 12


EPSILON = 1e-06
NEG_LARGE = -1e30
SCALE_SCORE = 0.125


def layer_norm(values, gain_vec, shift_vec):
    centre = values - jnp.mean(values, -1, keepdims=True)
    spread = jnp.mean(centre * centre, -1, keepdims=True)
    return centre * lax.rsqrt(spread + EPSILON) * gain_vec + shift_vec


def gelu_tanh(values):
    return (
        0.5
        * values
        * (1.0 + jnp.tanh(0.7978845608028654 * (values + 0.044715 * values * values * values)))
    )


def add_terms(first_terms, second_terms):
    if first_terms is None:
        return second_terms
    return jax.tree.map(jnp.add, first_terms, second_terms)


def on_device(
    inputs,
    segments,
    norm1_gain,
    norm1_bias,
    qkv_weight,
    query_bias,
    value_bias,
    out_weight,
    out_bias,
    norm2_gain,
    norm2_bias,
    up_weight,
    up_bias,
    down_weight,
    down_bias,
    cotangent,
):
    micro_count = inputs.shape[0]
    local_rows = inputs.shape[1]
    model_width = inputs.shape[2]
    group_rows = segments.shape[1]
    key_rows = math.gcd(512, group_rows)
    key_count = group_rows // key_rows
    offset = lax.axis_index("fsdp") * local_rows
    f32 = jnp.float32
    bf16 = jnp.bfloat16
    outputs = []
    in_grads = []
    totals = None
    for micro_index in range(micro_count):
        params_fwd = (
            lax.all_gather(norm1_gain, ("dp", "fsdp"), axis=0, tiled=True),
            lax.all_gather(norm1_bias, ("dp", "fsdp"), axis=0, tiled=True),
            lax.all_gather(qkv_weight, ("dp", "fsdp"), axis=0, tiled=True),
            lax.all_gather(query_bias, ("dp", "fsdp"), axis=0, tiled=True),
            lax.all_gather(value_bias, ("dp", "fsdp"), axis=0, tiled=True),
            lax.all_gather(out_weight, ("dp", "fsdp"), axis=0, tiled=True),
            lax.all_gather(out_bias, ("dp", "fsdp"), axis=0, tiled=True),
            lax.all_gather(norm2_gain, ("dp", "fsdp"), axis=0, tiled=True),
            lax.all_gather(norm2_bias, ("dp", "fsdp"), axis=0, tiled=True),
            lax.all_gather(up_weight, ("dp", "fsdp"), axis=0, tiled=True),
            lax.all_gather(up_bias, ("dp", "fsdp"), axis=0, tiled=True),
            lax.all_gather(down_weight, ("dp", "fsdp"), axis=0, tiled=True),
            lax.all_gather(down_bias, ("dp", "fsdp"), axis=0, tiled=True),
        )
        (
            gain_one,
            shift_one,
            qkv_full,
            bias_query,
            bias_value,
            out_full,
            bias_out,
            gain_two,
            shift_two,
            up_full,
            bias_up,
            down_full,
            bias_down,
        ) = params_fwd
        resid_in = inputs[micro_index].astype(f32)
        normed_one = layer_norm(resid_in, gain_one.astype(f32), shift_one.astype(f32)).astype(bf16)
        project = jnp.dot(normed_one, qkv_full, preferred_element_type=f32)
        queries = (project[:, :model_width] + bias_query.astype(f32)).astype(bf16)
        keys_local = project[:, model_width : 2 * model_width].astype(bf16)
        values_local = (project[:, 2 * model_width :] + bias_value.astype(f32)).astype(bf16)
        keys_all, values_all = (
            lax.all_gather(keys_local, "fsdp", axis=0, tiled=True),
            lax.all_gather(values_local, "fsdp", axis=0, tiled=True),
        )
        labels_all = segments[micro_index]
        labels_query = lax.dynamic_slice_in_dim(labels_all, offset, local_rows)
        query_heads = queries.reshape(local_rows, HEADS, -1)
        key_blocks = keys_all.reshape(key_count, key_rows, HEADS, -1)
        value_blocks = values_all.reshape(key_count, key_rows, HEADS, -1)
        label_blocks = labels_all.reshape(key_count, key_rows)

        def block_scores(key_block, label_block):
            scores = (
                jnp.einsum("qhd,khd->hqk", query_heads, key_block, preferred_element_type=f32)
                * SCALE_SCORE
            )
            allowed = (labels_query[:, None] == label_block[None, :])[None]
            return (jnp.where(allowed, scores, NEG_LARGE), allowed)

        def stat_step(state_in, pieces):
            running_max, running_sum = state_in
            scores, allowed = block_scores(pieces[0], pieces[1])
            newmax = jnp.maximum(running_max, jnp.max(scores, -1))
            exponent = jnp.where(allowed, jnp.exp(scores - newmax[..., None]), 0.0)
            running_sum = running_sum * jnp.exp(running_max - newmax) + jnp.sum(exponent, -1)
            return ((newmax, running_sum), None)

        start_state = (
            jnp.full((HEADS, local_rows), NEG_LARGE, f32),
            jnp.zeros((HEADS, local_rows), f32),
        )
        (final_max, final_sum), _ = lax.scan(stat_step, start_state, (key_blocks, label_blocks))
        log_total = final_max + jnp.log(final_sum)

        def block_prob(key_block, label_block):
            scores, allowed = block_scores(key_block, label_block)
            attend_prob = jnp.where(allowed, jnp.exp(scores - log_total[..., None]), 0.0)
            return (attend_prob, attend_prob.astype(bf16))

        def mix_step(state_in, pieces):
            mixed_acc, extra_acc = state_in
            attend_prob, prob_low = block_prob(pieces[0], pieces[2])
            remainder = (attend_prob - prob_low.astype(f32)).astype(bf16)
            mixed_acc = mixed_acc + jnp.einsum(
                "hqk,khd->qhd", prob_low, pieces[1], preferred_element_type=f32
            )
            extra_acc = extra_acc + jnp.einsum(
                "hqk,khd->qhd", remainder, pieces[1], preferred_element_type=f32
            )
            return ((mixed_acc, extra_acc), None)

        zero_heads = jnp.zeros(query_heads.shape, f32)
        (mixed_heads, extra_heads), _ = lax.scan(
            mix_step, (zero_heads, zero_heads), (key_blocks, value_blocks, label_blocks)
        )
        mixed_low = mixed_heads.reshape(local_rows, model_width).astype(bf16)
        full_mix = mixed_heads + extra_heads
        resid_mid = (
            resid_in
            + jnp.dot(mixed_low, out_full, preferred_element_type=f32)
            + bias_out.astype(f32)
        )
        normed_two = layer_norm(resid_mid, gain_two.astype(f32), shift_two.astype(f32)).astype(bf16)
        pre_act = jnp.dot(normed_two, up_full, preferred_element_type=f32) + bias_up.astype(f32)
        hidden_low = gelu_tanh(pre_act).astype(bf16)
        result = (
            resid_mid
            + jnp.dot(hidden_low, down_full, preferred_element_type=f32)
            + bias_down.astype(f32)
        )
        outputs.append(result.astype(bf16))
        params_bwd = (
            lax.all_gather(norm1_gain, ("dp", "fsdp"), axis=0, tiled=True),
            lax.all_gather(norm1_bias, ("dp", "fsdp"), axis=0, tiled=True),
            lax.all_gather(qkv_weight, ("dp", "fsdp"), axis=0, tiled=True),
            lax.all_gather(query_bias, ("dp", "fsdp"), axis=0, tiled=True),
            lax.all_gather(value_bias, ("dp", "fsdp"), axis=0, tiled=True),
            lax.all_gather(out_weight, ("dp", "fsdp"), axis=0, tiled=True),
            lax.all_gather(out_bias, ("dp", "fsdp"), axis=0, tiled=True),
            lax.all_gather(norm2_gain, ("dp", "fsdp"), axis=0, tiled=True),
            lax.all_gather(norm2_bias, ("dp", "fsdp"), axis=0, tiled=True),
            lax.all_gather(up_weight, ("dp", "fsdp"), axis=0, tiled=True),
            lax.all_gather(up_bias, ("dp", "fsdp"), axis=0, tiled=True),
            lax.all_gather(down_weight, ("dp", "fsdp"), axis=0, tiled=True),
            lax.all_gather(down_bias, ("dp", "fsdp"), axis=0, tiled=True),
        )
        (
            gain_one_b,
            shift_one_b,
            qkv_back,
            bias_query_b,
            bias_value_b,
            out_back,
            bias_out_b,
            gain_two_b,
            shift_two_b,
            up_back,
            bias_up_b,
            down_back,
            bias_down_b,
        ) = params_bwd
        cot_low = cotangent[micro_index]
        cot_full = cot_low.astype(f32)
        grad_down = jnp.einsum("tf,td->fd", hidden_low, cot_low, preferred_element_type=f32)
        grad_bias_down = jnp.sum(cot_full, 0)
        grad_hidden = jnp.einsum("td,fd->tf", cot_low, down_back, preferred_element_type=f32)
        _, gelu_pull = jax.vjp(gelu_tanh, pre_act)
        grad_pre = gelu_pull(grad_hidden)[0].astype(bf16)
        grad_up = jnp.einsum("td,tf->df", normed_two, grad_pre, preferred_element_type=f32)
        grad_bias_up = jnp.sum(grad_pre.astype(f32), 0)
        grad_normed_two = jnp.einsum("tf,df->td", grad_pre, up_back, preferred_element_type=f32)
        _, norm_two_pull = jax.vjp(
            layer_norm, resid_mid, gain_two_b.astype(f32), shift_two_b.astype(f32)
        )
        grad_mid_part, grad_gain_two, grad_shift_two = norm_two_pull(grad_normed_two)
        grad_mid = cot_full + grad_mid_part
        branch_low = grad_mid.astype(bf16)
        grad_out = jnp.einsum("td,te->de", mixed_low, branch_low, preferred_element_type=f32)
        grad_bias_out = jnp.sum(branch_low.astype(f32), 0)
        grad_mixed = jnp.einsum(
            "te,de->td", branch_low, out_back, preferred_element_type=f32
        ).astype(bf16)
        grad_heads = grad_mixed.reshape(local_rows, HEADS, -1)
        delta = jnp.einsum("qhd,qhd->hq", grad_heads.astype(f32), full_mix)

        def grad_step(query_acc, pieces):
            key_block, value_block, label_block = pieces
            attend_prob, prob_low = block_prob(key_block, label_block)
            grad_prob = jnp.einsum(
                "qhd,khd->hqk", grad_heads, value_block, preferred_element_type=f32
            )
            grad_scores = (attend_prob * (grad_prob - delta[..., None]) * SCALE_SCORE).astype(bf16)
            query_acc = query_acc + jnp.einsum(
                "hqk,khd->qhd", grad_scores, key_block, preferred_element_type=f32
            )
            key_part = jnp.einsum(
                "hqk,qhd->khd", grad_scores, query_heads, preferred_element_type=f32
            )
            value_part = jnp.einsum(
                "hqk,qhd->khd", prob_low, grad_heads, preferred_element_type=f32
            )
            return (query_acc, (key_part, value_part))

        query_grad, (key_parts, value_parts) = lax.scan(
            grad_step, zero_heads, (key_blocks, value_blocks, label_blocks)
        )
        key_parts = key_parts.reshape(group_rows, model_width)
        value_parts = value_parts.reshape(group_rows, model_width)
        key_grad, value_grad = (
            lax.psum_scatter(
                key_parts.astype(jnp.bfloat16), "fsdp", scatter_dimension=0, tiled=True
            ).astype(jnp.float32),
            lax.psum_scatter(
                value_parts.astype(jnp.bfloat16), "fsdp", scatter_dimension=0, tiled=True
            ).astype(jnp.float32),
        )
        query_low = query_grad.reshape(local_rows, model_width).astype(bf16)
        key_low = key_grad.astype(bf16)
        value_low = value_grad.astype(bf16)
        grad_project = jnp.concatenate([query_low, key_low, value_low], 1)
        grad_qkv = jnp.einsum("td,te->de", normed_one, grad_project, preferred_element_type=f32)
        grad_bias_query = jnp.sum(query_low.astype(f32), 0)
        grad_bias_value = jnp.sum(value_low.astype(f32), 0)
        grad_normed_one = jnp.einsum(
            "te,de->td", grad_project, qkv_back, preferred_element_type=f32
        )
        _, norm_one_pull = jax.vjp(
            layer_norm, resid_in, gain_one_b.astype(f32), shift_one_b.astype(f32)
        )
        grad_in_part, grad_gain_one, grad_shift_one = norm_one_pull(grad_normed_one)
        in_grads.append(grad_mid + grad_in_part)
        local_terms = (
            grad_gain_one,
            grad_shift_one,
            grad_qkv,
            grad_bias_query,
            grad_bias_value,
            grad_out,
            grad_bias_out,
            grad_gain_two,
            grad_shift_two,
            grad_up,
            grad_bias_up,
            grad_down,
            grad_bias_down,
        )
        shard_terms = (
            lax.psum_scatter(local_terms[0], ("dp", "fsdp"), scatter_dimension=0, tiled=True),
            lax.psum_scatter(local_terms[1], ("dp", "fsdp"), scatter_dimension=0, tiled=True),
            lax.psum_scatter(local_terms[2], ("dp", "fsdp"), scatter_dimension=0, tiled=True),
            lax.psum_scatter(local_terms[3], ("dp", "fsdp"), scatter_dimension=0, tiled=True),
            lax.psum_scatter(local_terms[4], ("dp", "fsdp"), scatter_dimension=0, tiled=True),
            lax.psum_scatter(local_terms[5], ("dp", "fsdp"), scatter_dimension=0, tiled=True),
            lax.psum_scatter(local_terms[6], ("dp", "fsdp"), scatter_dimension=0, tiled=True),
            lax.psum_scatter(local_terms[7], ("dp", "fsdp"), scatter_dimension=0, tiled=True),
            lax.psum_scatter(local_terms[8], ("dp", "fsdp"), scatter_dimension=0, tiled=True),
            lax.psum_scatter(local_terms[9], ("dp", "fsdp"), scatter_dimension=0, tiled=True),
            lax.psum_scatter(local_terms[10], ("dp", "fsdp"), scatter_dimension=0, tiled=True),
            lax.psum_scatter(local_terms[11], ("dp", "fsdp"), scatter_dimension=0, tiled=True),
            lax.psum_scatter(local_terms[12], ("dp", "fsdp"), scatter_dimension=0, tiled=True),
        )
        totals = add_terms(totals, shard_terms)
    return (
        jnp.stack(outputs),
        jnp.stack(in_grads),
        totals[0],
        totals[1],
        totals[2],
        totals[3],
        totals[4],
        totals[5],
        totals[6],
        totals[7],
        totals[8],
        totals[9],
        totals[10],
        totals[11],
        totals[12],
    )


def solution(mesh):
    placed = (
        P(None, ("dp", "fsdp"), None),
        P(None, "dp"),
        P(("dp", "fsdp")),
        P(("dp", "fsdp")),
        P(("dp", "fsdp"), None),
        P(("dp", "fsdp")),
        P(("dp", "fsdp")),
        P(("dp", "fsdp"), None),
        P(("dp", "fsdp")),
        P(("dp", "fsdp")),
        P(("dp", "fsdp")),
        P(("dp", "fsdp"), None),
        P(("dp", "fsdp")),
        P(("dp", "fsdp"), None),
        P(("dp", "fsdp")),
        P(None, ("dp", "fsdp"), None),
    )
    return jax.shard_map(
        on_device,
        mesh=mesh,
        in_specs=placed,
        out_specs=(
            P(None, ("dp", "fsdp"), None),
            P(None, ("dp", "fsdp"), None),
            P(("dp", "fsdp")),
            P(("dp", "fsdp")),
            P(("dp", "fsdp"), None),
            P(("dp", "fsdp")),
            P(("dp", "fsdp")),
            P(("dp", "fsdp"), None),
            P(("dp", "fsdp")),
            P(("dp", "fsdp")),
            P(("dp", "fsdp")),
            P(("dp", "fsdp"), None),
            P(("dp", "fsdp")),
            P(("dp", "fsdp"), None),
            P(("dp", "fsdp")),
        ),
        check_vma=False,
    )
```

profile of v0, /device:TPU:0, one launch (start us, length us, event | category | flops | bytes accessed | tf_op | source)
XLA Modules:
  0.0 1080.5 jit_solution(11872704157543386618)
XLA Ops:
  16.3 42.8 %all-reduce.19 = (bf16[768]{0:T(1024)(128)(2,1)S(1)}, bf16[768]{0:T(1024)(128)(2,1)S(1)}, bf16[768]{0:T(1024)(128)(2,1)S(1)}, bf16[768]{0:T(1024)(128)(2,1)S(1)}...) all-reduce(bf16[768]{0:T(1024)(128)(2,1)S(1)} %dynamic-update-slice, ...), channel_id=1, replica_groups=mesh['dp'=8,'fsdp'=4] {'dp','fsdp'}, use_global_device_ids=true, to_apply=%add.1 | all-reduce | flops 9216 | bytes 36864
  64.2 9.7 all-gather.5.cloned.1.call-done
  77.9 9.1 all_gather.58
  91.9 9.2 all_gather.60
  106.6 8.7 all_gather.62
  115.6 9.6 all_gather.61
  125.6 8.7 all_gather.57
  135.5 9.0 all_gather.59
  164.5 31.9 %all-gather.9.cloned.1.call-done = bf16[768,3072]{1,0:T(8,128)(2,1)} async-done(((bf16[24,3072]{1,0:T(8,128)(2,1)}), bf16[768,3072]{1,0:T(8,128)(2,1)}) %all-gather.9.cloned.1.call-update) | async-done | bytes 4718608 | tf_op jit(solution)/shard_map/all_gather | solution.py:77
  200.8 60.9 %all-gather.11.cloned.1.call-done = bf16[3072,768]{1,0:T(8,128)(2,1)} async-done(((bf16[96,768]{1,0:T(8,128)(2,1)}), bf16[3072,768]{1,0:T(8,128)(2,1)}) %all-gather.11.cloned.1.call-update) | async-done | bytes 4718608 | tf_op jit(solution)/shard_map/all_gather | solution.py:79
  354.1 15.7 %reduce-scatter.51.cloned.1.call-done = bf16[128,768]{1,0:T(8,128)(2,1)} async-done(((bf16[512,768]{1,0:T(8,128)(2,1)}), bf16[128,768]{1,0:T(8,128)(2,1)}) %reduce-scatter.51.cloned.1.call-update) | async-done | bytes 196624
  370.8 24.9 %reduce-scatter.49.cloned.1.call-done = bf16[128,768]{1,0:T(8,128)(2,1)} async-done(((bf16[512,768]{1,0:T(8,128)(2,1)}), bf16[128,768]{1,0:T(8,128)(2,1)}) %reduce-scatter.49.cloned.1.call-update) | async-done | bytes 196624
  397.5 24.1 %reduce-scatter.43.cloned.1.call-done = bf16[128,768]{1,0:T(8,128)(2,1)} async-done(((bf16[512,768]{1,0:T(8,128)(2,1)}), bf16[128,768]{1,0:T(8,128)(2,1)}) %reduce-scatter.43.cloned.1.call-update) | async-done | bytes 196624
  423.3 24.1 %reduce-scatter.41.cloned.1.call-done = bf16[128,768]{1,0:T(8,128)(2,1)} async-done(((bf16[512,768]{1,0:T(8,128)(2,1)}), bf16[128,768]{1,0:T(8,128)(2,1)}) %reduce-scatter.41.cloned.1.call-update) | async-done | bytes 196624
  460.0 9.3 all_gather.48
  471.6 9.6 all_gather.46
  537.0 23.2 %reduce-scatter.37.cloned.1.call-done = bf16[128,768]{1,0:T(8,128)(2,1)} async-done(((bf16[512,768]{1,0:T(8,128)(2,1)}), bf16[128,768]{1,0:T(8,128)(2,1)}) %reduce-scatter.37.cloned.1.call-update) | async-done | bytes 196624
  565.1 7.2 add_add_fusion.2
  587.0 11.4 %add_add_fusion = f32[3072,768]{1,0:T(8,128)} fusion(f32[3072,768]{1,0:T(8,128)} %fusion.140, f32[3072,768]{1,0:T(8,128)} %fusion.152, f32[3072,768]{1,0:T(8,128)S(1)} %fusion.146, bf16[4,128,768]{2,1,0:T(8,128)(2,1)S(1)} %copy-done.25, f32[128,3072]{1,0:T(8,128)S(1)} %copy-done.32), kind=kOutput, calls=%fused_computation | convolution fusion | flops 614596608 | bytes 39518208 | tf_op jit(solution)/shard_map/tf,td->fd/dot_general | solution.py:206
  611.8 12.5 %add_add_fusion.1 = f32[768,3072]{1,0:T(8,128)} fusion(f32[768,3072]{1,0:T(8,128)} %fusion.216, f32[768,3072]{1,0:T(8,128)} %fusion.214, f32[768,3072]{1,0:T(8,128)S(1)} %fusion.215, bf16[128,3072]{1,0:T(8,128)(2,1)S(1)} %copy-done.57, f32[128,768]{1,0:T(8,128)S(1)} %get-tuple-element.470, f32[128]{0:T(128)S(1)} %copy-done.210, f32[128]{0:T(128)S(1)} %copy-done.181, ...), kind=kOutput, calls=%fused_computation.1 | convolution fusion | flops 611549184 | bytes 38935552 | tf_op jit(solution)/shard_map/td,tf->df/dot_general | solution.py:211
  649.7 40.5 %all-reduce.18 = (f32[768]{0:T(1024)S(1)}, f32[768]{0:T(1024)S(1)}, f32[768]{0:T(1024)S(1)}, f32[768]{0:T(1024)S(1)}, f32[768]{0:T(1024)S(1)}, /*index=5*/f32[76...) all-reduce(f32[768]{0:T(1024)S(1)} %add_add_fusion.20, ...), channel_id=49, replica_groups=mesh['dp'=8,'fsdp'=4] {'dp','fsdp'}, use_global_device_ids=true, to_apply=%region_49.50.clone | all-reduce | flops 9216 | bytes 73728
  700.3 90.1 %reduce-scatter.29.cloned.1.call-done = f32[24,2304]{1,0:T(8,128)} async-done(((f32[768,2304]{1,0:T(8,128)}), f32[24,2304]{1,0:T(8,128)}) %reduce-scatter.29.cloned.1.call-update) | async-done | bytes 221200 | tf_op jit(solution)/shard_map/reduce_scatter | solution.py:292
  790.4 141.2 %reduce-scatter.35.cloned.1.call-done = f32[96,768]{1,0:T(8,128)} async-done(((f32[3072,768]{1,0:T(8,128)}), f32[96,768]{1,0:T(8,128)}) %reduce-scatter.35.cloned.1.call-update) | async-done | bytes 294928 | tf_op jit(solution)/shard_map/reduce_scatter | solution.py:301
  931.6 142.0 %reduce-scatter.33.cloned.1.call-done = f32[24,3072]{1,0:T(8,128)} async-done(((f32[768,3072]{1,0:T(8,128)}), f32[24,3072]{1,0:T(8,128)}) %reduce-scatter.33.cloned.1.call-update) | async-done | bytes 294928 | tf_op jit(solution)/shard_map/reduce_scatter | solution.py:299
  (810 shorter events, 287.5 us)
Async XLA Ops:
  7.3 53.6 %copy-start.220 = (s32[4,512]{1,0:T(4,128)S(1)}, s32[4,512]{1,0:T(4,128)}, u32[]{:S(2)}) copy-start(s32[4,512]{1,0:T(4,128)} %param.17) | copy-start | bytes 24580
  7.3 66.6 %all-gather.5.cloned.1.call-start = ((), (), s32[]{:S(2)}) async-start(), calls=%async_computation.12 | async-start | bytes 3649536 | tf_op jit(solution)/shard_map/all_gather | solution.py:70
  8.0 141.9 %all-gather.7.cloned.1.call-start = ((), (), s32[]{:S(2)}) async-start(), calls=%async_computation.13 | async-start | bytes 1216512 | tf_op jit(solution)/shard_map/all_gather | solution.py:73
  8.8 187.7 %all-gather.9.cloned.1.call-start = ((), (), s32[]{:S(2)}) async-start(), calls=%async_computation.14 | async-start | bytes 4866048 | tf_op jit(solution)/shard_map/all_gather | solution.py:77
  9.5 252.2 %all-gather.11.cloned.1.call-start = ((), (), s32[]{:S(2)}) async-start(), calls=%async_computation.15 | async-start | bytes 4866048 | tf_op jit(solution)/shard_map/all_gather | solution.py:79
  10.1 341.0 %reduce-scatter.47.cloned.1.call-start = ((), (), s32[]{:S(2)}) async-start(), calls=%async_computation.25 | async-start | bytes 983040
  105.6 40.1 %copy-start.62 = (bf16[128,768]{0,1:T(8,128)(2,1)}, bf16[128,768]{0,1:T(8,128)(2,1)S(1)}, u32[]{:S(2)}) copy-start(bf16[128,768]{0,1:T(8,128)(2,1)S(1)} %copy.89) | copy-start | bytes 589828
  106.6 45.7 %copy-start.64 = (bf16[128,768]{0,1:T(8,128)(2,1)}, bf16[128,768]{0,1:T(8,128)(2,1)S(1)}, u32[]{:S(2)}) copy-start(bf16[128,768]{0,1:T(8,128)(2,1)S(1)} %copy.86) | copy-start | bytes 589828
  295.8 56.4 %reduce-scatter.45.cloned.1.call-start = ((), (), s32[]{:S(2)}) async-start(), calls=%async_computation.24 | async-start | bytes 983040
  306.2 63.6 %reduce-scatter.51.cloned.1.call-start = ((), (), s32[]{:S(2)}) async-start(), calls=%async_computation.27 | async-start | bytes 983040
  313.8 81.9 %reduce-scatter.49.cloned.1.call-start = ((), (), s32[]{:S(2)}) async-start(), calls=%async_computation.26 | async-start | bytes 983040
  324.0 97.6 %reduce-scatter.43.cloned.1.call-start = ((), (), s32[]{:S(2)}) async-start(), calls=%async_computation.23 | async-start | bytes 983040
  331.2 116.3 %reduce-scatter.41.cloned.1.call-start = ((), (), s32[]{:S(2)}) async-start(), calls=%async_computation.22 | async-start | bytes 983040
  342.0 193.9 %reduce-scatter.39.cloned.1.call-start = ((), (), s32[]{:S(2)}) async-start(), calls=%async_computation.21 | async-start | bytes 983040
  352.2 100.6 %copy-start.68 = (bf16[128,768]{0,1:T(8,128)(2,1)}, bf16[128,768]{0,1:T(8,128)(2,1)S(1)}, u32[]{:S(2)}) copy-start(bf16[128,768]{0,1:T(8,128)(2,1)S(1)} %copy.138) | copy-start | bytes 589828
  370.8 82.0 %copy-start.58 = (bf16[128,768]{0,1:T(8,128)(2,1)}, bf16[128,768]{0,1:T(8,128)(2,1)S(1)}, u32[]{:S(2)}) copy-start(bf16[128,768]{0,1:T(8,128)(2,1)S(1)} %copy.142) | copy-start | bytes 589828
  509.3 50.9 %reduce-scatter.37.cloned.1.call-start = ((), (), s32[]{:S(2)}) async-start(), calls=%async_computation.20 | async-start | bytes 983040
  518.0 182.2 %reduce-scatter.31.cloned.1.call-start = ((), (), s32[]{:S(2)}) async-start(), calls=%async_computation.17 | async-start | bytes 2433024 | tf_op jit(solution)/shard_map/reduce_scatter | solution.py:295
  523.1 267.3 %reduce-scatter.29.cloned.1.call-start = ((), (), s32[]{:S(2)}) async-start(), calls=%async_computation.16 | async-start | bytes 7299072 | tf_op jit(solution)/shard_map/reduce_scatter | solution.py:292
  572.3 359.3 %reduce-scatter.35.cloned.1.call-start = ((), (), s32[]{:S(2)}) async-start(), calls=%async_computation.19 | async-start | bytes 9732096 | tf_op jit(solution)/shard_map/reduce_scatter | solution.py:301
  598.4 475.2 %reduce-scatter.33.cloned.1.call-start = ((), (), s32[]{:S(2)}) async-start(), calls=%async_computation.18 | async-start | bytes 9732096 | tf_op jit(solution)/shard_map/reduce_scatter | solution.py:299
  648.9 47.8 %copy-start.85 = (f32[128,768]{1,0:T(8,128)}, f32[128,768]{1,0:T(8,128)S(1)}, u32[]{:S(2)}) copy-start(f32[128,768]{1,0:T(8,128)S(1)} %get-tuple-element.492) | copy-start | bytes 1179652
  648.9 47.8 %copy-start.46 = (f32[128,768]{1,0:T(8,128)S(1)}, f32[128,768]{1,0:T(8,128)}, u32[]{:S(2)}) copy-start(f32[128,768]{1,0:T(8,128)} %copy-done.45) | copy-start | bytes 1179652
  648.9 47.8 %copy-start.48 = (f32[128,768]{1,0:T(8,128)S(1)}, f32[128,768]{1,0:T(8,128)}, u32[]{:S(2)}) copy-start(f32[128,768]{1,0:T(8,128)} %copy-done.47) | copy-start | bytes 1179652
  (264 other events, 1080.2 us)
Sparse Core Ops, SparseCore 0:
  11.0 62.8 all-gather.4
  76.8 54.0 all-gather.6
  133.8 62.5 all-gather.8
  199.2 62.4 all-gather.10
  295.9 22.0 reduce-scatter.46
  320.6 23.3 reduce-scatter.44
  346.5 23.2 reduce-scatter.50
  372.4 23.2 reduce-scatter.48
  398.3 23.2 reduce-scatter.42
  424.1 23.2 reduce-scatter.40
  509.4 24.2 reduce-scatter.38
  536.9 23.2 reduce-scatter.36
  566.0 99.0 reduce-scatter.30
  672.2 118.1 reduce-scatter.28
  796.7 134.8 reduce-scatter.34
  938.9 134.5 reduce-scatter.32
where the time goes:
time: 1090 us; the launch traced here: 1080 us
  waiting for transfers between devices  591 us (54%)
  matrix products  207 us (19%)
  blocking collectives  157 us (14%)
  local copies, waits for them, and re-layouts  76.3 us (7%)
  other arithmetic  30.6 us (3%)
  between operations  17.6 us (2%)
    reduce_scatter x1, waiting for transfers between devices, on_device(): lax.psum_scatter(local_terms[9], ('dp', 'fsdp'), scatter_dimension=0, til...  142 us
    reduce_scatter x1, waiting for transfers between devices, on_device(): lax.psum_scatter(local_terms[11], ('dp', 'fsdp'), scatter_dimension=0, ti...  141 us
    unnamed x24, waiting for transfers between devices  115 us
    reduce_scatter x1, waiting for transfers between devices, on_device(): lax.psum_scatter(local_terms[2], ('dp', 'fsdp'), scatter_dimension=0, til...  90.1 us
    unnamed x2, blocking collectives  83.3 us
    all_gather x1, waiting for transfers between devices, on_device(): lax.all_gather(down_weight, ('dp', 'fsdp'), axis=0, tiled=True)  60.9 us
    unnamed x587, local copies, waits for them, and re-layouts  58.4 us
    all_gather x4, blocking collectives, on_device(): lax.all_gather(values_local, 'fsdp', axis=0, tiled=True)  37 us
  transfers between devices with their start and end apart: 16, of which 11 were waited for; matrix products, arithmetic and copies ran while one was open for 21% of the time, Pallas kernels for 0%

commit v1 on v0

--- a/solution.py
+++ b/solution.py
@@ -1,8 +1,11 @@
+import functools
 import math
 
 import jax
 import jax.numpy as jnp
 from jax import lax
+from jax.experimental import pallas as pl
+from jax.experimental.pallas import tpu as pltpu
 from jax.sharding import PartitionSpec as P
 
 HEADS = 12
@@ -33,7 +36,7 @@
     return jax.tree.map(jnp.add, first_terms, second_terms)
 
 
-def on_device(
+def on_device_general(
     inputs,
     segments,
     norm1_gain,
@@ -321,6 +324,858 @@
     )
 
 
+AXES = ("dp", "fsdp")
+CORE, X, Y, Z0, Z1 = 1, 2, 4, 8, 16
+LINE = (0, Z1, Z0, Z1 ^ Z0)
+PLANE = (0, X, Y, X ^ Y)
+DEVICES = 32
+MIB = 1024 * 1024
+SMALL = pl.CostEstimate(flops=1024, transcendentals=0, bytes_accessed=1024)
+
+
+def swap(values, mask):
+    pairs = [(i, i ^ mask) for i in range(DEVICES)]
+    return lax.ppermute(values, AXES, pairs)
+
+
+SLOTS = [core ^ plane ^ line for core in (0, CORE) for plane in PLANE for line in LINE]
+
+
+def fence(*values):
+    return lax.optimization_barrier(values)
+
+
+def join(*parts):
+    return lax.optimization_barrier(jnp.concatenate(parts, 0))
+
+
+class Gather:
+    def __init__(self, shard):
+        self.held = shard[None]
+        self.across = []
+
+    def line(self):
+        self.got = [swap(self.held, mask) for mask in LINE[1:]]
+
+    def far(self):
+        self.got = [swap(self.held, Z1)]
+
+    def near(self):
+        self.held = join(self.held, *self.got)
+        self.got = [swap(self.held, Z0)]
+
+    def plane(self):
+        self.held = join(self.held, *self.got)
+        self.got = [swap(self.held, mask) for mask in PLANE[1:]]
+
+    def cores_early(self):
+        self.across = [swap(self.held, CORE)]
+
+    def cores(self):
+        own = [self.held, *self.got]
+        self.parts = own + self.across + [swap(piece, CORE) for piece in own[len(self.across) :]]
+
+    def places(self):
+        masks = [core ^ plane ^ line for core in (0, CORE) for plane in PLANE for line in LINE]
+        width = self.held.shape[2]
+        return [(i // 4, i % 4, mask, 0, width) for i, mask in enumerate(masks)]
+
+
+def sum_low(*terms):
+    total = sum(term.astype(jnp.float32) for term in terms)
+    return total.astype(jnp.bfloat16)
+
+
+class Scatter:
+    places = [
+        (slot // 16, slot % 16, core ^ plane ^ line)
+        for slot, (core, plane, line) in enumerate(
+            (core, plane, line) for core in (0, CORE) for plane in PLANE for line in LINE
+        )
+    ]
+
+    def __init__(self, halves):
+        self.kept, self.sent = halves
+
+    def cores(self):
+        self.got = swap(self.sent, CORE)
+
+    def plane(self):
+        self.kept, *quads = [
+            sum_low(self.kept[4 * i : 4 * i + 4], self.got[4 * i : 4 * i + 4]) for i in range(4)
+        ]
+        self.got = [swap(quad, mask) for quad, mask in zip(quads, PLANE[1:])]
+
+    def line(self):
+        terms = [self.kept, *self.got]
+        ones = [sum_low(*(term[i : i + 1] for term in terms)) for i in range(1, 4)]
+        self.kept = sum(term[0].astype(jnp.float32) for term in terms)
+        self.got = [swap(one, mask) for one, mask in zip(ones, LINE[1:])]
+
+    def near(self):
+        terms = [self.kept, *self.got]
+        self.kept = sum_low(*(term[:2] for term in terms))
+        self.got = [swap(sum_low(*(term[2:] for term in terms)), Z0)]
+
+    def far(self):
+        got = self.got[0]
+        self.got = [swap(sum_low(self.kept[1:], got[1:]), Z1)]
+        self.kept = self.kept[0].astype(jnp.float32) + got[0].astype(jnp.float32)
+
+    def total(self):
+        return self.kept + sum(got[0].astype(jnp.float32) for got in self.got)
+
+
+def cuts_of(parts):
+    ends = [sum(parts[: i + 1]) for i in range(len(parts))]
+    return tuple((end - part, end) for end, part in zip(ends, parts))
+
+
+def shuffle_kernel(moves, count, me_ref, *refs):
+    me = me_ref[0]
+
+    def part(slot):
+        return pl.ds(lax.bitwise_xor(me, slot[0]) if isinstance(slot, tuple) else slot, 1)
+
+    for source, source_slot, source_low, target, target_slot, target_low, width in moves:
+        refs[count + target][part(target_slot), :, target_low : target_low + width] = refs[source][
+            part(source_slot), :, source_low : source_low + width
+        ]
+
+
+def whole_block(shape):
+    return pl.BlockSpec(shape, lambda i: (0,) * len(shape), pipeline_mode=pl.Buffered(1))
+
+
+def shuffle(arrays, shapes, moves, me, pinned):
+    dtype = arrays[0].dtype
+    size = sum(math.prod(shape) for shape in shapes)
+    make = pltpu.HBM if pinned else jax.ShapeDtypeStruct
+    return pl.pallas_call(
+        functools.partial(shuffle_kernel, moves, len(arrays)),
+        grid=(1,),
+        out_shape=[make(shape, dtype) for shape in shapes],
+        in_specs=[pl.BlockSpec(memory_space=pltpu.SMEM)]
+        + [whole_block(array.shape) for array in arrays],
+        out_specs=[whole_block(shape) for shape in shapes],
+        compiler_params=pltpu.CompilerParams(vmem_limit_bytes=16 * MIB),
+        cost_estimate=SMALL,
+    )(me, *arrays)
+
+
+def restore(gather, cuts, me):
+    moves = []
+    for part, slot, mask, low, high in gather.places():
+        for target, (begin, end) in enumerate(cuts):
+            left, right = max(low, begin), min(high, end)
+            if left < right:
+                moves.append(
+                    (part, slot, left - low, target, (mask,), left - begin, right - left)
+                )
+    rows = gather.parts[0].shape[1]
+    shapes = [(DEVICES, rows, end - begin) for begin, end in cuts]
+    return shuffle(gather.parts, shapes, moves, me, True)
+
+
+TN = (((0,), (0,)), ((), ()))
+
+
+def parts_call(kernel, inputs, rows, width, scratch, limit, me):
+    half = (DEVICES // 2, rows, width)
+    return pl.pallas_call(
+        kernel,
+        grid=(1,),
+        out_shape=[jax.ShapeDtypeStruct(half, jnp.bfloat16)] * 2,
+        in_specs=[pl.BlockSpec(memory_space=pltpu.SMEM)]
+        + [whole_block(value.shape) for value in inputs],
+        out_specs=[whole_block(half)] * 2,
+        scratch_shapes=[pltpu.VMEM(scratch, jnp.float32)],
+        compiler_params=pltpu.CompilerParams(vmem_limit_bytes=limit * MIB),
+        cost_estimate=SMALL,
+    )(me, *inputs)
+
+
+def store_rows(me, sum_ref, outs, low, high):
+    rows = sum_ref.shape[0] // DEVICES
+    for half, slot, mask in Scatter.places:
+        first = pl.multiple_of(lax.bitwise_xor(me, mask) * rows, rows)
+        outs[half][slot, :, low:high] = sum_ref[pl.ds(first, rows), : high - low].astype(
+            jnp.bfloat16
+        )
+
+
+def multiply_rows(me, left_ref, right_refs, sum_ref, outs, low):
+    width = sum_ref.shape[1]
+    for ref in right_refs:
+        for begin in range(0, ref.shape[1], width):
+            sum_ref[...] = lax.dot_general(
+                left_ref[...],
+                ref[:, begin : begin + width],
+                TN,
+                preferred_element_type=jnp.float32,
+            )
+            store_rows(me, sum_ref, outs, low + begin, low + begin + width)
+        low += ref.shape[1]
+    return low
+
+
+def second_parts_kernel(
+    me_ref, mixed_ref, branch_ref, normed_ref, pre_ref, kept_ref, sent_ref, sum_ref
+):
+    me, outs = me_ref[0], (kept_ref, sent_ref)
+    low = multiply_rows(me, mixed_ref, [branch_ref], sum_ref, outs, 0)
+    multiply_rows(me, normed_ref, [pre_ref], sum_ref, outs, low)
+
+
+def first_parts_kernel(
+    me_ref, normed_ref, query_ref, key_ref, value_ref, sums_ref, kept_ref, sent_ref, sum_ref
+):
+    me, outs = me_ref[0], (kept_ref, sent_ref)
+    low = multiply_rows(me, normed_ref, [query_ref, key_ref, value_ref], sum_ref, outs, 0)
+    for half, slot, mask in Scatter.places:
+        outs[half][slot, :, low:] = sums_ref[lax.bitwise_xor(me, mask)]
+
+
+def third_parts_kernel(me_ref, hidden_ref, cot_ref, kept_ref, sent_ref, sum_ref):
+    me, outs = me_ref[0], (kept_ref, sent_ref)
+    rows = kept_ref.shape[1]
+    for block in range(DEVICES // 4):
+        first = pl.multiple_of(lax.bitwise_xor(me // 4, block) * (4 * rows), 4 * rows)
+        sum_ref[...] = lax.dot_general(
+            hidden_ref[:, pl.ds(first, 4 * rows)],
+            cot_ref[...],
+            TN,
+            preferred_element_type=jnp.float32,
+        )
+        for half, slot, mask in Scatter.places:
+            if mask // 4 == block:
+                first = pl.multiple_of(lax.bitwise_xor(me % 4, mask % 4) * rows, rows)
+                outs[half][slot] = sum_ref[pl.ds(first, rows)].astype(jnp.bfloat16)
+
+
+NT = (((1,), (1,)), ((), ()))
+
+
+def make_mask(labels_row_ref, labels_col_ref, mask_ref):
+    @pl.when(pl.program_id(0) == 0)
+    def _():
+        allowed = labels_col_ref[...] == labels_row_ref[...]
+        mask_ref[...] = jnp.where(allowed, 0.0, NEG_LARGE)
+
+
+def head_probs(keys, queries, head, mask_ref):
+    f32 = jnp.float32
+    lane = lax.broadcasted_iota(jnp.int32, queries.shape, 1)
+    own = (lane // 64) == head
+    chosen = jnp.where(own, queries.astype(f32) * SCALE_SCORE, 0.0).astype(jnp.bfloat16)
+    scores = lax.dot_general(keys, chosen, NT, preferred_element_type=f32) + mask_ref[...]
+    exponent = jnp.exp(scores - jnp.max(scores, 0, keepdims=True))
+    return exponent * (1.0 / jnp.sum(exponent, 0, keepdims=True))
+
+
+def attend_kernel(row_ref, col_ref, query_ref, key_ref, value_ref, out_ref, prob_ref, mask_ref):
+    make_mask(row_ref, col_ref, mask_ref)
+    keys, queries = key_ref[...], query_ref[...]
+    values_across = value_ref[...].astype(jnp.float32).T.astype(jnp.bfloat16)
+    mixed = []
+    for head in range(2):
+        prob_ref[head] = head_probs(keys, queries, head, mask_ref).astype(jnp.bfloat16)
+        mixed.append(
+            jnp.dot(
+                values_across[64 * head : 64 * head + 64],
+                prob_ref[head],
+                preferred_element_type=jnp.float32,
+            )
+        )
+    out_ref[...] = jnp.concatenate(mixed, 0).T.astype(jnp.bfloat16)
+
+
+def attend_back_kernel(
+    query_ref, key_ref, value_ref, prob_ref, grad_ref, dquery_ref, dkey_ref, dvalue_ref
+):
+    f32, bf16 = jnp.float32, jnp.bfloat16
+    keys, queries, values, grads = key_ref[...], query_ref[...], value_ref[...], grad_ref[...]
+    keys_across = keys.astype(f32).T.astype(bf16)
+    lane = lax.broadcasted_iota(jnp.int32, keys.shape, 1)
+    dquery, dkey, dvalue = [], [], []
+    for head in range(2):
+        chosen = jnp.where((lane // 64) == head, grads.astype(f32), 0.0).astype(bf16)
+        grad_prob = lax.dot_general(values, chosen, NT, preferred_element_type=f32)
+        prob = prob_ref[head].astype(f32)
+        delta = jnp.sum(prob * grad_prob, 0, keepdims=True)
+        grad_scores = (prob * (grad_prob - delta)).astype(bf16)
+        dvalue.append(jnp.dot(prob_ref[head], grads, preferred_element_type=f32))
+        dkey.append(jnp.dot(grad_scores, queries, preferred_element_type=f32))
+        dquery.append(
+            jnp.dot(
+                keys_across[64 * head : 64 * head + 64], grad_scores, preferred_element_type=f32
+            )
+        )
+    low_half = lane < 64
+    dquery_ref[...] = (jnp.concatenate(dquery, 0).T * SCALE_SCORE).astype(bf16)
+    dkey_ref[...] = (jnp.where(low_half, dkey[0], dkey[1]) * SCALE_SCORE).astype(bf16)
+    dvalue_ref[...] = jnp.where(low_half, dvalue[0], dvalue[1]).astype(bf16)
+
+
+def pair_specs(tokens, pairs):
+    parts = [
+        pl.BlockSpec((tokens, 128), lambda i, part=part: (0, i + part * pairs))
+        for part in range(3)
+    ]
+    return parts, pl.BlockSpec((2, tokens, tokens), lambda i: (i, 0, 0))
+
+
+def in_hbm(array):
+    return pltpu.with_memory_space_constraint(array, pltpu.HBM)
+
+
+def attend(labels, project):
+    tokens, pairs = project.shape[0], HEADS // 2
+    parts, probs = pair_specs(tokens, pairs)
+    return pl.pallas_call(
+        attend_kernel,
+        grid=(pairs,),
+        out_shape=[
+            jax.ShapeDtypeStruct((tokens, 128 * pairs), jnp.bfloat16),
+            pltpu.HBM((HEADS, tokens, tokens), jnp.bfloat16),
+        ],
+        in_specs=[
+            pl.BlockSpec((1, tokens), lambda i: (0, 0)),
+            pl.BlockSpec((tokens, 1), lambda i: (0, 0)),
+            *parts,
+        ],
+        out_specs=[pl.BlockSpec((tokens, 128), lambda i: (0, i)), probs],
+        scratch_shapes=[pltpu.VMEM((tokens, tokens), jnp.float32)],
+        compiler_params=pltpu.CompilerParams(vmem_limit_bytes=12 * MIB),
+        cost_estimate=SMALL,
+    )(labels.reshape(1, tokens), labels.reshape(tokens, 1), project, project, project)
+
+
+def attend_back(project, probs, grads):
+    tokens, pairs = project.shape[0], HEADS // 2
+    block = pl.BlockSpec((tokens, 128), lambda i: (0, i))
+    shape = jax.ShapeDtypeStruct((tokens, 128 * pairs), jnp.bfloat16)
+    parts, prob_spec = pair_specs(tokens, pairs)
+    return pl.pallas_call(
+        attend_back_kernel,
+        grid=(pairs,),
+        out_shape=[shape] * 3,
+        in_specs=[*parts, prob_spec, block],
+        out_specs=[block] * 3,
+        compiler_params=pltpu.CompilerParams(vmem_limit_bytes=14 * MIB),
+        cost_estimate=SMALL,
+    )(project, project, project, in_hbm(probs), grads)
+
+
+def norm_parts(values):
+    centre = values - jnp.mean(values, -1, keepdims=True)
+    scale = lax.rsqrt(jnp.mean(centre * centre, -1, keepdims=True) + EPSILON)
+    return centre * scale, scale
+
+
+def norm_back(grads, values, gain_row):
+    unit, scale = norm_parts(values)
+    inner = grads * gain_row
+    part = inner - jnp.mean(inner, -1, keepdims=True)
+    part = part - unit * jnp.mean(inner * unit, -1, keepdims=True)
+    gain, shift = jnp.sum(grads * unit, 0, keepdims=True), jnp.sum(grads, 0, keepdims=True)
+    return part * scale, gain, shift
+
+
+def column_sum(values):
+    return jnp.sum(values.astype(jnp.float32), 0, keepdims=True)
+
+
+def up_kernel(normed_ref, weight_ref, bias_ref, hidden_ref, slope_ref):
+    bf16 = jnp.bfloat16
+    pre = jnp.dot(normed_ref[...], weight_ref[...], preferred_element_type=jnp.float32)
+    pre = pre + bias_ref[...]
+    square = pre * pre
+    bend = jnp.tanh(pre * (0.7978845608028654 + 0.7978845608028654 * 0.044715 * square))
+    half = 0.5 * (1.0 + bend)
+    hidden_ref[...] = (pre * half).astype(bf16)
+    inner = 0.7978845608028654 + 3 * 0.7978845608028654 * 0.044715 * square
+    slope_ref[...] = (half + 0.5 * pre * (1.0 - bend * bend) * inner).astype(bf16)
+
+
+def up_forward(normed, up_full, bias_row):
+    tokens, width = normed.shape
+    inner, tile = up_full.shape[1], 512
+    block = pl.BlockSpec((tokens, tile), lambda i: (0, i))
+    shape = jax.ShapeDtypeStruct((tokens, inner), jnp.bfloat16)
+    return pl.pallas_call(
+        up_kernel,
+        grid=(inner // tile,),
+        out_shape=[shape, shape],
+        in_specs=[
+            pl.BlockSpec((tokens, width), lambda i: (0, 0)),
+            pl.BlockSpec((width, tile), lambda i: (0, i)),
+            pl.BlockSpec((1, tile), lambda i: (0, i)),
+        ],
+        out_specs=[block, block],
+        compiler_params=pltpu.CompilerParams(vmem_limit_bytes=14 * MIB),
+        cost_estimate=SMALL,
+    )(normed, in_hbm(up_full), bias_row)
+
+
+def pre_kernel(cot_ref, weight_ref, slope_ref, pre_ref, sum_ref):
+    f32 = jnp.float32
+    grads = lax.dot_general(cot_ref[...], weight_ref[...], NT, preferred_element_type=f32)
+    low = (grads * slope_ref[...].astype(f32)).astype(jnp.bfloat16)
+    pre_ref[...] = low
+    sum_ref[...] = column_sum(low)
+
+
+def pre_back(cot_low, down_full, slope):
+    tokens, width = cot_low.shape
+    inner, tile = down_full.shape[0], 512
+    block = pl.BlockSpec((tokens, tile), lambda i: (0, i))
+    return pl.pallas_call(
+        pre_kernel,
+        grid=(inner // tile,),
+        out_shape=[
+            jax.ShapeDtypeStruct((tokens, inner), jnp.bfloat16),
+            jax.ShapeDtypeStruct((1, inner), jnp.float32),
+        ],
+        in_specs=[
+            pl.BlockSpec((tokens, width), lambda i: (0, 0)),
+            pl.BlockSpec((tile, width), lambda i: (i, 0)),
+            block,
+        ],
+        out_specs=[block, pl.BlockSpec((1, tile), lambda i: (0, i))],
+        compiler_params=pltpu.CompilerParams(vmem_limit_bytes=12 * MIB),
+        cost_estimate=SMALL,
+    )(cot_low, in_hbm(down_full), slope)
+
+
+def middle_kernel(pre_ref, up_ref, resid_ref, gain_ref, cot_ref, out_ref, mid_ref, low_ref, mixed_ref, sums_ref):
+    f32, bf16 = jnp.float32, jnp.bfloat16
+
+    @pl.when(pl.program_id(0) == 0)
+    def _():
+        sums_ref[...] = jnp.zeros_like(sums_ref)
+
+    grads = lax.dot_general(pre_ref[...], up_ref[...], NT, preferred_element_type=f32)
+    part, gain, shift = norm_back(grads, resid_ref[...], gain_ref[...])
+    cot = cot_ref[...].astype(f32)
+    mid = cot + part
+    low = mid.astype(bf16)
+    mid_ref[...] = mid
+    low_ref[...] = low
+    mixed_ref[...] = lax.dot_general(
+        low, out_ref[...], NT, preferred_element_type=f32
+    ).astype(bf16)
+    for row, value in enumerate((column_sum(low), gain, shift, column_sum(cot))):
+        sums_ref[row : row + 1] += value
+
+
+def middle_back(grad_pre, up_full, resid_mid, gain_row, cot_low, out_full):
+    tokens, inner = grad_pre.shape
+    width, tile = resid_mid.shape[1], 256
+    block = pl.BlockSpec((tile, width), lambda i: (i, 0))
+    whole = lambda *shape: pl.BlockSpec(shape, lambda i: (0, 0))
+    return pl.pallas_call(
+        middle_kernel,
+        grid=(tokens // tile,),
+        out_shape=[
+            jax.ShapeDtypeStruct((tokens, width), jnp.float32),
+            jax.ShapeDtypeStruct((tokens, width), jnp.bfloat16),
+            jax.ShapeDtypeStruct((tokens, width), jnp.bfloat16),
+            jax.ShapeDtypeStruct((8, width), jnp.float32),
+        ],
+        in_specs=[
+            pl.BlockSpec((tile, inner), lambda i: (i, 0)),
+            whole(width, inner),
+            block,
+            whole(1, width),
+            block,
+            whole(width, width),
+        ],
+        out_specs=[block, block, block, whole(8, width)],
+        compiler_params=pltpu.CompilerParams(vmem_limit_bytes=20 * MIB),
+        cost_estimate=SMALL,
+    )(grad_pre, up_full, resid_mid, gain_row, cot_low, out_full)
+
+
+def first_kernel(
+    query_ref, key_ref, value_ref, weight_ref, token_ref, gain_ref, mid_ref, in_ref, sums_ref
+):
+    f32 = jnp.float32
+
+    @pl.when(pl.program_id(0) == 0)
+    def _():
+        sums_ref[...] = jnp.zeros_like(sums_ref)
+
+    width = query_ref.shape[1]
+    grads = sum(
+        lax.dot_general(
+            ref[...],
+            weight_ref[:, width * i : width * (i + 1)],
+            NT,
+            preferred_element_type=f32,
+        )
+        for i, ref in enumerate((query_ref, key_ref, value_ref))
+    )
+    part, gain, shift = norm_back(grads, token_ref[...].astype(f32), gain_ref[...])
+    in_ref[...] = (mid_ref[...] + part).astype(jnp.bfloat16)
+    rows = (gain, shift, column_sum(query_ref[...]), column_sum(value_ref[...]))
+    for row, value in enumerate(rows):
+        sums_ref[row : row + 1] += value
+
+
+def first_back(grad_query, grad_key, grad_value, qkv_full, tokens_in, gain_row, grad_mid):
+    tokens, width = tokens_in.shape
+    tile = 256
+    block = pl.BlockSpec((tile, width), lambda i: (i, 0))
+    whole = lambda *shape: pl.BlockSpec(shape, lambda i: (0, 0))
+    return pl.pallas_call(
+        first_kernel,
+        grid=(tokens // tile,),
+        out_shape=[
+            jax.ShapeDtypeStruct((tokens, width), jnp.bfloat16),
+            jax.ShapeDtypeStruct((8, width), jnp.float32),
+        ],
+        in_specs=[
+            block,
+            block,
+            block,
+            whole(width, 3 * width),
+            block,
+            whole(1, width),
+            block,
+        ],
+        out_specs=[block, whole(8, width)],
+        compiler_params=pltpu.CompilerParams(vmem_limit_bytes=16 * MIB),
+        cost_estimate=SMALL,
+    )(grad_query, grad_key, grad_value, qkv_full, tokens_in, gain_row, grad_mid)
+
+
+def pick(values, index, axis=0):
+    return lax.dynamic_index_in_dim(values, index, axis, keepdims=False)
+
+
+def to_micro_x(values, side):
+    count, rows, width = values.shape
+    halves = values.reshape(2, 2, rows, width)
+    return swap(pick(halves, 1 - side), 2), halves
+
+
+def to_micro_c(got, halves, side, core):
+    both = jnp.stack([pick(halves, side), got], 1)
+    return pick(both, core), swap(pick(both, 1 - core), CORE)
+
+
+def to_micro_end(kept, got):
+    return jnp.concatenate([kept, got]).reshape(-1, kept.shape[-1])
+
+
+def from_micro_c(values):
+    rows, width = values.shape[0] // 4, values.shape[1]
+    parts = values.reshape(2, 2, rows, width)
+    return parts[0], swap(parts[1], CORE)
+
+
+def from_micro_x(kept, got, core):
+    both = jnp.where(core == 0, jnp.stack([kept, got]), jnp.stack([got, kept]))
+    return both[:, 0], swap(both[:, 1], 2)
+
+
+def from_micro_end(kept, got, side):
+    halves = jnp.where(side == 0, jnp.stack([kept, got]), jnp.stack([got, kept]))
+    return halves.reshape(4, *kept.shape[1:])
+
+
+def on_device_fast(
+    inputs,
+    segments,
+    norm1_gain,
+    norm1_bias,
+    qkv_weight,
+    query_bias,
+    value_bias,
+    out_weight,
+    out_bias,
+    norm2_gain,
+    norm2_bias,
+    up_weight,
+    up_bias,
+    down_weight,
+    down_bias,
+    cotangent,
+):
+    f32, bf16 = jnp.float32, jnp.bfloat16
+    local_rows, width = inputs.shape[1], inputs.shape[2]
+    rows = width // DEVICES
+    wide, inner = qkv_weight.shape[1], up_weight.shape[1]
+    group = lax.axis_index("fsdp")
+    side, core = group // 2, group % 2
+    me = (lax.axis_index("dp") * 4 + group).astype(jnp.int32).reshape(1)
+
+    vectors = (
+        norm1_gain,
+        norm1_bias,
+        query_bias,
+        value_bias,
+        out_bias,
+        norm2_gain,
+        norm2_bias,
+        down_bias,
+    )
+    row = lax.broadcasted_iota(jnp.int32, (rows, rows), 0)
+    block = jnp.pad(up_bias.reshape(4, rows), ((8, rows - 12), (0, 0)))
+    for j, vector in enumerate(vectors):
+        block = jnp.where(row == j, vector[None], block)
+    block = jnp.pad(block, ((0, 0), (0, 128 - rows)))
+    first = Gather(jnp.concatenate([qkv_weight, block], 1))
+    second = Gather(jnp.concatenate([out_weight, up_weight], 1))
+    third = Gather(down_weight)
+
+    first.line()
+    token_got, token_halves = to_micro_x(inputs, side)
+    own = pick(segments, group).reshape(4, local_rows)
+    labels = jnp.concatenate(
+        [pick(own, lax.bitwise_xor(group, source)) for source in (0, 2, 1, 3)]
+    )
+    first.held, first.got, token_got, token_halves, second.held = fence(
+        first.held, first.got, token_got, token_halves, second.held
+    )
+
+    first.plane()
+    second.far()
+    second.near()
+    third.far()
+    token_kept, token_got = to_micro_c(token_got, token_halves, side, core)
+    tokens = to_micro_end(token_kept, token_got)
+    resid_in = tokens.astype(f32)
+    unit_one, _ = norm_parts(resid_in)
+    first.held, first.got, second.held, second.got, third.held, third.got, unit_one = fence(
+        first.held, first.got, second.held, second.got, third.held, third.got, unit_one
+    )
+
+    first.cores()
+    second.plane()
+    third.near()
+    qkv_full, vectors = restore(first, cuts_of((wide, 128)), me)
+    qkv_full = qkv_full.reshape(width, wide)
+    vectors = vectors[:, :12, :rows].astype(f32)
+    bias_up = vectors[:, 8:].reshape(1, -1)
+    (vectors,) = fence(vectors[:, :8].transpose(1, 0, 2).reshape(8, width))
+    (
+        gain_one,
+        shift_one,
+        bias_query,
+        bias_value,
+        bias_out,
+        gain_two,
+        shift_two,
+        bias_down,
+    ) = (vectors[i : i + 1] for i in range(8))
+    normed_one = (unit_one * gain_one + shift_one).astype(bf16)
+    bias_project = jnp.concatenate([bias_query, jnp.zeros_like(bias_query), bias_value], 1)
+    project = (
+        jnp.dot(normed_one, qkv_full, preferred_element_type=f32) + bias_project
+    ).astype(bf16)
+    mixed, probs = attend(labels, project)
+    second.held, second.got, third.held, third.got, mixed, cotangent = fence(
+        second.held, second.got, third.held, third.got, mixed, cotangent
+    )
+
+    second.cores()
+    cot_got, cot_halves = to_micro_x(cotangent, side)
+    second.parts, third.held, third.got, mixed, cot_got, cot_halves = fence(
+        second.parts, third.held, third.got, mixed, cot_got, cot_halves
+    )
+
+    third.plane()
+    cot_kept, cot_got = to_micro_c(cot_got, cot_halves, side, core)
+    cot_low = to_micro_end(cot_kept, cot_got)
+    out_full, up_full = restore(second, cuts_of((width, inner)), me)
+    out_full, up_full = out_full.reshape(width, width), up_full.reshape(width, inner)
+    resid_mid = resid_in + jnp.dot(mixed, out_full, preferred_element_type=f32) + bias_out
+    unit_two, _ = norm_parts(resid_mid)
+    normed_two = (unit_two * gain_two + shift_two).astype(bf16)
+    hidden, slope = up_forward(normed_two, up_full, bias_up)
+    deep = inner // DEVICES
+    down_sum = Scatter(
+        parts_call(
+            third_parts_kernel, [hidden, cot_low], deep, width, (4 * deep, width), 16, me
+        )
+    )
+    third.held, third.got, down_sum.kept, down_sum.sent, hidden, cot_low = fence(
+        third.held, third.got, down_sum.kept, down_sum.sent, hidden, cot_low
+    )
+
+    third.cores()
+    down_sum.cores()
+    third.parts, down_sum.kept, down_sum.got, hidden, cot_low = fence(
+        third.parts, down_sum.kept, down_sum.got, hidden, cot_low
+    )
+
+    down_sum.plane()
+    (down_full,) = restore(third, cuts_of((width,)), me)
+    down_full = down_full.reshape(inner, width)
+    grad_pre, grad_bias_up = pre_back(cot_low, down_full, slope)
+    grad_mid, branch_low, grad_mixed, sums_two = middle_back(
+        grad_pre, up_full, resid_mid, gain_two, cot_low, out_full
+    )
+    up_sum = Scatter(
+        parts_call(
+            second_parts_kernel,
+            [mixed, branch_low, normed_two, grad_pre],
+            rows,
+            width + inner,
+            (width, width),
+            20,
+            me,
+        )
+    )
+    result = resid_mid + jnp.dot(hidden, down_full, preferred_element_type=f32) + bias_down
+    result = result.astype(bf16)
+    down_sum.kept, down_sum.got, up_sum.kept, up_sum.sent, grad_mixed, result = fence(
+        down_sum.kept, down_sum.got, up_sum.kept, up_sum.sent, grad_mixed, result
+    )
+
+    up_sum.cores()
+    out_kept, out_got = from_micro_c(result)
+    (
+        down_sum.kept,
+        down_sum.got,
+        up_sum.kept,
+        up_sum.got,
+        grad_mixed,
+        out_kept,
+        out_got,
+    ) = fence(
+        down_sum.kept, down_sum.got, up_sum.kept, up_sum.got, grad_mixed, out_kept, out_got
+    )
+
+    up_sum.plane()
+    down_sum.near()
+    down_sum.far()
+    grad_query, grad_key, grad_value = attend_back(project, probs, grad_mixed)
+    in_grad, sums_one = first_back(
+        grad_query, grad_key, grad_value, qkv_full, tokens, gain_one, grad_mid
+    )
+    sums = jnp.concatenate([sums_one[:4], sums_two[:4]], 0)
+    sums = sums.reshape(8, DEVICES, rows).transpose(1, 0, 2)
+    sums = jnp.concatenate([sums, grad_bias_up.reshape(DEVICES, 4, rows)], 1)
+    sums = jnp.pad(sums, ((0, 0), (0, rows - 12), (0, 128 - rows))).astype(bf16)
+    qkv_sum = Scatter(
+        parts_call(
+            first_parts_kernel,
+            [normed_one, grad_query, grad_key, grad_value, sums],
+            rows,
+            wide + 128,
+            (width, width),
+            16,
+            me,
+        )
+    )
+    (
+        down_sum.kept,
+        down_sum.got,
+        up_sum.kept,
+        up_sum.got,
+        qkv_sum.kept,
+        qkv_sum.sent,
+        in_grad,
+        out_kept,
+        out_got,
+    ) = fence(
+        down_sum.kept,
+        down_sum.got,
+        up_sum.kept,
+        up_sum.got,
+        qkv_sum.kept,
+        qkv_sum.sent,
+        in_grad,
+        out_kept,
+        out_got,
+    )
+
+    qkv_sum.cores()
+    in_kept, in_got = from_micro_c(in_grad)
+    (
+        down_sum.kept,
+        down_sum.got,
+        up_sum.kept,
+        up_sum.got,
+        qkv_sum.kept,
+        qkv_sum.got,
+        in_kept,
+        in_got,
+    ) = fence(
+        down_sum.kept,
+        down_sum.got,
+        up_sum.kept,
+        up_sum.got,
+        qkv_sum.kept,
+        qkv_sum.got,
+        in_kept,
+        in_got,
+    )
+
+    qkv_sum.plane()
+    up_sum.near()
+    up_sum.far()
+    out_kept, out_got = from_micro_x(out_kept, out_got, core)
+    (
+        qkv_sum.kept,
+        qkv_sum.got,
+        up_sum.kept,
+        up_sum.got,
+        down_sum.kept,
+        down_sum.got,
+        in_kept,
+        in_got,
+        out_kept,
+        out_got,
+    ) = fence(
+        qkv_sum.kept,
+        qkv_sum.got,
+        up_sum.kept,
+        up_sum.got,
+        down_sum.kept,
+        down_sum.got,
+        in_kept,
+        in_got,
+        out_kept,
+        out_got,
+    )
+
+    qkv_sum.line()
+    in_kept, in_got = from_micro_x(in_kept, in_got, core)
+    grad_down = down_sum.total()
+    last = up_sum.total()
+    grad_out, grad_up = last[:, :width], last[:, width:]
+    qkv_sum.kept, qkv_sum.got, in_kept, in_got, out_kept, out_got = fence(
+        qkv_sum.kept, qkv_sum.got, in_kept, in_got, out_kept, out_got
+    )
+
+    output = from_micro_end(out_kept, out_got, side)
+    in_grad = from_micro_end(in_kept, in_got, side).astype(f32)
+    last = qkv_sum.total()
+    grad_qkv = last[:, :wide]
+    sums = last[:12, wide : wide + rows]
+    return (
+        output,
+        in_grad,
+        sums[0],
+        sums[1],
+        grad_qkv,
+        sums[2],
+        sums[3],
+        grad_out,
+        sums[4],
+        sums[5],
+        sums[6],
+        grad_up,
+        sums[8:12].reshape(-1),
+        grad_down,
+        sums[7],
+    )
+
+
 def solution(mesh):
     placed = (
         P(None, ("dp", "fsdp"), None),
@@ -340,8 +1195,9 @@
         P(("dp", "fsdp")),
         P(None, ("dp", "fsdp"), None),
     )
+    fits = mesh.shape["dp"] == 8 and mesh.shape["fsdp"] == 4
     return jax.shard_map(
-        on_device,
+        on_device_fast if fits else on_device_general,
         mesh=mesh,
         in_specs=placed,
         out_specs=(

time: 1090 us -> 268 us (0.25)
  waiting for transfers between devices: 591 us -> 93.1 us
  matrix products: 207 us -> 9.09 us
  blocking collectives: 157 us -> 0 us
  Pallas kernels: 0 us -> 68.3 us
  local copies, waits for them, and re-layouts: 76.3 us -> 19 us
  starting transfers between devices: 1.42 us -> 49.1 us
  between operations: 17.6 us -> 1.54 us
    reduce_scatter x4 -> x0, waiting for transfers between devices: 373 us -> none  [the longest x1 142 us: on_device(): lax.psum_scatter(local_terms[9], ('dp', 'fsdp'), scatter_dimension=0, til...]
    dot_general x76 -> x3, matrix products: 207 us -> 9.09 us  [the longest x1 4.3 us: on_device_fast(): jnp.dot(normed_one, qkv_full, preferred_element_type=f32) + bias_project]
    unnamed x24 -> x0, waiting for transfers between devices: 115 us -> none
    all_gather x4 -> x0, waiting for transfers between devices: 103 us -> none  [the longest x1 60.9 us: on_device(): lax.all_gather(down_weight, ('dp', 'fsdp'), axis=0, tiled=True)]
    ppermute x0 -> x55, waiting for transfers between devices: none -> 93.1 us  [swap(): return lax.ppermute(values, AXES, pairs)]
    unnamed x2 -> x0, blocking collectives: 83.3 us -> none
    all_gather x8 -> x0, blocking collectives: 73.3 us -> none  [the longest x4 37 us: on_device(): lax.all_gather(values_local, 'fsdp', axis=0, tiled=True)]
    pallas_call x0 -> x12, Pallas kernels: none -> 68.3 us  [the longest x1 11.7 us: attend_back(): pl.pallas_call(attend_back_kernel, grid=(pairs,), out_shape=[shape] * 3,...]
  transfers between devices with their start and end apart: 16 -> 55, of which waited for: 11 -> 25; matrix products, arithmetic and copies ran while one was open for 21% -> 13% of each run, Pallas kernels for 0% -> 26%
where the time goes in v1:
time: 268 us; the launch traced here: 267 us
  waiting for transfers between devices  93.1 us (35%)
  Pallas kernels  68.3 us (25%)
  starting transfers between devices  49.1 us (18%)
  other arithmetic  27.2 us (10%)
  local copies, waits for them, and re-layouts  19 us (7%)
  matrix products  9.09 us (3%)
    ppermute x55, waiting for transfers between devices, swap(): return lax.ppermute(values, AXES, pairs)  93.1 us
    ppermute x55, starting transfers between devices, swap(): return lax.ppermute(values, AXES, pairs)  49.1 us
    pallas_call x1, Pallas kernels, attend_back(): pl.pallas_call(attend_back_kernel, grid=(pairs,), out_shape=[shape] * 3,...  11.7 us
    pallas_call x1, Pallas kernels, attend(): pl.pallas_call(attend_kernel, grid=(pairs,), out_shape=[jax.ShapeDtypeStr...  11 us
    convert_element_type x8, other arithmetic, sum_low(): return total.astype(jnp.bfloat16)  10.9 us
    pallas_call x3, Pallas kernels, parts_call(): pl.pallas_call(kernel, grid=(1,), out_shape=[jax.ShapeDtypeStruct(half, j...  10.6 us
    pallas_call x3, Pallas kernels, shuffle(): pl.pallas_call(functools.partial(shuffle_kernel, moves, len(arrays)), gri...  10.2 us
    pallas_call x1, Pallas kernels, up_forward(): pl.pallas_call(up_kernel, grid=(inner // tile,), out_shape=[shape, shape]...  7.99 us
  transfers between devices with their start and end apart: 55, of which 25 were waited for; matrix products, arithmetic and copies ran while one was open for 13% of the time, Pallas kernels for 26%

profile of v1, /device:TPU:0, one launch (start us, length us, event | category | flops | bytes accessed | tf_op | source)
XLA Modules:
  0.0 267.5 jit_solution(2422879468321308569)
XLA Ops:
  3.3 5.1 %collective-permute-start.2 = (bf16[1,24,2432]{2,1,0:T(8,128)(2,1)S(1)}, bf16[1,24,2432]{2,1,0:T(8,128)(2,1)S(1)}, u32[]{:S(2)}, u32[]{:S(2)}) collective-permute-start(bf16[1,24,2432]{2,1,0:T(8,128)(2,1)S(1)} %fusion.21), channel_id=1, source_target_pairs={{0,24},{1,25},{2,26},{3,27},{4,28},{5,29},{6,30},{7,31},{8,16},{9,... | collective-permute-start | bytes 350216 | tf_op jit(solution)/shard_map/ppermute | solution.py:338
  15.2 7.2 %collective-permute-done = bf16[1,24,2432]{2,1,0:T(8,128)(2,1)S(1)} collective-permute-done((bf16[1,24,2432]{2,1,0:T(8,128)(2,1)S(1)}, bf16[1,24,2432]{2,1,0:T(8,128)(2,1)S(1)}, u32[]{:S(2)}, u32[]{:S(2)}) %collective-permute-start) | collective-permute-done | bytes 116768 | tf_op jit(solution)/shard_map/ppermute | solution.py:338
  26.1 8.6 %collective-permute-done.7 = bf16[1,24,3840]{2,1,0:T(8,128)(2,1)S(1)} collective-permute-done((bf16[1,24,3840]{2,1,0:T(8,128)(2,1)S(1)}, bf16[1,24,3840]{2,1,0:T(8,128)(2,1)S(1)}, u32[]{:S(2)}, u32[]{:S(2)}) %collective-permute-start.7) | collective-permute-done | bytes 184352 | tf_op jit(solution)/shard_map/ppermute | solution.py:338
  37.4 6.8 %collective-permute-done.5.refs_2_ = bf16[4,24,2432]{2,1,0:T(8,128)(2,1)S(1)} collective-permute-done((bf16[4,24,2432]{2,1,0:T(8,128)(2,1)S(1)}, bf16[4,24,2432]{2,1,0:T(8,128)(2,1)S(1)}, u32[]{:S(2)}, u32[]{:S(2)}) %collective-permute-start.5) | collective-permute-done | bytes 466976 | tf_op jit(solution)/shard_map/ppermute | solution.py:338
  58.3 4.3 %fusion.query_ref.key_ref.value_ref = bf16[512,2304]{1,0:T(8,128)(2,1)S(1)} fusion(bf16[512,768]{1,0:T(8,128)(2,1)S(1)} %add_convert_fusion.2.normed_ref, bf16[768,2304]{1,0:T(8,128)(2,1)} %bitcast.126, f32[2304]{0:T(1024)S(1)} %fusion.23), kind=kOutput, calls=%fused_computation.1 | convolution fusion | flops 1814298624 | bytes 6693888 | tf_op jit(solution)/shard_map/dot_general | solution.py:976
  62.6 11.0 %shard_map.272 = (bf16[512,768]{1,0:T(8,128)(2,1)S(1)}, bf16[12,512,512]{2,1,0:T(8,128)(2,1)}) custom-call(s32[1,512]{1,0:T(1,128)S(1)} %bitcast.131, s32[512,1]{1,0:T(8,128)S(1)} %copy.35.col_ref, bf16[512,2304]{1,0:T(8,128)(2,1)S(1)} %fusion.query_ref.key_ref.value_ref, bf16[512,2304]{1,0:T(8,128)(2,1)S(1)} %fusion.query_ref.key_ref.value_ref, ...), custom_call_target="tpu_custom_call" | custom-call | flops 1024 | bytes 1024 | tf_op jit(solution)/shard_map/pallas_call | solution.py:635
  74.5 11.6 %collective-permute-done.12.refs_2_ = bf16[4,24,3840]{2,1,0:T(8,128)(2,1)} collective-permute-done((bf16[4,24,3840]{2,1,0:T(8,128)(2,1)}, bf16[4,24,3840]{2,1,0:T(8,128)(2,1)}, u32[]{:S(2)}, u32[]{:S(2)}) %collective-permute-start.12) | collective-permute-done | bytes 737312 | tf_op jit(solution)/shard_map/ppermute | solution.py:338
  90.6 8.8 %collective-permute-done.23 = bf16[2,128,768]{2,1,0:T(8,128)(2,1)} collective-permute-done((bf16[2,128,768]{2,1,0:T(8,128)(2,1)}, bf16[2,128,768]{2,1,0:T(8,128)(2,1)}, u32[]{:S(2)}, u32[]{:S(2)}) %collective-permute-start.23) | collective-permute-done | bytes 393248 | tf_op jit(solution)/shard_map/ppermute | solution.py:338
  106.3 5.7 %shard_map.273 = (bf16[32,24,768]{2,1,0:T(8,128)(2,1)}, bf16[32,24,3072]{2,1,0:T(8,128)(2,1)}) custom-call(s32[1]{0:T(128)} %bitcast.19.me_ref, bf16[4,24,3840]{2,1,0:T(8,128)(2,1)} %pad_maximum_fusion.2.refs_0_, bf16[4,24,3840]{2,1,0:T(8,128)(2,1)} %collective-permute-done.11.refs_1_, bf16[4,24,3840]{2,1,0:T(8,128)(2,1)} %collective-permute-done.12.refs_2_, ...), custom_call_target="tpu_custom_call" | custom-call | flops 1024 | bytes 1024 | tf_op jit(solution)/shard_map/pallas_call | solution.py:454
  114.8 8.0 %shard_map.274 = (bf16[512,3072]{1,0:T(8,128)(2,1)S(1)}, bf16[512,3072]{1,0:T(8,128)(2,1)S(1)}) custom-call(bf16[512,768]{1,0:T(8,128)(2,1)S(1)} %add_convert_fusion.1.normed_ref, bf16[768,3072]{1,0:T(8,128)(2,1)} %bitcast.117, f32[1,3072]{1,0:T(1,128)S(1)} %reshape.197.bias_ref), custom_call_target="tpu_custom_call" | custom-call | flops 1024 | bytes 1024 | tf_op jit(solution)/shard_map/pallas_call | solution.py:706
  122.9 3.1 %shard_map.275 = (bf16[16,96,768]{2,1,0:T(8,128)(2,1)S(1)}, bf16[16,96,768]{2,1,0:T(8,128)(2,1)S(1)}) custom-call(s32[1]{0:T(128)} %bitcast.19.me_ref, bf16[512,3072]{1,0:T(8,128)(2,1)S(1)} %get-tuple-element.225.hidden_ref, bf16[512,768]{1,0:T(8,128)(2,1)S(1)} %bitcast.121), custom_call_target="tpu_custom_call" | custom-call | flops 1024 | bytes 1024 | tf_op jit(solution)/shard_map/pallas_call | solution.py:485
  129.6 4.4 %collective-permute-done.28.refs_4_ = bf16[4,96,768]{2,1,0:T(8,128)(2,1)S(1)} collective-permute-done((bf16[4,96,768]{2,1,0:T(8,128)(2,1)S(1)}, bf16[4,96,768]{2,1,0:T(8,128)(2,1)S(1)}, u32[]{:S(2)}, u32[]{:S(2)}) %collective-permute-start.28) | collective-permute-done | bytes 589856 | tf_op jit(solution)/shard_map/ppermute | solution.py:338
  143.1 7.9 %shard_map.277 = (bf16[512,3072]{1,0:T(8,128)(2,1)S(1)}, f32[1,3072]{1,0:T(1,128)S(1)}) custom-call(bf16[512,768]{1,0:T(8,128)(2,1)S(1)} %bitcast.122, bf16[3072,768]{1,0:T(8,128)(2,1)} %bitcast.132, bf16[512,3072]{1,0:T(8,128)(2,1)S(1)} %get-tuple-element.219.slope_ref), custom_call_target="tpu_custom_call" | custom-call | flops 1024 | bytes 1024 | tf_op jit(solution)/shard_map/pallas_call | solution.py:733
  151.0 5.6 %shard_map.278 = (f32[512,768]{1,0:T(8,128)S(1)}, bf16[512,768]{1,0:T(8,128)(2,1)S(1)}, bf16[512,768]{1,0:T(8,128)(2,1)S(1)}, f32[8,768]{1,0:T(8,128)S(1)}) custom-call(bf16[512,3072]{1,0:T(8,128)(2,1)S(1)} %get-tuple-element.220.pre_ref, bf16[768,3072]{1,0:T(8,128)(2,1)S(1)} %bitcast.120, f32[512,768]{1,0:T(8,128)S(1)} %get-tuple-element.356.resid_ref, ...), custom_call_target="tpu_custom_call" | custom-call | flops 1024 | bytes 1024 | tf_op jit(solution)/shard_map/pallas_call | solution.py:777
  158.6 4.0 %shard_map.279 = (bf16[16,24,3840]{2,1,0:T(8,128)(2,1)S(1)}, bf16[16,24,3840]{2,1,0:T(8,128)(2,1)S(1)}) custom-call(s32[1]{0:T(128)} %bitcast.19.me_ref, bf16[512,768]{1,0:T(8,128)(2,1)S(1)} %copy-done.21, bf16[512,768]{1,0:T(8,128)(2,1)S(1)} %get-tuple-element.221.branch_ref, bf16[512,768]{1,0:T(8,128)(2,1)S(1)} %add_convert_fusion.1.normed_ref, ...), custom_call_target="tpu_custom_call" | custom-call | flops 1024 | bytes 1024 | tf_op jit(solution)/shard_map/pallas_call | solution.py:485
  166.7 5.3 %collective-permute-done.37 = bf16[2,128,768]{2,1,0:T(8,128)(2,1)S(1)} collective-permute-done((bf16[2,128,768]{2,1,0:T(8,128)(2,1)S(1)}, bf16[2,128,768]{2,1,0:T(8,128)(2,1)S(1)}, u32[]{:S(2)}, u32[]{:S(2)}) %collective-permute-start.37) | collective-permute-done | bytes 393248 | tf_op jit(solution)/shard_map/ppermute | solution.py:338
  181.6 11.7 %shard_map.280 = (bf16[512,768]{1,0:T(8,128)(2,1)S(1)}, bf16[512,768]{1,0:T(8,128)(2,1)S(1)}, bf16[512,768]{1,0:T(8,128)(2,1)S(1)}) custom-call(bf16[512,2304]{1,0:T(8,128)(2,1)S(1)} %fusion.query_ref.key_ref.value_ref, bf16[512,2304]{1,0:T(8,128)(2,1)S(1)} %fusion.query_ref.key_ref.value_ref, bf16[512,2304]{1,0:T(8,128)(2,1)S(1)} %fusion.query_ref.key_ref.value_ref, ...), custom_call_target="tpu_custom_call" | custom-call | flops 1024 | bytes 1024 | tf_op jit(solution)/shard_map/pallas_call | solution.py:659
  193.5 3.4 %shard_map.281 = (bf16[512,768]{1,0:T(8,128)(2,1)S(1)}, f32[8,768]{1,0:T(8,128)S(1)}) custom-call(bf16[512,768]{1,0:T(8,128)(2,1)S(1)} %get-tuple-element.242.query_ref, bf16[512,768]{1,0:T(8,128)(2,1)S(1)} %get-tuple-element.243.key_ref, bf16[512,768]{1,0:T(8,128)(2,1)S(1)} %get-tuple-element.244.value_ref, bf16[768,2304]{1,0:T(8,128)(2,1)S(1)} %bitcast.127, ...), custom_call_target="tpu_custom_call" | custom-call | flops 1024 | bytes 1024 | tf_op jit(solution)/shard_map/pallas_call | solution.py:831
  202.6 3.6 %shard_map.282 = (bf16[16,24,2432]{2,1,0:T(8,128)(2,1)S(1)}, bf16[16,24,2432]{2,1,0:T(8,128)(2,1)}) custom-call(s32[1]{0:T(128)} %bitcast.19.me_ref, bf16[512,768]{1,0:T(8,128)(2,1)S(1)} %copy-done.10, bf16[512,768]{1,0:T(8,128)(2,1)S(1)} %copy-done.4, bf16[512,768]{1,0:T(8,128)(2,1)S(1)} %copy-done.6, bf16[512,768]{1,0:T(8,128)(2,1)S(1)} %copy-done.8, ...), custom_call_target="tpu_custom_call" | custom-call | flops 1024 | bytes 1024 | tf_op jit(solution)/shard_map/pallas_call | solution.py:485
  224.5 3.9 %collective-permute-done.48 = bf16[2,24,3840]{2,1,0:T(8,128)(2,1)S(1)} collective-permute-done((bf16[2,24,3840]{2,1,0:T(8,128)(2,1)S(1)}, bf16[2,24,3840]{2,1,0:T(8,128)(2,1)S(1)}, u32[]{:S(2)}, u32[]{:S(2)}) %collective-permute-start.48) | collective-permute-done | bytes 368672 | tf_op jit(solution)/shard_map/ppermute | solution.py:338
  230.0 6.3 %collective-permute-done.47 = bf16[4,24,2432]{2,1,0:T(8,128)(2,1)S(1)} collective-permute-done((bf16[4,24,2432]{2,1,0:T(8,128)(2,1)}, bf16[4,24,2432]{2,1,0:T(8,128)(2,1)S(1)}, u32[]{:S(2)}, u32[]{:S(2)}) %collective-permute-start.47) | collective-permute-done | bytes 466976 | tf_op jit(solution)/shard_map/ppermute | solution.py:338
  236.3 8.5 %collective-permute-done.46 = bf16[4,24,2432]{2,1,0:T(8,128)(2,1)S(1)} collective-permute-done((bf16[4,24,2432]{2,1,0:T(8,128)(2,1)}, bf16[4,24,2432]{2,1,0:T(8,128)(2,1)S(1)}, u32[]{:S(2)}, u32[]{:S(2)}) %collective-permute-start.46) | collective-permute-done | bytes 466976 | tf_op jit(solution)/shard_map/ppermute | solution.py:338
  255.6 3.5 %collective-permute-done.51 = bf16[1,24,2432]{2,1,0:T(8,128)(2,1)S(1)} collective-permute-done((bf16[1,24,2432]{2,1,0:T(8,128)(2,1)S(1)}, bf16[1,24,2432]{2,1,0:T(8,128)(2,1)S(1)}, u32[]{:S(2)}, u32[]{:S(2)}) %collective-permute-start.51) | collective-permute-done | bytes 116768 | tf_op jit(solution)/shard_map/ppermute | solution.py:338
  259.2 2.8 %collective-permute-done.54 = bf16[2,128,768]{2,1,0:T(8,128)(2,1)S(1)} collective-permute-done((bf16[2,128,768]{2,1,0:T(8,128)(2,1)S(1)}, bf16[2,128,768]{2,1,0:T(8,128)(2,1)S(1)}, u32[]{:S(2)}, u32[]{:S(2)}) %collective-permute-start.54) | collective-permute-done | bytes 393248 | tf_op jit(solution)/shard_map/ppermute | solution.py:338
  (264 shorter events, 115.0 us)
Async XLA Ops:
  9.1 28.4 %collective-permute-start.9 = (bf16[1,96,768]{2,1,0:T(8,128)(2,1)}, bf16[1,96,768]{2,1,0:T(8,128)(2,1)}, u32[]{:S(2)}, u32[]{:S(2)}) collective-permute-start(bf16[1,96,768]{2,1,0:T(8,128)(2,1)} %bitcast.148), channel_id=1, source_target_pairs={{0,16},{1,17},{2,18},{3,19},{4,20},{5,21},{6,22},{7,23},{8,24},{9,... | collective-permute-start | bytes 442376 | tf_op jit(solution)/shard_map/ppermute | solution.py:338
  22.5 15.0 %collective-permute-start.6 = (bf16[4,24,2432]{2,1,0:T(8,128)(2,1)S(1)}, bf16[4,24,2432]{2,1,0:T(8,128)(2,1)S(1)}, u32[]{:S(2)}, u32[]{:S(2)}) collective-permute-start(bf16[4,24,2432]{2,1,0:T(8,128)(2,1)S(1)} %pad_maximum_fusion.4.refs_0_), channel_id=1, source_target_pairs={{0,6},{1,7},{2,4},{3,5},{4,2},{5,3},{6,0},{7,1},{8,14},{9,15},{10,... | collective-permute-start | bytes 1400840 | tf_op jit(solution)/shard_map/ppermute | solution.py:338
  25.0 19.2 %collective-permute-start.5 = (bf16[4,24,2432]{2,1,0:T(8,128)(2,1)S(1)}, bf16[4,24,2432]{2,1,0:T(8,128)(2,1)S(1)}, u32[]{:S(2)}, u32[]{:S(2)}) collective-permute-start(bf16[4,24,2432]{2,1,0:T(8,128)(2,1)S(1)} %pad_maximum_fusion.4.refs_0_), channel_id=1, source_target_pairs={{0,4},{1,5},{2,6},{3,7},{4,0},{5,1},{6,2},{7,3},{8,12},{9,13},{10,... | collective-permute-start | bytes 1400840 | tf_op jit(solution)/shard_map/ppermute | solution.py:338
  25.5 18.8 %collective-permute-start.4 = (bf16[4,24,2432]{2,1,0:T(8,128)(2,1)S(1)}, bf16[4,24,2432]{2,1,0:T(8,128)(2,1)S(1)}, u32[]{:S(2)}, u32[]{:S(2)}) collective-permute-start(bf16[4,24,2432]{2,1,0:T(8,128)(2,1)S(1)} %pad_maximum_fusion.4.refs_0_), channel_id=1, source_target_pairs={{0,2},{1,3},{2,0},{3,1},{4,6},{5,7},{6,4},{7,5},{8,10},{9,11},{10,... | collective-permute-start | bytes 1400840 | tf_op jit(solution)/shard_map/ppermute | solution.py:338
  50.7 23.8 %collective-permute-start.13 = (bf16[4,24,3840]{2,1,0:T(8,128)(2,1)}, bf16[4,24,3840]{2,1,0:T(8,128)(2,1)}, u32[]{:S(2)}, u32[]{:S(2)}) collective-permute-start(bf16[4,24,3840]{2,1,0:T(8,128)(2,1)} %pad_maximum_fusion.2.refs_0_), channel_id=1, source_target_pairs={{0,6},{1,7},{2,4},{3,5},{4,2},{5,3},{6,0},{7,1},{8,14},{9,15},{10,... | collective-permute-start | bytes 2211848 | tf_op jit(solution)/shard_map/ppermute | solution.py:338
  53.2 33.0 %collective-permute-start.12 = (bf16[4,24,3840]{2,1,0:T(8,128)(2,1)}, bf16[4,24,3840]{2,1,0:T(8,128)(2,1)}, u32[]{:S(2)}, u32[]{:S(2)}) collective-permute-start(bf16[4,24,3840]{2,1,0:T(8,128)(2,1)} %pad_maximum_fusion.2.refs_0_), channel_id=1, source_target_pairs={{0,4},{1,5},{2,6},{3,7},{4,0},{5,1},{6,2},{7,3},{8,12},{9,13},{10,... | collective-permute-start | bytes 2211848 | tf_op jit(solution)/shard_map/ppermute | solution.py:338
  53.7 32.6 %collective-permute-start.11 = (bf16[4,24,3840]{2,1,0:T(8,128)(2,1)}, bf16[4,24,3840]{2,1,0:T(8,128)(2,1)}, u32[]{:S(2)}, u32[]{:S(2)}) collective-permute-start(bf16[4,24,3840]{2,1,0:T(8,128)(2,1)} %pad_maximum_fusion.2.refs_0_), channel_id=1, source_target_pairs={{0,2},{1,3},{2,0},{3,1},{4,6},{5,7},{6,4},{7,5},{8,10},{9,11},{10,... | collective-permute-start | bytes 2211848 | tf_op jit(solution)/shard_map/ppermute | solution.py:338
  54.2 20.3 %collective-permute-start.14 = (bf16[2,96,768]{2,1,0:T(8,128)(2,1)}, bf16[2,96,768]{2,1,0:T(8,128)(2,1)}, u32[]{:S(2)}, u32[]{:S(2)}) collective-permute-start(bf16[2,96,768]{2,1,0:T(8,128)(2,1)} %pad_maximum_fusion.6), channel_id=1, source_target_pairs={{0,8},{1,9},{2,10},{3,11},{4,12},{5,13},{6,14},{7,15},{8,0},{9,1},... | collective-permute-start | bytes 884744 | tf_op jit(solution)/shard_map/ppermute | solution.py:338
  100.5 25.4 %collective-permute-start.26 = (bf16[4,96,768]{2,1,0:T(8,128)(2,1)S(1)}, bf16[4,96,768]{2,1,0:T(8,128)(2,1)S(1)}, u32[]{:S(2)}, u32[]{:S(2)}) collective-permute-start(bf16[4,96,768]{2,1,0:T(8,128)(2,1)S(1)} %pad_maximum_fusion.3.refs_0_), channel_id=1, source_target_pairs={{0,6},{1,7},{2,4},{3,5},{4,2},{5,3},{6,0},{7,1},{8,14},{9,15},{10,... | collective-permute-start | bytes 1769480 | tf_op jit(solution)/shard_map/ppermute | solution.py:338
  102.2 26.3 %collective-permute-start.25 = (bf16[4,96,768]{2,1,0:T(8,128)(2,1)S(1)}, bf16[4,96,768]{2,1,0:T(8,128)(2,1)S(1)}, u32[]{:S(2)}, u32[]{:S(2)}) collective-permute-start(bf16[4,96,768]{2,1,0:T(8,128)(2,1)S(1)} %pad_maximum_fusion.3.refs_0_), channel_id=1, source_target_pairs={{0,4},{1,5},{2,6},{3,7},{4,0},{5,1},{6,2},{7,3},{8,12},{9,13},{10,... | collective-permute-start | bytes 1769480 | tf_op jit(solution)/shard_map/ppermute | solution.py:338
  103.5 25.0 %collective-permute-start.24 = (bf16[4,96,768]{2,1,0:T(8,128)(2,1)S(1)}, bf16[4,96,768]{2,1,0:T(8,128)(2,1)S(1)}, u32[]{:S(2)}, u32[]{:S(2)}) collective-permute-start(bf16[4,96,768]{2,1,0:T(8,128)(2,1)S(1)} %pad_maximum_fusion.3.refs_0_), channel_id=1, source_target_pairs={{0,2},{1,3},{2,0},{3,1},{4,6},{5,7},{6,4},{7,5},{8,10},{9,11},{10,... | collective-permute-start | bytes 1769480 | tf_op jit(solution)/shard_map/ppermute | solution.py:338
  106.2 16.6 %collective-permute-start.27 = (bf16[2,128,768]{2,1,0:T(8,128)(2,1)S(1)}, bf16[2,128,768]{2,1,0:T(8,128)(2,1)S(1)}, u32[]{:S(2)}, u32[]{:S(2)}) collective-permute-start(bf16[2,128,768]{2,1,0:T(8,128)(2,1)S(1)} %get-tuple-element.330), channel_id=1, source_target_pairs={{0,1},{1,0},{2,3},{3,2},{4,5},{5,4},{6,7},{7,6},{8,9},{9,8},{10,11... | collective-permute-start | bytes 1179656 | tf_op jit(solution)/shard_map/ppermute | solution.py:338
  137.1 28.1 %collective-permute-start.35 = (bf16[4,96,768]{2,1,0:T(8,128)(2,1)S(1)}, bf16[4,96,768]{2,1,0:T(8,128)(2,1)S(1)}, u32[]{:S(2)}, u32[]{:S(2)}) collective-permute-start(bf16[4,96,768]{2,1,0:T(8,128)(2,1)S(1)} %get-tuple-element.305), channel_id=1, source_target_pairs={{0,6},{1,7},{2,4},{3,5},{4,2},{5,3},{6,0},{7,1},{8,14},{9,15},{10,... | collective-permute-start | bytes 1769480 | tf_op jit(solution)/shard_map/ppermute | solution.py:338
  138.8 27.3 %collective-permute-start.34 = (bf16[4,96,768]{2,1,0:T(8,128)(2,1)S(1)}, bf16[4,96,768]{2,1,0:T(8,128)(2,1)S(1)}, u32[]{:S(2)}, u32[]{:S(2)}) collective-permute-start(bf16[4,96,768]{2,1,0:T(8,128)(2,1)S(1)} %get-tuple-element.306), channel_id=1, source_target_pairs={{0,4},{1,5},{2,6},{3,7},{4,0},{5,1},{6,2},{7,3},{8,12},{9,13},{10,... | collective-permute-start | bytes 1769480 | tf_op jit(solution)/shard_map/ppermute | solution.py:338
  140.1 26.0 %collective-permute-start.33 = (bf16[4,96,768]{2,1,0:T(8,128)(2,1)S(1)}, bf16[4,96,768]{2,1,0:T(8,128)(2,1)S(1)}, u32[]{:S(2)}, u32[]{:S(2)}) collective-permute-start(bf16[4,96,768]{2,1,0:T(8,128)(2,1)S(1)} %get-tuple-element.307), channel_id=1, source_target_pairs={{0,2},{1,3},{2,0},{3,1},{4,6},{5,7},{6,4},{7,5},{8,10},{9,11},{10,... | collective-permute-start | bytes 1769480 | tf_op jit(solution)/shard_map/ppermute | solution.py:338
  173.2 24.6 %collective-permute-start.38 = (bf16[2,96,768]{2,1,0:T(8,128)(2,1)}, bf16[2,96,768]{2,1,0:T(8,128)(2,1)}, u32[]{:S(2)}, u32[]{:S(2)}) collective-permute-start(bf16[2,96,768]{2,1,0:T(8,128)(2,1)} %get-tuple-element.316), channel_id=1, source_target_pairs={{0,8},{1,9},{2,10},{3,11},{4,12},{5,13},{6,14},{7,15},{8,0},{9,1},... | collective-permute-start | bytes 884744 | tf_op jit(solution)/shard_map/ppermute | solution.py:338
  175.6 33.1 %collective-permute-start.42 = (bf16[4,24,3840]{2,1,0:T(8,128)(2,1)}, bf16[4,24,3840]{2,1,0:T(8,128)(2,1)}, u32[]{:S(2)}, u32[]{:S(2)}) collective-permute-start(bf16[4,24,3840]{2,1,0:T(8,128)(2,1)} %get-tuple-element.301), channel_id=1, source_target_pairs={{0,6},{1,7},{2,4},{3,5},{4,2},{5,3},{6,0},{7,1},{8,14},{9,15},{10,... | collective-permute-start | bytes 2211848 | tf_op jit(solution)/shard_map/ppermute | solution.py:338
  177.3 33.6 %collective-permute-start.41 = (bf16[4,24,3840]{2,1,0:T(8,128)(2,1)}, bf16[4,24,3840]{2,1,0:T(8,128)(2,1)}, u32[]{:S(2)}, u32[]{:S(2)}) collective-permute-start(bf16[4,24,3840]{2,1,0:T(8,128)(2,1)} %get-tuple-element.302), channel_id=1, source_target_pairs={{0,4},{1,5},{2,6},{3,7},{4,0},{5,1},{6,2},{7,3},{8,12},{9,13},{10,... | collective-permute-start | bytes 2211848 | tf_op jit(solution)/shard_map/ppermute | solution.py:338
  178.6 32.4 %collective-permute-start.40 = (bf16[4,24,3840]{2,1,0:T(8,128)(2,1)}, bf16[4,24,3840]{2,1,0:T(8,128)(2,1)}, u32[]{:S(2)}, u32[]{:S(2)}) collective-permute-start(bf16[4,24,3840]{2,1,0:T(8,128)(2,1)} %get-tuple-element.303), channel_id=1, source_target_pairs={{0,2},{1,3},{2,0},{3,1},{4,6},{5,7},{6,4},{7,5},{8,10},{9,11},{10,... | collective-permute-start | bytes 2211848 | tf_op jit(solution)/shard_map/ppermute | solution.py:338
  213.3 16.7 %collective-permute-start.50 = (bf16[2,128,768]{2,1,0:T(8,128)(2,1)}, bf16[2,128,768]{2,1,0:T(8,128)(2,1)}, u32[]{:S(2)}, u32[]{:S(2)}) collective-permute-start(bf16[2,128,768]{2,1,0:T(8,128)(2,1)} %get-tuple-element.323), channel_id=1, source_target_pairs={{0,2},{1,3},{2,0},{3,1},{4,6},{5,7},{6,4},{7,5},{8,10},{9,11},{10,... | collective-permute-start | bytes 1179656 | tf_op jit(solution)/shard_map/ppermute | solution.py:338
  221.0 15.3 %collective-permute-start.47 = (bf16[4,24,2432]{2,1,0:T(8,128)(2,1)}, bf16[4,24,2432]{2,1,0:T(8,128)(2,1)S(1)}, u32[]{:S(2)}, u32[]{:S(2)}) collective-permute-start(bf16[4,24,2432]{2,1,0:T(8,128)(2,1)} %get-tuple-element.309), channel_id=1, source_target_pairs={{0,6},{1,7},{2,4},{3,5},{4,2},{5,3},{6,0},{7,1},{8,14},{9,15},{10,... | collective-permute-start | bytes 1400840 | tf_op jit(solution)/shard_map/ppermute | solution.py:338
  222.6 22.2 %collective-permute-start.46 = (bf16[4,24,2432]{2,1,0:T(8,128)(2,1)}, bf16[4,24,2432]{2,1,0:T(8,128)(2,1)S(1)}, u32[]{:S(2)}, u32[]{:S(2)}) collective-permute-start(bf16[4,24,2432]{2,1,0:T(8,128)(2,1)} %get-tuple-element.310), channel_id=1, source_target_pairs={{0,4},{1,5},{2,6},{3,7},{4,0},{5,1},{6,2},{7,3},{8,12},{9,13},{10,... | collective-permute-start | bytes 1400840 | tf_op jit(solution)/shard_map/ppermute | solution.py:338
  223.9 20.9 %collective-permute-start.45 = (bf16[4,24,2432]{2,1,0:T(8,128)(2,1)}, bf16[4,24,2432]{2,1,0:T(8,128)(2,1)}, u32[]{:S(2)}, u32[]{:S(2)}) collective-permute-start(bf16[4,24,2432]{2,1,0:T(8,128)(2,1)} %get-tuple-element.311), channel_id=1, source_target_pairs={{0,2},{1,3},{2,0},{3,1},{4,6},{5,7},{6,4},{7,5},{8,10},{9,11},{10,... | collective-permute-start | bytes 1400840 | tf_op jit(solution)/shard_map/ppermute | solution.py:338
  228.5 16.3 %collective-permute-start.49 = (bf16[1,24,3840]{2,1,0:T(8,128)(2,1)S(1)}, bf16[1,24,3840]{2,1,0:T(8,128)(2,1)S(1)}, u32[]{:S(2)}, u32[]{:S(2)}) collective-permute-start(bf16[1,24,3840]{2,1,0:T(8,128)(2,1)S(1)} %get-tuple-element.333), channel_id=1, source_target_pairs={{0,16},{1,17},{2,18},{3,19},{4,20},{5,21},{6,22},{7,23},{8,24},{9,... | collective-permute-start | bytes 552968 | tf_op jit(solution)/shard_map/ppermute | solution.py:338
  (72 other events, 516.5 us)

commit v2 on v1

--- a/solution.py
+++ b/solution.py
@@ -349,6 +349,11 @@
     return lax.optimization_barrier(jnp.concatenate(parts, 0))
 
 
+def halves_of(width):
+    half = width // 256 * 128
+    return ((0, half), (half, width))
+
+
 class Gather:
     def __init__(self, shard):
         self.held = shard[None]
@@ -368,17 +373,37 @@
         self.held = join(self.held, *self.got)
         self.got = [swap(self.held, mask) for mask in PLANE[1:]]
 
-    def cores_early(self):
-        self.across = [swap(self.held, CORE)]
+    def plane_one(self):
+        self.held = join(self.held, *self.got)
+        self.quads = [self.held[..., low:high] for low, high in halves_of(self.held.shape[2])]
+        self.got = [swap(quad, bit) for quad, bit in zip(self.quads, (X, Y))]
+
+    def plane_two(self):
+        own = []
+        for quad, got, bit in zip(self.quads, self.got, (Y, X)):
+            eight = join(quad, got)
+            own += [eight, swap(eight, bit)]
+        self.held, self.got = own[0], own[1:]
 
     def cores(self):
         own = [self.held, *self.got]
-        self.parts = own + self.across + [swap(piece, CORE) for piece in own[len(self.across) :]]
+        self.parts = own + [swap(piece, CORE) for piece in own]
 
     def places(self):
-        masks = [core ^ plane ^ line for core in (0, CORE) for plane in PLANE for line in LINE]
         width = self.held.shape[2]
-        return [(i // 4, i % 4, mask, 0, width) for i, mask in enumerate(masks)]
+        if self.held.shape[0] == 4:
+            masks = [core ^ plane ^ line for core in (0, CORE) for plane in PLANE for line in LINE]
+            return [(i // 4, i % 4, mask, 0, width) for i, mask in enumerate(masks)]
+        spans = ((0, width), (width, width + self.got[1].shape[2]))
+        return [
+            (4 * core + 2 * half + second, 4 * first + i, mask, low, high)
+            for core in (0, CORE)
+            for half, ((low, high), bits) in enumerate(zip(spans, ((X, Y), (Y, X))))
+            for second in (0, 1)
+            for first in (0, 1)
+            for i, line in enumerate(LINE)
+            for mask in (core ^ line ^ bits[0] * first ^ bits[1] * second,)
+        ]
 
 
 def sum_low(*terms):
@@ -411,6 +436,32 @@
         ones = [sum_low(*(term[i : i + 1] for term in terms)) for i in range(1, 4)]
         self.kept = sum(term[0].astype(jnp.float32) for term in terms)
         self.got = [swap(one, mask) for one, mask in zip(ones, LINE[1:])]
+
+    def plane_one(self):
+        kept, got = [], []
+        spans = halves_of(self.kept.shape[2])
+        for (low, high), bit, order in zip(spans, (Y, X), ((0, 1, 2, 3), (0, 2, 1, 3))):
+            quads = [
+                sum_low(
+                    self.kept[4 * i : 4 * i + 4, :, low:high],
+                    self.got[4 * i : 4 * i + 4, :, low:high],
+                )
+                for i in order
+            ]
+            kept.append(quads[:2])
+            got.append(swap(jnp.concatenate(quads[2:], 0), bit))
+        self.kept, self.got = kept, got
+
+    def plane_two(self):
+        sent = [
+            swap(sum_low(kept[1], got[4:]), bit)
+            for kept, got, bit in zip(self.kept, self.got, (X, Y))
+        ]
+        kept = [sum_low(kept[0], got[:4]) for kept, got in zip(self.kept, self.got)]
+        self.kept, self.got = jnp.concatenate(kept, -1), sent
+
+    def plane_end(self):
+        self.got = [jnp.concatenate(self.got, -1)]
 
     def near(self):
         terms = [self.kept, *self.got]
@@ -463,7 +514,7 @@
     )(me, *arrays)
 
 
-def restore(gather, cuts, me):
+def restore(gather, cuts, me, pinned=True):
     moves = []
     for part, slot, mask, low, high in gather.places():
         for target, (begin, end) in enumerate(cuts):
@@ -474,7 +525,7 @@
                 )
     rows = gather.parts[0].shape[1]
     shapes = [(DEVICES, rows, end - begin) for begin, end in cuts]
-    return shuffle(gather.parts, shapes, moves, me, True)
+    return shuffle(gather.parts, shapes, moves, me, pinned)
 
 
 TN = (((0,), (0,)), ((), ()))
@@ -528,12 +579,32 @@
 
 
 def first_parts_kernel(
-    me_ref, normed_ref, query_ref, key_ref, value_ref, sums_ref, kept_ref, sent_ref, sum_ref
+    me_ref,
+    normed_ref,
+    query_ref,
+    key_ref,
+    value_ref,
+    one_ref,
+    two_ref,
+    bias_ref,
+    kept_ref,
+    sent_ref,
+    sum_ref,
 ):
     me, outs = me_ref[0], (kept_ref, sent_ref)
     low = multiply_rows(me, normed_ref, [query_ref, key_ref, value_ref], sum_ref, outs, 0)
+    rows = kept_ref.shape[1]
+    vectors = jnp.concatenate([one_ref[:4], two_ref[:4]], 0)
+    width, bias = vectors.shape[1], jnp.broadcast_to(bias_ref[...], (8, bias_ref.shape[1]))
+    deep = bias.shape[1] // DEVICES
+    spare = jnp.zeros((rows - 16, 128), jnp.float32)
     for half, slot, mask in Scatter.places:
-        outs[half][slot, :, low:] = sums_ref[lax.bitwise_xor(me, mask)]
+        owner = lax.bitwise_xor(me, mask)
+        here = pltpu.roll(vectors, lax.rem(width - rows * owner, width), 1)[:, :128]
+        bias_here = pltpu.roll(bias, lax.rem(DEVICES * deep - deep * owner, DEVICES * deep), 1)
+        outs[half][slot, :, low:] = jnp.concatenate(
+            [here, bias_here[:, :128], spare], 0
+        ).astype(jnp.bfloat16)
 
 
 def third_parts_kernel(me_ref, hidden_ref, cot_ref, kept_ref, sent_ref, sum_ref):
@@ -688,19 +759,21 @@
 
 def up_kernel(normed_ref, weight_ref, bias_ref, hidden_ref, slope_ref):
     bf16 = jnp.bfloat16
-    pre = jnp.dot(normed_ref[...], weight_ref[...], preferred_element_type=jnp.float32)
-    pre = pre + bias_ref[...]
-    square = pre * pre
-    bend = jnp.tanh(pre * (0.7978845608028654 + 0.7978845608028654 * 0.044715 * square))
-    half = 0.5 * (1.0 + bend)
-    hidden_ref[...] = (pre * half).astype(bf16)
-    inner = 0.7978845608028654 + 3 * 0.7978845608028654 * 0.044715 * square
-    slope_ref[...] = (half + 0.5 * pre * (1.0 - bend * bend) * inner).astype(bf16)
+    first, third = 0.7978845608028654, 0.7978845608028654 * 0.044715
+    for row in range(0, normed_ref.shape[0], 128):
+        rows = slice(row, row + 128)
+        pre = jnp.dot(normed_ref[rows], weight_ref[...], preferred_element_type=jnp.float32)
+        pre = pre + bias_ref[...]
+        square = pre * pre
+        half = 0.5 + 0.5 * jnp.tanh(pre * (first + third * square))
+        hidden_ref[rows] = (pre * half).astype(bf16)
+        inner = pre * (2 * first + 6 * third * square)
+        slope_ref[rows] = (half + half * inner * (1.0 - half)).astype(bf16)
 
 
 def up_forward(normed, up_full, bias_row):
     tokens, width = normed.shape
-    inner, tile = up_full.shape[1], 512
+    inner, tile = up_full.shape[1], 768
     block = pl.BlockSpec((tokens, tile), lambda i: (0, i))
     shape = jax.ShapeDtypeStruct((tokens, inner), jnp.bfloat16)
     return pl.pallas_call(
@@ -713,7 +786,7 @@
             pl.BlockSpec((1, tile), lambda i: (0, i)),
         ],
         out_specs=[block, block],
-        compiler_params=pltpu.CompilerParams(vmem_limit_bytes=14 * MIB),
+        compiler_params=pltpu.CompilerParams(vmem_limit_bytes=18 * MIB),
         cost_estimate=SMALL,
     )(normed, in_hbm(up_full), bias_row)
 
@@ -745,7 +818,7 @@
         out_specs=[block, pl.BlockSpec((1, tile), lambda i: (0, i))],
         compiler_params=pltpu.CompilerParams(vmem_limit_bytes=12 * MIB),
         cost_estimate=SMALL,
-    )(cot_low, in_hbm(down_full), slope)
+    )(cot_low, down_full, slope)
 
 
 def middle_kernel(pre_ref, up_ref, resid_ref, gain_ref, cot_ref, out_ref, mid_ref, low_ref, mixed_ref, sums_ref):
@@ -875,9 +948,9 @@
     return parts[0], swap(parts[1], CORE)
 
 
-def from_micro_x(kept, got, core):
+def from_micro_pick(kept, got, core):
     both = jnp.where(core == 0, jnp.stack([kept, got]), jnp.stack([got, kept]))
-    return both[:, 0], swap(both[:, 1], 2)
+    return both[:, 0], both[:, 1]
 
 
 def from_micro_end(kept, got, side):
@@ -922,10 +995,12 @@
         down_bias,
     )
     row = lax.broadcasted_iota(jnp.int32, (rows, rows), 0)
-    block = jnp.pad(up_bias.reshape(4, rows), ((8, rows - 12), (0, 0)))
+    block = jnp.zeros((rows, rows), bf16)
     for j, vector in enumerate(vectors):
         block = jnp.where(row == j, vector[None], block)
     block = jnp.pad(block, ((0, 0), (0, 128 - rows)))
+    row = lax.broadcasted_iota(jnp.int32, (rows, 128), 0)
+    block = jnp.where(row == 8, jnp.pad(up_bias, (0, 128 - up_bias.shape[0]))[None], block)
     first = Gather(jnp.concatenate([qkv_weight, block], 1))
     second = Gather(jnp.concatenate([out_weight, up_weight], 1))
     third = Gather(down_weight)
@@ -943,23 +1018,22 @@
     first.plane()
     second.far()
     second.near()
-    third.far()
     token_kept, token_got = to_micro_c(token_got, token_halves, side, core)
     tokens = to_micro_end(token_kept, token_got)
     resid_in = tokens.astype(f32)
     unit_one, _ = norm_parts(resid_in)
-    first.held, first.got, second.held, second.got, third.held, third.got, unit_one = fence(
-        first.held, first.got, second.held, second.got, third.held, third.got, unit_one
+    first.held, first.got, second.held, second.got, third.held, unit_one = fence(
+        first.held, first.got, second.held, second.got, third.held, unit_one
     )
 
     first.cores()
-    second.plane()
-    third.near()
+    second.plane_one()
+    third.far()
     qkv_full, vectors = restore(first, cuts_of((wide, 128)), me)
     qkv_full = qkv_full.reshape(width, wide)
-    vectors = vectors[:, :12, :rows].astype(f32)
-    bias_up = vectors[:, 8:].reshape(1, -1)
-    (vectors,) = fence(vectors[:, :8].transpose(1, 0, 2).reshape(8, width))
+    vectors = vectors[:, :9].astype(f32)
+    bias_up = vectors[:, 8, : up_bias.shape[0]].reshape(1, -1)
+    (vectors,) = fence(vectors[:, :8, :rows].transpose(1, 0, 2).reshape(8, width))
     (
         gain_one,
         shift_one,
@@ -975,6 +1049,12 @@
     project = (
         jnp.dot(normed_one, qkv_full, preferred_element_type=f32) + bias_project
     ).astype(bf16)
+    second.quads, second.got, third.held, third.got, project = fence(
+        second.quads, second.got, third.held, third.got, project
+    )
+
+    second.plane_two()
+    third.near()
     mixed, probs = attend(labels, project)
     second.held, second.got, third.held, third.got, mixed, cotangent = fence(
         second.held, second.got, third.held, third.got, mixed, cotangent
@@ -1011,13 +1091,33 @@
         third.parts, down_sum.kept, down_sum.got, hidden, cot_low
     )
 
-    down_sum.plane()
-    (down_full,) = restore(third, cuts_of((width,)), me)
+    down_sum.plane_one()
+    (down_full,) = restore(third, cuts_of((width,)), me, False)
     down_full = down_full.reshape(inner, width)
     grad_pre, grad_bias_up = pre_back(cot_low, down_full, slope)
     grad_mid, branch_low, grad_mixed, sums_two = middle_back(
         grad_pre, up_full, resid_mid, gain_two, cot_low, out_full
     )
+    (
+        down_sum.kept,
+        down_sum.got,
+        grad_mid,
+        branch_low,
+        grad_mixed,
+        grad_pre,
+        down_full,
+        hidden,
+    ) = fence(
+        down_sum.kept,
+        down_sum.got,
+        grad_mid,
+        branch_low,
+        grad_mixed,
+        grad_pre,
+        down_full,
+        hidden,
+    )
+    down_sum.plane_two()
     up_sum = Scatter(
         parts_call(
             second_parts_kernel,
@@ -1029,41 +1129,60 @@
             me,
         )
     )
+    down_sum.kept, down_sum.got, up_sum.kept, up_sum.sent, grad_mixed, hidden, down_full = fence(
+        down_sum.kept, down_sum.got, up_sum.kept, up_sum.sent, grad_mixed, hidden, down_full
+    )
+
+    up_sum.cores()
+    down_sum.plane_end()
     result = resid_mid + jnp.dot(hidden, down_full, preferred_element_type=f32) + bias_down
     result = result.astype(bf16)
-    down_sum.kept, down_sum.got, up_sum.kept, up_sum.sent, grad_mixed, result = fence(
-        down_sum.kept, down_sum.got, up_sum.kept, up_sum.sent, grad_mixed, result
-    )
-
-    up_sum.cores()
+    down_sum.kept, down_sum.got, up_sum.kept, up_sum.got, grad_mixed, result = fence(
+        down_sum.kept, down_sum.got, up_sum.kept, up_sum.got, grad_mixed, result
+    )
+
+    up_sum.plane_one()
+    down_sum.near()
     out_kept, out_got = from_micro_c(result)
+    grad_query, grad_key, grad_value = attend_back(project, probs, grad_mixed)
     (
         down_sum.kept,
         down_sum.got,
         up_sum.kept,
         up_sum.got,
-        grad_mixed,
+        grad_query,
+        grad_key,
+        grad_value,
         out_kept,
         out_got,
     ) = fence(
-        down_sum.kept, down_sum.got, up_sum.kept, up_sum.got, grad_mixed, out_kept, out_got
-    )
-
-    up_sum.plane()
-    down_sum.near()
+        down_sum.kept,
+        down_sum.got,
+        up_sum.kept,
+        up_sum.got,
+        grad_query,
+        grad_key,
+        grad_value,
+        out_kept,
+        out_got,
+    )
+    up_sum.plane_two()
     down_sum.far()
-    grad_query, grad_key, grad_value = attend_back(project, probs, grad_mixed)
     in_grad, sums_one = first_back(
         grad_query, grad_key, grad_value, qkv_full, tokens, gain_one, grad_mid
     )
-    sums = jnp.concatenate([sums_one[:4], sums_two[:4]], 0)
-    sums = sums.reshape(8, DEVICES, rows).transpose(1, 0, 2)
-    sums = jnp.concatenate([sums, grad_bias_up.reshape(DEVICES, 4, rows)], 1)
-    sums = jnp.pad(sums, ((0, 0), (0, rows - 12), (0, 128 - rows))).astype(bf16)
     qkv_sum = Scatter(
         parts_call(
             first_parts_kernel,
-            [normed_one, grad_query, grad_key, grad_value, sums],
+            [
+                normed_one,
+                grad_query,
+                grad_key,
+                grad_value,
+                sums_one,
+                sums_two,
+                grad_bias_up,
+            ],
             rows,
             wide + 128,
             (width, width),
@@ -1093,41 +1212,65 @@
         out_got,
     )
 
+    up_sum.plane_end()
     qkv_sum.cores()
     in_kept, in_got = from_micro_c(in_grad)
+    out_kept, out_sent = from_micro_pick(out_kept, out_got, core)
     (
-        down_sum.kept,
-        down_sum.got,
         up_sum.kept,
         up_sum.got,
         qkv_sum.kept,
         qkv_sum.got,
         in_kept,
         in_got,
+        out_kept,
+        out_sent,
     ) = fence(
-        down_sum.kept,
-        down_sum.got,
         up_sum.kept,
         up_sum.got,
         qkv_sum.kept,
         qkv_sum.got,
         in_kept,
         in_got,
-    )
-
-    qkv_sum.plane()
+        out_kept,
+        out_sent,
+    )
+
+    qkv_sum.plane_one()
     up_sum.near()
-    up_sum.far()
-    out_kept, out_got = from_micro_x(out_kept, out_got, core)
+    in_kept, in_sent = from_micro_pick(in_kept, in_got, core)
+    grad_down = down_sum.total()
     (
         qkv_sum.kept,
         qkv_sum.got,
         up_sum.kept,
         up_sum.got,
-        down_sum.kept,
-        down_sum.got,
         in_kept,
-        in_got,
+        in_sent,
+        out_kept,
+        out_sent,
+        grad_down,
+    ) = fence(
+        qkv_sum.kept,
+        qkv_sum.got,
+        up_sum.kept,
+        up_sum.got,
+        in_kept,
+        in_sent,
+        out_kept,
+        out_sent,
+        grad_down,
+    )
+    qkv_sum.plane_two()
+    up_sum.far()
+    out_got = swap(out_sent, X)
+    (
+        qkv_sum.kept,
+        qkv_sum.got,
+        up_sum.kept,
+        up_sum.got,
+        in_kept,
+        in_sent,
         out_kept,
         out_got,
     ) = fence(
@@ -1135,28 +1278,26 @@
         qkv_sum.got,
         up_sum.kept,
         up_sum.got,
-        down_sum.kept,
-        down_sum.got,
         in_kept,
-        in_got,
+        in_sent,
         out_kept,
         out_got,
     )
 
+    in_got = swap(in_sent, X)
+    qkv_sum.plane_end()
     qkv_sum.line()
-    in_kept, in_got = from_micro_x(in_kept, in_got, core)
-    grad_down = down_sum.total()
     last = up_sum.total()
     grad_out, grad_up = last[:, :width], last[:, width:]
-    qkv_sum.kept, qkv_sum.got, in_kept, in_got, out_kept, out_got = fence(
-        qkv_sum.kept, qkv_sum.got, in_kept, in_got, out_kept, out_got
-    )
-
     output = from_micro_end(out_kept, out_got, side)
+    qkv_sum.kept, qkv_sum.got, in_kept, in_got, output, grad_out, grad_up = fence(
+        qkv_sum.kept, qkv_sum.got, in_kept, in_got, output, grad_out, grad_up
+    )
+
     in_grad = from_micro_end(in_kept, in_got, side).astype(f32)
     last = qkv_sum.total()
     grad_qkv = last[:, :wide]
-    sums = last[:12, wide : wide + rows]
+    deep, sums = last[8, wide : wide + deep], last[:8, wide : wide + rows]
     return (
         output,
         in_grad,
@@ -1170,7 +1311,7 @@
         sums[5],
         sums[6],
         grad_up,
-        sums[8:12].reshape(-1),
+        deep,
         grad_down,
         sums[7],
     )

time: 268 us -> 250 us (0.933)
  waiting for transfers between devices: 93.1 us -> 82.2 us
  local copies, waits for them, and re-layouts: 19 us -> 12 us
  starting transfers between devices: 49.1 us -> 55.9 us
  Pallas kernels: 68.3 us -> 61.7 us
    ppermute x55 -> x59, waiting for transfers between devices: 93.1 us -> 82.2 us  [swap(): return lax.ppermute(values, AXES, pairs)]
    ppermute x55 -> x59, starting transfers between devices: 49.1 us -> 55.9 us  [swap(): return lax.ppermute(values, AXES, pairs)]
    unnamed x82 -> x33, local copies, waits for them, and re-layouts: 7.68 us -> 1.24 us
    convert_element_type x8 -> x15, other arithmetic: 10.9 us -> 6.77 us  [sum_low(): return total.astype(jnp.bfloat16)]
    pallas_call x1, Pallas kernels: 7.85 us -> 4.39 us  [pre_back(): pl.pallas_call(pre_kernel, grid=(inner // tile,), out_shape=[jax.ShapeDty...]
    concatenate x5 -> x7, other arithmetic: 3.82 us -> 6.99 us  [join(): return lax.optimization_barrier(jnp.concatenate(parts, 0))]
  transfers between devices with their start and end apart: 55 -> 59, of which waited for: 25 -> 31; matrix products, arithmetic and copies ran while one was open for 13% -> 12% of each run, Pallas kernels for 26% -> 25%
where the time goes in v2:
time: 250 us; the launch traced here: 249 us
  waiting for transfers between devices  82.2 us (33%)
  Pallas kernels  61.7 us (25%)
  starting transfers between devices  55.9 us (22%)
  other arithmetic  26.8 us (11%)
  local copies, waits for them, and re-layouts  12 us (5%)
  matrix products  9.07 us (4%)
    ppermute x59, waiting for transfers between devices, swap(): return lax.ppermute(values, AXES, pairs)  82.2 us
    ppermute x59, starting transfers between devices, swap(): return lax.ppermute(values, AXES, pairs)  55.9 us
    pallas_call x1, Pallas kernels, attend_back(): pl.pallas_call(attend_back_kernel, grid=(pairs,), out_shape=[shape] * 3,...  11.6 us
    pallas_call x1, Pallas kernels, attend(): pl.pallas_call(attend_kernel, grid=(pairs,), out_shape=[jax.ShapeDtypeStr...  11.1 us
    pallas_call x3, Pallas kernels, parts_call(): pl.pallas_call(kernel, grid=(1,), out_shape=[jax.ShapeDtypeStruct(half, j...  10.8 us
    pallas_call x3, Pallas kernels, shuffle(): pl.pallas_call(functools.partial(shuffle_kernel, moves, len(arrays)), gri...  8.08 us
    concatenate x7, other arithmetic, join(): return lax.optimization_barrier(jnp.concatenate(parts, 0))  6.99 us
    convert_element_type x15, other arithmetic, sum_low(): return total.astype(jnp.bfloat16)  6.77 us
  transfers between devices with their start and end apart: 59, of which 31 were waited for; matrix products, arithmetic and copies ran while one was open for 12% of the time, Pallas kernels for 25%

profile of v2, /device:TPU:0, one launch (start us, length us, event | category | flops | bytes accessed | tf_op | source)
XLA Modules:
  0.0 249.0 jit_solution(8517313190578792098)
XLA Ops:
  3.3 5.1 %collective-permute-start.2 = (bf16[1,24,2432]{2,1,0:T(8,128)(2,1)S(1)}, bf16[1,24,2432]{2,1,0:T(8,128)(2,1)S(1)}, u32[]{:S(2)}, u32[]{:S(2)}) collective-permute-start(bf16[1,24,2432]{2,1,0:T(8,128)(2,1)S(1)} %maximum_bitcast_fusion.1), channel_id=1, source_target_pairs={{0,24},{1,25},{2,26},{3,27},{4,28},{5,29},{6,30},{7,31},{8,16},{9,... | collective-permute-start | bytes 350216 | tf_op jit(solution)/shard_map/ppermute | solution.py:338
  12.5 2.7 %collective-permute-done.1 = bf16[1,24,2432]{2,1,0:T(8,128)(2,1)S(1)} collective-permute-done((bf16[1,24,2432]{2,1,0:T(8,128)(2,1)S(1)}, bf16[1,24,2432]{2,1,0:T(8,128)(2,1)S(1)}, u32[]{:S(2)}, u32[]{:S(2)}) %collective-permute-start.1) | collective-permute-done | bytes 116768 | tf_op jit(solution)/shard_map/ppermute | solution.py:338
  15.2 3.1 %collective-permute-done = bf16[1,24,2432]{2,1,0:T(8,128)(2,1)S(1)} collective-permute-done((bf16[1,24,2432]{2,1,0:T(8,128)(2,1)S(1)}, bf16[1,24,2432]{2,1,0:T(8,128)(2,1)S(1)}, u32[]{:S(2)}, u32[]{:S(2)}) %collective-permute-start) | collective-permute-done | bytes 116768 | tf_op jit(solution)/shard_map/ppermute | solution.py:338
  25.6 6.5 %collective-permute-done.7 = bf16[1,24,3840]{2,1,0:T(8,128)(2,1)S(1)} collective-permute-done((bf16[1,24,3840]{2,1,0:T(8,128)(2,1)S(1)}, bf16[1,24,3840]{2,1,0:T(8,128)(2,1)S(1)}, u32[]{:S(2)}, u32[]{:S(2)}) %collective-permute-start.7) | collective-permute-done | bytes 184352 | tf_op jit(solution)/shard_map/ppermute | solution.py:338
  34.2 7.3 %collective-permute-done.5.refs_2_ = bf16[4,24,2432]{2,1,0:T(8,128)(2,1)S(1)} collective-permute-done((bf16[4,24,2432]{2,1,0:T(8,128)(2,1)S(1)}, bf16[4,24,2432]{2,1,0:T(8,128)(2,1)S(1)}, u32[]{:S(2)}, u32[]{:S(2)}) %collective-permute-start.5) | collective-permute-done | bytes 466976 | tf_op jit(solution)/shard_map/ppermute | solution.py:338
  51.8 4.3 %fusion.query_ref.key_ref.value_ref = bf16[512,2304]{1,0:T(8,128)(2,1)S(1)} fusion(bf16[512,768]{1,0:T(8,128)(2,1)S(1)} %add_convert_fusion.2.normed_ref, bf16[768,2304]{1,0:T(8,128)(2,1)} %bitcast.127, f32[2304]{0:T(1024)S(1)} %fusion.14), kind=kOutput, calls=%fused_computation.1 | convolution fusion | flops 1814298624 | bytes 6693888 | tf_op jit(solution)/shard_map/dot_general | solution.py:1050
  68.1 11.1 %shard_map.272 = (bf16[512,768]{1,0:T(8,128)(2,1)S(1)}, bf16[12,512,512]{2,1,0:T(8,128)(2,1)}) custom-call(s32[1,512]{1,0:T(1,128)S(1)} %bitcast.132, s32[512,1]{1,0:T(8,128)S(1)} %copy.35.col_ref, bf16[512,2304]{1,0:T(8,128)(2,1)S(1)} %fusion.query_ref.key_ref.value_ref, bf16[512,2304]{1,0:T(8,128)(2,1)S(1)} %fusion.query_ref.key_ref.value_ref, ...), custom_call_target="tpu_custom_call" | custom-call | flops 1024 | bytes 1024 | tf_op jit(solution)/shard_map/pallas_call | solution.py:706
  84.2 9.5 %collective-permute-done.24 = bf16[2,128,768]{2,1,0:T(8,128)(2,1)} collective-permute-done((bf16[2,128,768]{2,1,0:T(8,128)(2,1)}, bf16[2,128,768]{2,1,0:T(8,128)(2,1)}, u32[]{:S(2)}, u32[]{:S(2)}) %collective-permute-start.24) | collective-permute-done | bytes 393248 | tf_op jit(solution)/shard_map/ppermute | solution.py:338
  100.6 5.7 %shard_map.273 = (bf16[32,24,768]{2,1,0:T(8,128)(2,1)}, bf16[32,24,3072]{2,1,0:T(8,128)(2,1)}) custom-call(s32[1]{0:T(128)} %bitcast.12.me_ref, bf16[8,24,1920]{2,1,0:T(8,128)(2,1)} %pad_maximum_fusion.3.refs_0_, bf16[8,24,1920]{2,1,0:T(8,128)(2,1)} %collective-permute-done.17.refs_1_, bf16[8,24,1920]{2,1,0:T(8,128)(2,1)} %pad_maximum_fusion.4.refs_2_, ...), custom_call_target="tpu_custom_call" | custom-call | flops 1024 | bytes 1024 | tf_op jit(solution)/shard_map/pallas_call | solution.py:505
  109.1 6.7 %shard_map.274 = (bf16[512,3072]{1,0:T(8,128)(2,1)S(1)}, bf16[512,3072]{1,0:T(8,128)(2,1)S(1)}) custom-call(bf16[512,768]{1,0:T(8,128)(2,1)S(1)} %add_convert_fusion.1.normed_ref, bf16[768,3072]{1,0:T(8,128)(2,1)} %bitcast.116, f32[1,3072]{1,0:T(1,128)S(1)} %reshape_squeeze.3.bias_ref), custom_call_target="tpu_custom_call" | custom-call | flops 1024 | bytes 1024 | tf_op jit(solution)/shard_map/pallas_call | solution.py:779
  115.8 3.1 %shard_map.275 = (bf16[16,96,768]{2,1,0:T(8,128)(2,1)S(1)}, bf16[16,96,768]{2,1,0:T(8,128)(2,1)S(1)}) custom-call(s32[1]{0:T(128)} %bitcast.12.me_ref, bf16[512,3072]{1,0:T(8,128)(2,1)S(1)} %get-tuple-element.286.hidden_ref, bf16[512,768]{1,0:T(8,128)(2,1)S(1)} %bitcast.122), custom_call_target="tpu_custom_call" | custom-call | flops 1024 | bytes 1024 | tf_op jit(solution)/shard_map/pallas_call | solution.py:536
  119.0 3.8 %collective-permute-done.26.refs_2_ = bf16[4,96,768]{2,1,0:T(8,128)(2,1)S(1)} collective-permute-done((bf16[4,96,768]{2,1,0:T(8,128)(2,1)S(1)}, bf16[4,96,768]{2,1,0:T(8,128)(2,1)S(1)}, u32[]{:S(2)}, u32[]{:S(2)}) %collective-permute-start.26) | collective-permute-done | bytes 589856 | tf_op jit(solution)/shard_map/ppermute | solution.py:338
  123.8 4.3 %collective-permute-done.29.refs_4_ = bf16[4,96,768]{2,1,0:T(8,128)(2,1)S(1)} collective-permute-done((bf16[4,96,768]{2,1,0:T(8,128)(2,1)S(1)}, bf16[4,96,768]{2,1,0:T(8,128)(2,1)S(1)}, u32[]{:S(2)}, u32[]{:S(2)}) %collective-permute-start.29) | collective-permute-done | bytes 589856 | tf_op jit(solution)/shard_map/ppermute | solution.py:338
  134.1 4.4 %shard_map.277 = (bf16[512,3072]{1,0:T(8,128)(2,1)S(1)}, f32[1,3072]{1,0:T(1,128)S(1)}) custom-call(bf16[512,768]{1,0:T(8,128)(2,1)S(1)} %bitcast.123, bf16[3072,768]{1,0:T(8,128)(2,1)S(1)} %bitcast.120, bf16[512,3072]{1,0:T(8,128)(2,1)S(1)} %get-tuple-element.261.slope_ref), custom_call_target="tpu_custom_call" | custom-call | flops 1024 | bytes 1024 | tf_op jit(solution)/shard_map/pallas_call | solution.py:806
  138.5 5.6 %shard_map.278 = (f32[512,768]{1,0:T(8,128)S(1)}, bf16[512,768]{1,0:T(8,128)(2,1)S(1)}, bf16[512,768]{1,0:T(8,128)(2,1)S(1)}, f32[8,768]{1,0:T(8,128)S(1)}) custom-call(bf16[512,3072]{1,0:T(8,128)(2,1)S(1)} %get-tuple-element.274.pre_ref, bf16[768,3072]{1,0:T(8,128)(2,1)S(1)} %bitcast.119, f32[512,768]{1,0:T(8,128)S(1)} %get-tuple-element.454.resid_ref, ...), custom_call_target="tpu_custom_call" | custom-call | flops 1024 | bytes 1024 | tf_op jit(solution)/shard_map/pallas_call | solution.py:850
  144.1 2.8 %collective-permute-done.34 = bf16[8,96,384]{2,1,0:T(8,128)(2,1)S(1)} collective-permute-done((bf16[8,96,384]{2,1,0:T(8,128)(2,1)S(1)}, bf16[8,96,384]{2,1,0:T(8,128)(2,1)S(1)}, u32[]{:S(2)}, u32[]{:S(2)}) %collective-permute-start.34) | collective-permute-done | bytes 589856 | tf_op jit(solution)/shard_map/ppermute | solution.py:338
  150.0 4.0 %shard_map.279 = (bf16[16,24,3840]{2,1,0:T(8,128)(2,1)S(1)}, bf16[16,24,3840]{2,1,0:T(8,128)(2,1)S(1)}) custom-call(s32[1]{0:T(128)} %bitcast.12.me_ref, bf16[512,768]{1,0:T(8,128)(2,1)S(1)} %copy-done.8, bf16[512,768]{1,0:T(8,128)(2,1)S(1)} %get-tuple-element.273.branch_ref, bf16[512,768]{1,0:T(8,128)(2,1)S(1)} %add_convert_fusion.1.normed_ref, ...), custom_call_target="tpu_custom_call" | custom-call | flops 1024 | bytes 1024 | tf_op jit(solution)/shard_map/pallas_call | solution.py:536
  159.6 2.7 %collective-permute-done.38 = bf16[16,24,3840]{2,1,0:T(8,128)(2,1)S(1)} collective-permute-done((bf16[16,24,3840]{2,1,0:T(8,128)(2,1)S(1)}, bf16[16,24,3840]{2,1,0:T(8,128)(2,1)S(1)}, u32[]{:S(2)}, u32[]{:S(2)}) %collective-permute-start.38) | collective-permute-done | bytes 2949152 | tf_op jit(solution)/shard_map/ppermute | solution.py:338
  167.6 11.6 %shard_map.280 = (bf16[512,768]{1,0:T(8,128)(2,1)S(1)}, bf16[512,768]{1,0:T(8,128)(2,1)S(1)}, bf16[512,768]{1,0:T(8,128)(2,1)S(1)}) custom-call(bf16[512,2304]{1,0:T(8,128)(2,1)S(1)} %fusion.query_ref.key_ref.value_ref, bf16[512,2304]{1,0:T(8,128)(2,1)S(1)} %fusion.query_ref.key_ref.value_ref, bf16[512,2304]{1,0:T(8,128)(2,1)S(1)} %fusion.query_ref.key_ref.value_ref, ...), custom_call_target="tpu_custom_call" | custom-call | flops 1024 | bytes 1024 | tf_op jit(solution)/shard_map/pallas_call | solution.py:730
  186.3 3.4 %shard_map.281 = (bf16[512,768]{1,0:T(8,128)(2,1)S(1)}, f32[8,768]{1,0:T(8,128)S(1)}) custom-call(bf16[512,768]{1,0:T(8,128)(2,1)S(1)} %get-tuple-element.306.query_ref, bf16[512,768]{1,0:T(8,128)(2,1)S(1)} %get-tuple-element.307.key_ref, bf16[512,768]{1,0:T(8,128)(2,1)S(1)} %get-tuple-element.308.value_ref, bf16[768,2304]{1,0:T(8,128)(2,1)S(1)} %bitcast.128, ...), custom_call_target="tpu_custom_call" | custom-call | flops 1024 | bytes 1024 | tf_op jit(solution)/shard_map/pallas_call | solution.py:904
  189.7 3.8 %shard_map.282 = (bf16[16,24,2432]{2,1,0:T(8,128)(2,1)S(1)}, bf16[16,24,2432]{2,1,0:T(8,128)(2,1)}) custom-call(s32[1]{0:T(128)} %bitcast.12.me_ref, bf16[512,768]{1,0:T(8,128)(2,1)S(1)} %copy-done.4, bf16[512,768]{1,0:T(8,128)(2,1)S(1)} %get-tuple-element.306.query_ref, bf16[512,768]{1,0:T(8,128)(2,1)S(1)} %get-tuple-element.307.key_ref, ...), custom_call_target="tpu_custom_call" | custom-call | flops 1024 | bytes 1024 | tf_op jit(solution)/shard_map/pallas_call | solution.py:536
  206.7 8.3 %collective-permute-done.50 = bf16[2,24,3840]{2,1,0:T(8,128)(2,1)S(1)} collective-permute-done((bf16[2,24,3840]{2,1,0:T(8,128)(2,1)S(1)}, bf16[2,24,3840]{2,1,0:T(8,128)(2,1)S(1)}, u32[]{:S(2)}, u32[]{:S(2)}) %collective-permute-start.50) | collective-permute-done | bytes 368672 | tf_op jit(solution)/shard_map/ppermute | solution.py:338
  222.7 6.8 %collective-permute-done.53 = bf16[1,24,3840]{2,1,0:T(8,128)(2,1)S(1)} collective-permute-done((bf16[1,24,3840]{2,1,0:T(8,128)(2,1)S(1)}, bf16[1,24,3840]{2,1,0:T(8,128)(2,1)S(1)}, u32[]{:S(2)}, u32[]{:S(2)}) %collective-permute-start.53) | collective-permute-done | bytes 184352 | tf_op jit(solution)/shard_map/ppermute | solution.py:338
  234.0 3.3 %collective-permute-start.57 = (bf16[1,24,2432]{2,1,0:T(8,128)(2,1)S(1)}, bf16[1,24,2432]{2,1,0:T(8,128)(2,1)S(1)}, u32[]{:S(2)}, u32[]{:S(2)}) collective-permute-start(bf16[1,24,2432]{2,1,0:T(8,128)(2,1)S(1)} %get-tuple-element.401), channel_id=1, source_target_pairs={{0,24},{1,25},{2,26},{3,27},{4,28},{5,29},{6,30},{7,31},{8,16},{9,... | collective-permute-start | bytes 350216 | tf_op jit(solution)/shard_map/ppermute | solution.py:338
  (237 shorter events, 117.9 us)
Async XLA Ops:
  19.5 14.6 %collective-permute-start.6 = (bf16[4,24,2432]{2,1,0:T(8,128)(2,1)S(1)}, bf16[4,24,2432]{2,1,0:T(8,128)(2,1)S(1)}, u32[]{:S(2)}, u32[]{:S(2)}) collective-permute-start(bf16[4,24,2432]{2,1,0:T(8,128)(2,1)S(1)} %pad_maximum_fusion.15.refs_0_), channel_id=1, source_target_pairs={{0,6},{1,7},{2,4},{3,5},{4,2},{5,3},{6,0},{7,1},{8,14},{9,15},{10,... | collective-permute-start | bytes 1400840 | tf_op jit(solution)/shard_map/ppermute | solution.py:338
  22.0 19.4 %collective-permute-start.5 = (bf16[4,24,2432]{2,1,0:T(8,128)(2,1)S(1)}, bf16[4,24,2432]{2,1,0:T(8,128)(2,1)S(1)}, u32[]{:S(2)}, u32[]{:S(2)}) collective-permute-start(bf16[4,24,2432]{2,1,0:T(8,128)(2,1)S(1)} %pad_maximum_fusion.15.refs_0_), channel_id=1, source_target_pairs={{0,4},{1,5},{2,6},{3,7},{4,0},{5,1},{6,2},{7,3},{8,12},{9,13},{10,... | collective-permute-start | bytes 1400840 | tf_op jit(solution)/shard_map/ppermute | solution.py:338
  22.5 18.9 %collective-permute-start.4 = (bf16[4,24,2432]{2,1,0:T(8,128)(2,1)S(1)}, bf16[4,24,2432]{2,1,0:T(8,128)(2,1)S(1)}, u32[]{:S(2)}, u32[]{:S(2)}) collective-permute-start(bf16[4,24,2432]{2,1,0:T(8,128)(2,1)S(1)} %pad_maximum_fusion.15.refs_0_), channel_id=1, source_target_pairs={{0,2},{1,3},{2,0},{3,1},{4,6},{5,7},{6,4},{7,5},{8,10},{9,11},{10,... | collective-permute-start | bytes 1400840 | tf_op jit(solution)/shard_map/ppermute | solution.py:338
  41.5 14.6 %collective-permute-start.12 = (bf16[1,96,768]{2,1,0:T(8,128)(2,1)}, bf16[1,96,768]{2,1,0:T(8,128)(2,1)}, u32[]{:S(2)}, u32[]{:S(2)}) collective-permute-start(bf16[1,96,768]{2,1,0:T(8,128)(2,1)} %bitcast.4), channel_id=1, source_target_pairs={{0,16},{1,17},{2,18},{3,19},{4,20},{5,21},{6,22},{7,23},{8,24},{9,... | collective-permute-start | bytes 442376 | tf_op jit(solution)/shard_map/ppermute | solution.py:338
  61.9 18.1 %collective-permute-start.18 = (bf16[8,24,1920]{2,1,0:T(8,128)(2,1)}, bf16[8,24,1920]{2,1,0:T(8,128)(2,1)}, u32[]{:S(2)}, u32[]{:S(2)}) collective-permute-start(bf16[8,24,1920]{2,1,0:T(8,128)(2,1)} %pad_maximum_fusion.4.refs_2_), channel_id=1, source_target_pairs={{0,2},{1,3},{2,0},{3,1},{4,6},{5,7},{6,4},{7,5},{8,10},{9,11},{10,... | collective-permute-start | bytes 2211848 | tf_op jit(solution)/shard_map/ppermute | solution.py:338
  62.9 17.7 %collective-permute-start.17 = (bf16[8,24,1920]{2,1,0:T(8,128)(2,1)}, bf16[8,24,1920]{2,1,0:T(8,128)(2,1)}, u32[]{:S(2)}, u32[]{:S(2)}) collective-permute-start(bf16[8,24,1920]{2,1,0:T(8,128)(2,1)} %pad_maximum_fusion.3.refs_0_), channel_id=1, source_target_pairs={{0,4},{1,5},{2,6},{3,7},{4,0},{5,1},{6,2},{7,3},{8,12},{9,13},{10,... | collective-permute-start | bytes 2211848 | tf_op jit(solution)/shard_map/ppermute | solution.py:338
  65.7 14.3 %collective-permute-start.19 = (bf16[2,96,768]{2,1,0:T(8,128)(2,1)}, bf16[2,96,768]{2,1,0:T(8,128)(2,1)}, u32[]{:S(2)}, u32[]{:S(2)}) collective-permute-start(bf16[2,96,768]{2,1,0:T(8,128)(2,1)} %pad_maximum_fusion.19), channel_id=1, source_target_pairs={{0,8},{1,9},{2,10},{3,11},{4,12},{5,13},{6,14},{7,15},{8,0},{9,1},... | collective-permute-start | bytes 884744 | tf_op jit(solution)/shard_map/ppermute | solution.py:338
  80.5 13.1 %collective-permute-start.20 = (bf16[8,24,1920]{2,1,0:T(8,128)(2,1)}, bf16[8,24,1920]{2,1,0:T(8,128)(2,1)}, u32[]{:S(2)}, u32[]{:S(2)}) collective-permute-start(bf16[8,24,1920]{2,1,0:T(8,128)(2,1)} %pad_maximum_fusion.3.refs_0_), channel_id=1, source_target_pairs={{0,1},{1,0},{2,3},{3,2},{4,5},{5,4},{6,7},{7,6},{8,9},{9,8},{10,11... | collective-permute-start | bytes 2211848 | tf_op jit(solution)/shard_map/ppermute | solution.py:338
  80.6 13.1 %collective-permute-start.21 = (bf16[8,24,1920]{2,1,0:T(8,128)(2,1)}, bf16[8,24,1920]{2,1,0:T(8,128)(2,1)}, u32[]{:S(2)}, u32[]{:S(2)}) collective-permute-start(bf16[8,24,1920]{2,1,0:T(8,128)(2,1)} %collective-permute-done.17.refs_1_), channel_id=1, source_target_pairs={{0,1},{1,0},{2,3},{3,2},{4,5},{5,4},{6,7},{7,6},{8,9},{9,8},{10,11... | collective-permute-start | bytes 2211848 | tf_op jit(solution)/shard_map/ppermute | solution.py:338
  81.1 12.6 %collective-permute-start.23 = (bf16[8,24,1920]{2,1,0:T(8,128)(2,1)}, bf16[8,24,1920]{2,1,0:T(8,128)(2,1)}, u32[]{:S(2)}, u32[]{:S(2)}) collective-permute-start(bf16[8,24,1920]{2,1,0:T(8,128)(2,1)} %collective-permute-done.18.refs_3_), channel_id=1, source_target_pairs={{0,1},{1,0},{2,3},{3,2},{4,5},{5,4},{6,7},{7,6},{8,9},{9,8},{10,11... | collective-permute-start | bytes 2211848 | tf_op jit(solution)/shard_map/ppermute | solution.py:338
  94.8 24.1 %collective-permute-start.27 = (bf16[4,96,768]{2,1,0:T(8,128)(2,1)S(1)}, bf16[4,96,768]{2,1,0:T(8,128)(2,1)S(1)}, u32[]{:S(2)}, u32[]{:S(2)}) collective-permute-start(bf16[4,96,768]{2,1,0:T(8,128)(2,1)S(1)} %pad_maximum_fusion.9.refs_0_), channel_id=1, source_target_pairs={{0,6},{1,7},{2,4},{3,5},{4,2},{5,3},{6,0},{7,1},{8,14},{9,15},{10,... | collective-permute-start | bytes 1769480 | tf_op jit(solution)/shard_map/ppermute | solution.py:338
  96.4 26.4 %collective-permute-start.26 = (bf16[4,96,768]{2,1,0:T(8,128)(2,1)S(1)}, bf16[4,96,768]{2,1,0:T(8,128)(2,1)S(1)}, u32[]{:S(2)}, u32[]{:S(2)}) collective-permute-start(bf16[4,96,768]{2,1,0:T(8,128)(2,1)S(1)} %pad_maximum_fusion.9.refs_0_), channel_id=1, source_target_pairs={{0,4},{1,5},{2,6},{3,7},{4,0},{5,1},{6,2},{7,3},{8,12},{9,13},{10,... | collective-permute-start | bytes 1769480 | tf_op jit(solution)/shard_map/ppermute | solution.py:338
  97.1 25.7 %collective-permute-start.25 = (bf16[4,96,768]{2,1,0:T(8,128)(2,1)S(1)}, bf16[4,96,768]{2,1,0:T(8,128)(2,1)S(1)}, u32[]{:S(2)}, u32[]{:S(2)}) collective-permute-start(bf16[4,96,768]{2,1,0:T(8,128)(2,1)S(1)} %pad_maximum_fusion.9.refs_0_), channel_id=1, source_target_pairs={{0,2},{1,3},{2,0},{3,1},{4,6},{5,7},{6,4},{7,5},{8,10},{9,11},{10,... | collective-permute-start | bytes 1769480 | tf_op jit(solution)/shard_map/ppermute | solution.py:338
  100.5 15.2 %collective-permute-start.28 = (bf16[2,128,768]{2,1,0:T(8,128)(2,1)S(1)}, bf16[2,128,768]{2,1,0:T(8,128)(2,1)S(1)}, u32[]{:S(2)}, u32[]{:S(2)}) collective-permute-start(bf16[2,128,768]{2,1,0:T(8,128)(2,1)S(1)} %get-tuple-element.414), channel_id=1, source_target_pairs={{0,1},{1,0},{2,3},{3,2},{4,5},{5,4},{6,7},{7,6},{8,9},{9,8},{10,11... | collective-permute-start | bytes 1179656 | tf_op jit(solution)/shard_map/ppermute | solution.py:338
  131.5 15.4 %collective-permute-start.34 = (bf16[8,96,384]{2,1,0:T(8,128)(2,1)S(1)}, bf16[8,96,384]{2,1,0:T(8,128)(2,1)S(1)}, u32[]{:S(2)}, u32[]{:S(2)}) collective-permute-start(bf16[8,96,384]{2,1,0:T(8,128)(2,1)S(1)} %pad_maximum_fusion.10), channel_id=1, source_target_pairs={{0,4},{1,5},{2,6},{3,7},{4,0},{5,1},{6,2},{7,3},{8,12},{9,13},{10,... | collective-permute-start | bytes 1769480 | tf_op jit(solution)/shard_map/ppermute | solution.py:338
  132.5 15.2 %collective-permute-start.35 = (bf16[8,96,384]{2,1,0:T(8,128)(2,1)S(1)}, bf16[8,96,384]{2,1,0:T(8,128)(2,1)S(1)}, u32[]{:S(2)}, u32[]{:S(2)}) collective-permute-start(bf16[8,96,384]{2,1,0:T(8,128)(2,1)S(1)} %pad_maximum_fusion.11), channel_id=1, source_target_pairs={{0,2},{1,3},{2,0},{3,1},{4,6},{5,7},{6,4},{7,5},{8,10},{9,11},{10,... | collective-permute-start | bytes 1769480 | tf_op jit(solution)/shard_map/ppermute | solution.py:338
  163.1 18.6 %collective-permute-start.40 = (bf16[8,24,1920]{2,1,0:T(8,128)(2,1)S(1)}, bf16[8,24,1920]{2,1,0:T(8,128)(2,1)S(1)}, u32[]{:S(2)}, u32[]{:S(2)}) collective-permute-start(bf16[8,24,1920]{2,1,0:T(8,128)(2,1)S(1)} %pad_maximum_fusion.5), channel_id=1, source_target_pairs={{0,4},{1,5},{2,6},{3,7},{4,0},{5,1},{6,2},{7,3},{8,12},{9,13},{10,... | collective-permute-start | bytes 2211848 | tf_op jit(solution)/shard_map/ppermute | solution.py:338
  164.0 18.3 %collective-permute-start.41 = (bf16[8,24,1920]{2,1,0:T(8,128)(2,1)S(1)}, bf16[8,24,1920]{2,1,0:T(8,128)(2,1)S(1)}, u32[]{:S(2)}, u32[]{:S(2)}) collective-permute-start(bf16[8,24,1920]{2,1,0:T(8,128)(2,1)S(1)} %pad_maximum_fusion.6), channel_id=1, source_target_pairs={{0,2},{1,3},{2,0},{3,1},{4,6},{5,7},{6,4},{7,5},{8,10},{9,11},{10,... | collective-permute-start | bytes 2211848 | tf_op jit(solution)/shard_map/ppermute | solution.py:338
  166.1 13.1 %collective-permute-start.42 = (bf16[2,128,768]{2,1,0:T(8,128)(2,1)S(1)}, bf16[2,128,768]{2,1,0:T(8,128)(2,1)S(1)}, u32[]{:S(2)}, u32[]{:S(2)}) collective-permute-start(bf16[2,128,768]{2,1,0:T(8,128)(2,1)S(1)} %bitcast.145), channel_id=1, source_target_pairs={{0,1},{1,0},{2,3},{3,2},{4,5},{5,4},{6,7},{7,6},{8,9},{9,8},{10,11... | collective-permute-start | bytes 1179656 | tf_op jit(solution)/shard_map/ppermute | solution.py:338
  166.2 13.0 %collective-permute-start.39 = (bf16[2,96,768]{2,1,0:T(8,128)(2,1)S(1)}, bf16[2,96,768]{2,1,0:T(8,128)(2,1)S(1)}, u32[]{:S(2)}, u32[]{:S(2)}) collective-permute-start(bf16[2,96,768]{2,1,0:T(8,128)(2,1)S(1)} %get-tuple-element.399), channel_id=1, source_target_pairs={{0,8},{1,9},{2,10},{3,11},{4,12},{5,13},{6,14},{7,15},{8,0},{9,1},... | collective-permute-start | bytes 884744 | tf_op jit(solution)/shard_map/ppermute | solution.py:338
  203.5 12.9 %collective-permute-start.49 = (bf16[8,24,1280]{2,1,0:T(8,128)(2,1)S(1)}, bf16[8,24,1280]{2,1,0:T(8,128)(2,1)S(1)}, u32[]{:S(2)}, u32[]{:S(2)}) collective-permute-start(bf16[8,24,1280]{2,1,0:T(8,128)(2,1)S(1)} %pad_maximum_fusion.14), channel_id=1, source_target_pairs={{0,2},{1,3},{2,0},{3,1},{4,6},{5,7},{6,4},{7,5},{8,10},{9,11},{10,... | collective-permute-start | bytes 1474568 | tf_op jit(solution)/shard_map/ppermute | solution.py:338
  216.6 12.9 %collective-permute-start.51 = (bf16[4,24,1152]{2,1,0:T(8,128)(2,1)S(1)}, bf16[4,24,1152]{2,1,0:T(8,128)(2,1)S(1)}, u32[]{:S(2)}, u32[]{:S(2)}) collective-permute-start(bf16[4,24,1152]{2,1,0:T(8,128)(2,1)S(1)} %get-tuple-element.433), channel_id=1, source_target_pairs={{0,2},{1,3},{2,0},{3,1},{4,6},{5,7},{6,4},{7,5},{8,10},{9,11},{10,... | collective-permute-start | bytes 663560 | tf_op jit(solution)/shard_map/ppermute | solution.py:338
  217.8 13.4 %collective-permute-start.54 = (bf16[2,128,768]{2,1,0:T(8,128)(2,1)S(1)}, bf16[2,128,768]{2,1,0:T(8,128)(2,1)S(1)}, u32[]{:S(2)}, u32[]{:S(2)}) collective-permute-start(bf16[2,128,768]{2,1,0:T(8,128)(2,1)S(1)} %get-tuple-element.347), channel_id=1, source_target_pairs={{0,2},{1,3},{2,0},{3,1},{4,6},{5,7},{6,4},{7,5},{8,10},{9,11},{10,... | collective-permute-start | bytes 1179656 | tf_op jit(solution)/shard_map/ppermute | solution.py:338
  231.3 14.5 %collective-permute-start.58 = (bf16[2,128,768]{2,1,0:T(8,128)(2,1)S(1)}, bf16[2,128,768]{2,1,0:T(8,128)(2,1)S(1)}, u32[]{:S(2)}, u32[]{:S(2)}) collective-permute-start(bf16[2,128,768]{2,1,0:T(8,128)(2,1)S(1)} %get-tuple-element.352), channel_id=1, source_target_pairs={{0,2},{1,3},{2,0},{3,1},{4,6},{5,7},{6,4},{7,5},{8,10},{9,11},{10,... | collective-permute-start | bytes 1179656 | tf_op jit(solution)/shard_map/ppermute | solution.py:338
  (51 other events, 342.9 us)

commit v3 on v2

--- a/solution.py
+++ b/solution.py
@@ -369,8 +369,11 @@
         self.held = join(self.held, *self.got)
         self.got = [swap(self.held, Z0)]
 
+    def line_end(self):
+        self.held, self.got = join(self.held, *self.got), []
+
     def plane(self):
-        self.held = join(self.held, *self.got)
+        self.held = join(self.held, *self.got) if self.got else self.held
         self.got = [swap(self.held, mask) for mask in PLANE[1:]]
 
     def plane_one(self):
@@ -379,11 +382,9 @@
         self.got = [swap(quad, bit) for quad, bit in zip(self.quads, (X, Y))]
 
     def plane_two(self):
-        own = []
-        for quad, got, bit in zip(self.quads, self.got, (Y, X)):
-            eight = join(quad, got)
-            own += [eight, swap(eight, bit)]
-        self.held, self.got = own[0], own[1:]
+        own = [one for pair in zip(self.quads, self.got) for one in pair]
+        bits = (Y, Y, X, X)
+        self.held, self.got = own[0], own[1:] + [swap(one, bit) for one, bit in zip(own, bits)]
 
     def cores(self):
         own = [self.held, *self.got]
@@ -391,12 +392,12 @@
 
     def places(self):
         width = self.held.shape[2]
-        if self.held.shape[0] == 4:
+        if len(self.got) == 3:
             masks = [core ^ plane ^ line for core in (0, CORE) for plane in PLANE for line in LINE]
             return [(i // 4, i % 4, mask, 0, width) for i, mask in enumerate(masks)]
-        spans = ((0, width), (width, width + self.got[1].shape[2]))
+        spans = ((0, width), (width, width + self.got[2].shape[2]))
         return [
-            (4 * core + 2 * half + second, 4 * first + i, mask, low, high)
+            (8 * core + 4 * second + 2 * half + first, i, mask, low, high)
             for core in (0, CORE)
             for half, ((low, high), bits) in enumerate(zip(spans, ((X, Y), (Y, X))))
             for second in (0, 1)
@@ -413,10 +414,13 @@
 
 class Scatter:
     places = [
-        (slot // 16, slot % 16, core ^ plane ^ line)
-        for slot, (core, plane, line) in enumerate(
-            (core, plane, line) for core in (0, CORE) for plane in PLANE for line in LINE
-        )
+        [
+            (slot // 16, slot % 16, core ^ plane ^ line)
+            for slot, (core, plane, line) in enumerate(
+                (core, plane, line) for core in (0, CORE) for plane in planes for line in LINE
+            )
+        ]
+        for planes in ((0, X, Y, X ^ Y), (0, Y, X, X ^ Y))
     ]
 
     def __init__(self, halves):
@@ -424,12 +428,6 @@
 
     def cores(self):
         self.got = swap(self.sent, CORE)
-
-    def plane(self):
-        self.kept, *quads = [
-            sum_low(self.kept[4 * i : 4 * i + 4], self.got[4 * i : 4 * i + 4]) for i in range(4)
-        ]
-        self.got = [swap(quad, mask) for quad, mask in zip(quads, PLANE[1:])]
 
     def line(self):
         terms = [self.kept, *self.got]
@@ -438,26 +436,19 @@
         self.got = [swap(one, mask) for one, mask in zip(ones, LINE[1:])]
 
     def plane_one(self):
-        kept, got = [], []
-        spans = halves_of(self.kept.shape[2])
-        for (low, high), bit, order in zip(spans, (Y, X), ((0, 1, 2, 3), (0, 2, 1, 3))):
-            quads = [
-                sum_low(
-                    self.kept[4 * i : 4 * i + 4, :, low:high],
-                    self.got[4 * i : 4 * i + 4, :, low:high],
-                )
-                for i in order
-            ]
-            kept.append(quads[:2])
-            got.append(swap(jnp.concatenate(quads[2:], 0), bit))
-        self.kept, self.got = kept, got
+        kept, sent = [], []
+        for low, high in halves_of(self.kept.shape[2]):
+            pairs = [(one[..., low:high]) for one in (self.kept, self.got)]
+            kept.append(sum_low(*(one[:8] for one in pairs)))
+            sent.append(sum_low(*(one[8:] for one in pairs)))
+        self.kept, self.got = kept, [swap(one, bit) for one, bit in zip(sent, (Y, X))]
 
     def plane_two(self):
         sent = [
-            swap(sum_low(kept[1], got[4:]), bit)
+            swap(sum_low(kept[4:], got[4:]), bit)
             for kept, got, bit in zip(self.kept, self.got, (X, Y))
         ]
-        kept = [sum_low(kept[0], got[:4]) for kept, got in zip(self.kept, self.got)]
+        kept = [sum_low(kept[:4], got[:4]) for kept, got in zip(self.kept, self.got)]
         self.kept, self.got = jnp.concatenate(kept, -1), sent
 
     def plane_end(self):
@@ -531,6 +522,29 @@
 TN = (((0,), (0,)), ((), ()))
 
 
+def finish_kernel(cuts, *refs):
+    kept_ref, got_refs, outs = refs[0], refs[1 : -len(cuts)], refs[-len(cuts) :]
+    for out_ref, (begin, end) in zip(outs, cuts):
+        total = kept_ref[:, begin:end]
+        for ref in got_refs:
+            total = total + ref[0, :, begin:end].astype(jnp.float32)
+        out_ref[...] = total
+
+
+def finish(scatter, parts):
+    inputs = [scatter.kept, *scatter.got]
+    shapes = [(scatter.kept.shape[0], part) for part in parts]
+    return pl.pallas_call(
+        functools.partial(finish_kernel, cuts_of(parts)),
+        grid=(1,),
+        out_shape=[jax.ShapeDtypeStruct(shape, jnp.float32) for shape in shapes],
+        in_specs=[whole_block(value.shape) for value in inputs],
+        out_specs=[whole_block(shape) for shape in shapes],
+        compiler_params=pltpu.CompilerParams(vmem_limit_bytes=8 * MIB),
+        cost_estimate=SMALL,
+    )(*inputs)
+
+
 def parts_call(kernel, inputs, rows, width, scratch, limit, me):
     half = (DEVICES // 2, rows, width)
     return pl.pallas_call(
@@ -548,11 +562,14 @@
 
 def store_rows(me, sum_ref, outs, low, high):
     rows = sum_ref.shape[0] // DEVICES
-    for half, slot, mask in Scatter.places:
-        first = pl.multiple_of(lax.bitwise_xor(me, mask) * rows, rows)
-        outs[half][slot, :, low:high] = sum_ref[pl.ds(first, rows), : high - low].astype(
-            jnp.bfloat16
-        )
+    for places, (begin, end) in zip(Scatter.places, halves_of(outs[0].shape[2])):
+        left, right = max(low, begin), min(high, end)
+        if left < right:
+            for half, slot, mask in places:
+                first = pl.multiple_of(lax.bitwise_xor(me, mask) * rows, rows)
+                outs[half][slot, :, left:right] = sum_ref[
+                    pl.ds(first, rows), left - low : right - low
+                ].astype(jnp.bfloat16)
 
 
 def multiply_rows(me, left_ref, right_refs, sum_ref, outs, low):
@@ -598,7 +615,7 @@
     width, bias = vectors.shape[1], jnp.broadcast_to(bias_ref[...], (8, bias_ref.shape[1]))
     deep = bias.shape[1] // DEVICES
     spare = jnp.zeros((rows - 16, 128), jnp.float32)
-    for half, slot, mask in Scatter.places:
+    for half, slot, mask in Scatter.places[1]:
         owner = lax.bitwise_xor(me, mask)
         here = pltpu.roll(vectors, lax.rem(width - rows * owner, width), 1)[:, :128]
         bias_here = pltpu.roll(bias, lax.rem(DEVICES * deep - deep * owner, DEVICES * deep), 1)
@@ -618,19 +635,24 @@
             TN,
             preferred_element_type=jnp.float32,
         )
-        for half, slot, mask in Scatter.places:
-            if mask // 4 == block:
-                first = pl.multiple_of(lax.bitwise_xor(me % 4, mask % 4) * rows, rows)
-                outs[half][slot] = sum_ref[pl.ds(first, rows)].astype(jnp.bfloat16)
+        for places, (low, high) in zip(Scatter.places, halves_of(cot_ref.shape[1])):
+            for half, slot, mask in places:
+                if mask // 4 == block:
+                    first = pl.multiple_of(lax.bitwise_xor(me % 4, mask % 4) * rows, rows)
+                    outs[half][slot, :, low:high] = sum_ref[pl.ds(first, rows), low:high].astype(
+                        jnp.bfloat16
+                    )
 
 
 NT = (((1,), (1,)), ((), ()))
 
 
-def make_mask(labels_row_ref, labels_col_ref, mask_ref):
+def make_mask(labels_ref, mask_ref):
     @pl.when(pl.program_id(0) == 0)
     def _():
-        allowed = labels_col_ref[...] == labels_row_ref[...]
+        across = labels_ref[...].astype(jnp.float32)
+        down = jnp.broadcast_to(across, (8, across.shape[1])).T[:, :1]
+        allowed = down == across
         mask_ref[...] = jnp.where(allowed, 0.0, NEG_LARGE)
 
 
@@ -644,8 +666,8 @@
     return exponent * (1.0 / jnp.sum(exponent, 0, keepdims=True))
 
 
-def attend_kernel(row_ref, col_ref, query_ref, key_ref, value_ref, out_ref, prob_ref, mask_ref):
-    make_mask(row_ref, col_ref, mask_ref)
+def attend_kernel(row_ref, query_ref, key_ref, value_ref, out_ref, prob_ref, mask_ref):
+    make_mask(row_ref, mask_ref)
     keys, queries = key_ref[...], query_ref[...]
     values_across = value_ref[...].astype(jnp.float32).T.astype(jnp.bfloat16)
     mixed = []
@@ -712,14 +734,13 @@
         ],
         in_specs=[
             pl.BlockSpec((1, tokens), lambda i: (0, 0)),
-            pl.BlockSpec((tokens, 1), lambda i: (0, 0)),
             *parts,
         ],
         out_specs=[pl.BlockSpec((tokens, 128), lambda i: (0, i)), probs],
         scratch_shapes=[pltpu.VMEM((tokens, tokens), jnp.float32)],
         compiler_params=pltpu.CompilerParams(vmem_limit_bytes=12 * MIB),
         cost_estimate=SMALL,
-    )(labels.reshape(1, tokens), labels.reshape(tokens, 1), project, project, project)
+    )(labels.reshape(1, tokens), project, project, project)
 
 
 def attend_back(project, probs, grads):
@@ -755,6 +776,31 @@
 
 def column_sum(values):
     return jnp.sum(values.astype(jnp.float32), 0, keepdims=True)
+
+
+def project_kernel(normed_ref, weight_ref, bias_ref, out_ref):
+    for row in range(0, normed_ref.shape[0], 128):
+        rows = slice(row, row + 128)
+        out = jnp.dot(normed_ref[rows], weight_ref[...], preferred_element_type=jnp.float32)
+        out_ref[rows] = (out + bias_ref[...]).astype(jnp.bfloat16)
+
+
+def project_forward(normed, qkv_full, bias_row):
+    tokens, width = normed.shape
+    wide, tile = qkv_full.shape[1], 768
+    return pl.pallas_call(
+        project_kernel,
+        grid=(wide // tile,),
+        out_shape=jax.ShapeDtypeStruct((tokens, wide), jnp.bfloat16),
+        in_specs=[
+            pl.BlockSpec((tokens, width), lambda i: (0, 0)),
+            pl.BlockSpec((width, tile), lambda i: (0, i)),
+            pl.BlockSpec((1, tile), lambda i: (0, i)),
+        ],
+        out_specs=pl.BlockSpec((tokens, tile), lambda i: (0, i)),
+        compiler_params=pltpu.CompilerParams(vmem_limit_bytes=12 * MIB),
+        cost_estimate=SMALL,
+    )(normed, in_hbm(qkv_full), bias_row)
 
 
 def up_kernel(normed_ref, weight_ref, bias_ref, hidden_ref, slope_ref):
@@ -1046,29 +1092,32 @@
     ) = (vectors[i : i + 1] for i in range(8))
     normed_one = (unit_one * gain_one + shift_one).astype(bf16)
     bias_project = jnp.concatenate([bias_query, jnp.zeros_like(bias_query), bias_value], 1)
-    project = (
-        jnp.dot(normed_one, qkv_full, preferred_element_type=f32) + bias_project
-    ).astype(bf16)
+    project = project_forward(normed_one, qkv_full, bias_project)
     second.quads, second.got, third.held, third.got, project = fence(
         second.quads, second.got, third.held, third.got, project
     )
 
     second.plane_two()
     third.near()
+    cot_parts = cotangent.reshape(2, 2, local_rows, width)
+    cot_sent, cot_own = pick(cot_parts, 1 - side), pick(cot_parts, side)
     mixed, probs = attend(labels, project)
-    second.held, second.got, third.held, third.got, mixed, cotangent = fence(
-        second.held, second.got, third.held, third.got, mixed, cotangent
+    second.held, second.got, third.held, third.got, mixed, cot_sent, cot_own = fence(
+        second.held, second.got, third.held, third.got, mixed, cot_sent, cot_own
     )
 
     second.cores()
-    cot_got, cot_halves = to_micro_x(cotangent, side)
-    second.parts, third.held, third.got, mixed, cot_got, cot_halves = fence(
-        second.parts, third.held, third.got, mixed, cot_got, cot_halves
+    cot_got = swap(cot_sent, X)
+    third.line_end()
+    second.parts, third.held, third.got, mixed, cot_got, cot_own = fence(
+        second.parts, third.held, third.got, mixed, cot_got, cot_own
     )
 
     third.plane()
-    cot_kept, cot_got = to_micro_c(cot_got, cot_halves, side, core)
+    cot_parts = jnp.stack([cot_own, cot_got], 1)
+    cot_kept, cot_got = pick(cot_parts, core), swap(pick(cot_parts, 1 - core), CORE)
     cot_low = to_micro_end(cot_kept, cot_got)
+    second.parts = [in_hbm(part) for part in second.parts]
     out_full, up_full = restore(second, cuts_of((width, inner)), me)
     out_full, up_full = out_full.reshape(width, width), up_full.reshape(width, inner)
     resid_mid = resid_in + jnp.dot(mixed, out_full, preferred_element_type=f32) + bias_out
@@ -1239,7 +1288,6 @@
     qkv_sum.plane_one()
     up_sum.near()
     in_kept, in_sent = from_micro_pick(in_kept, in_got, core)
-    grad_down = down_sum.total()
     (
         qkv_sum.kept,
         qkv_sum.got,
@@ -1249,7 +1297,8 @@
         in_sent,
         out_kept,
         out_sent,
-        grad_down,
+        down_sum.kept,
+        down_sum.got,
     ) = fence(
         qkv_sum.kept,
         qkv_sum.got,
@@ -1259,7 +1308,8 @@
         in_sent,
         out_kept,
         out_sent,
-        grad_down,
+        down_sum.kept,
+        down_sum.got,
     )
     qkv_sum.plane_two()
     up_sum.far()
@@ -1287,17 +1337,16 @@
     in_got = swap(in_sent, X)
     qkv_sum.plane_end()
     qkv_sum.line()
-    last = up_sum.total()
-    grad_out, grad_up = last[:, :width], last[:, width:]
+    grad_out, grad_up = finish(up_sum, (width, inner))
+    (grad_down,) = finish(down_sum, (width,))
     output = from_micro_end(out_kept, out_got, side)
-    qkv_sum.kept, qkv_sum.got, in_kept, in_got, output, grad_out, grad_up = fence(
-        qkv_sum.kept, qkv_sum.got, in_kept, in_got, output, grad_out, grad_up
-    )
-
     in_grad = from_micro_end(in_kept, in_got, side).astype(f32)
-    last = qkv_sum.total()
-    grad_qkv = last[:, :wide]
-    deep, sums = last[8, wide : wide + deep], last[:8, wide : wide + rows]
+    qkv_sum.kept, qkv_sum.got, output, grad_out, grad_up, grad_down = fence(
+        qkv_sum.kept, qkv_sum.got, output, grad_out, grad_up, grad_down
+    )
+
+    grad_qkv, sums = finish(qkv_sum, (wide, 128))
+    deep, sums = sums[8, :deep], sums[:8, :rows]
     return (
         output,
         in_grad,

time: 250 us -> 241 us (0.964)
  other arithmetic: 26.8 us -> 19.6 us
  Pallas kernels: 61.7 us -> 68.2 us
  matrix products: 9.07 us -> 4.75 us
  waiting for transfers between devices: 82.2 us -> 78.6 us
    pallas_call x0 -> x4, Pallas kernels: none -> 7.05 us  [the longest x1 4.8 us: project_forward(): pl.pallas_call(project_kernel, grid=(wide // tile,), out_shape=jax.ShapeD...]
    concatenate x7 -> x5, other arithmetic: 6.99 us -> 2.29 us  [join(): return lax.optimization_barrier(jnp.concatenate(parts, 0))]
    dot_general x1 -> x0, matrix products: 4.3 us -> none  [on_device_fast(): jnp.dot(normed_one, qkv_full, preferred_element_type=f32) + bias_project]
    ppermute x59 -> x65, waiting for transfers between devices: 82.2 us -> 78.6 us  [swap(): return lax.ppermute(values, AXES, pairs)]
    ppermute x59 -> x65, starting transfers between devices: 55.9 us -> 57.9 us  [swap(): return lax.ppermute(values, AXES, pairs)]
  transfers between devices with their start and end apart: 59 -> 65, of which waited for: 31 -> 30; matrix products, arithmetic and copies ran while one was open for 12% -> 10% of each run, Pallas kernels for 25% -> 28%
where the time goes in v3:
time: 241 us; the launch traced here: 240 us
  waiting for transfers between devices  78.6 us (33%)
  Pallas kernels  68.2 us (28%)
  starting transfers between devices  57.9 us (24%)
  other arithmetic  19.6 us (8%)
  local copies, waits for them, and re-layouts  9.91 us (4%)
  matrix products  4.75 us (2%)
    ppermute x65, waiting for transfers between devices, swap(): return lax.ppermute(values, AXES, pairs)  78.6 us
    ppermute x65, starting transfers between devices, swap(): return lax.ppermute(values, AXES, pairs)  57.9 us
    pallas_call x1, Pallas kernels, attend_back(): pl.pallas_call(attend_back_kernel, grid=(pairs,), out_shape=[shape] * 3,...  11.6 us
    pallas_call x1, Pallas kernels, attend(): pl.pallas_call(attend_kernel, grid=(pairs,), out_shape=[jax.ShapeDtypeStr...  11 us
    pallas_call x3, Pallas kernels, parts_call(): pl.pallas_call(kernel, grid=(1,), out_shape=[jax.ShapeDtypeStruct(half, j...  10.9 us
    pallas_call x3, Pallas kernels, shuffle(): pl.pallas_call(functools.partial(shuffle_kernel, moves, len(arrays)), gri...  8.05 us
    pallas_call x1, Pallas kernels, up_forward(): pl.pallas_call(up_kernel, grid=(inner // tile,), out_shape=[shape, shape]...  6.67 us
    convert_element_type x15, other arithmetic, sum_low(): return total.astype(jnp.bfloat16)  5.59 us
  transfers between devices with their start and end apart: 65, of which 30 were waited for; matrix products, arithmetic and copies ran while one was open for 10% of the time, Pallas kernels for 28%

profile of v3, /device:TPU:0, one launch (start us, length us, event | category | flops | bytes accessed | tf_op | source)
XLA Modules:
  0.0 240.5 jit_solution(17551616483072501159)
XLA Ops:
  3.3 5.1 %collective-permute-start.2 = (bf16[1,24,2432]{2,1,0:T(8,128)(2,1)S(1)}, bf16[1,24,2432]{2,1,0:T(8,128)(2,1)S(1)}, u32[]{:S(2)}, u32[]{:S(2)}) collective-permute-start(bf16[1,24,2432]{2,1,0:T(8,128)(2,1)S(1)} %maximum_bitcast_fusion.1), channel_id=1, source_target_pairs={{0,24},{1,25},{2,26},{3,27},{4,28},{5,29},{6,30},{7,31},{8,16},{9,... | collective-permute-start | bytes 350216 | tf_op jit(solution)/shard_map/ppermute | solution.py:338
  15.2 3.1 %collective-permute-done = bf16[1,24,2432]{2,1,0:T(8,128)(2,1)S(1)} collective-permute-done((bf16[1,24,2432]{2,1,0:T(8,128)(2,1)S(1)}, bf16[1,24,2432]{2,1,0:T(8,128)(2,1)S(1)}, u32[]{:S(2)}, u32[]{:S(2)}) %collective-permute-start) | collective-permute-done | bytes 116768 | tf_op jit(solution)/shard_map/ppermute | solution.py:338
  25.6 6.5 %collective-permute-done.7 = bf16[1,24,3840]{2,1,0:T(8,128)(2,1)S(1)} collective-permute-done((bf16[1,24,3840]{2,1,0:T(8,128)(2,1)S(1)}, bf16[1,24,3840]{2,1,0:T(8,128)(2,1)S(1)}, u32[]{:S(2)}, u32[]{:S(2)}) %collective-permute-start.7) | collective-permute-done | bytes 184352 | tf_op jit(solution)/shard_map/ppermute | solution.py:338
  34.2 7.3 %collective-permute-done.5.refs_2_ = bf16[4,24,2432]{2,1,0:T(8,128)(2,1)S(1)} collective-permute-done((bf16[4,24,2432]{2,1,0:T(8,128)(2,1)S(1)}, bf16[4,24,2432]{2,1,0:T(8,128)(2,1)S(1)}, u32[]{:S(2)}, u32[]{:S(2)}) %collective-permute-start.5) | collective-permute-done | bytes 466976 | tf_op jit(solution)/shard_map/ppermute | solution.py:338
  52.1 4.8 %shard_map.272.query_ref.key_ref.value_ref = bf16[512,2304]{1,0:T(8,128)(2,1)S(1)} custom-call(bf16[512,768]{1,0:T(8,128)(2,1)S(1)} %add_convert_fusion.2.normed_ref, bf16[768,2304]{1,0:T(8,128)(2,1)} %bitcast.112, f32[1,2304]{1,0:T(1,128)S(1)} %fusion.12.bias_ref), custom_call_target="tpu_custom_call" | custom-call | flops 1024 | bytes 1024 | tf_op jit(solution)/shard_map/pallas_call | solution.py:791
  65.5 11.0 %shard_map.273 = (bf16[512,768]{1,0:T(8,128)(2,1)S(1)}, bf16[12,512,512]{2,1,0:T(8,128)(2,1)}) custom-call(s32[1,512]{1,0:T(1,128)S(1)} %bitcast.121, bf16[512,2304]{1,0:T(8,128)(2,1)S(1)} %shard_map.272.query_ref.key_ref.value_ref, bf16[512,2304]{1,0:T(8,128)(2,1)S(1)} %shard_map.272.query_ref.key_ref.value_ref, ...), custom_call_target="tpu_custom_call" | custom-call | flops 1024 | bytes 1024 | tf_op jit(solution)/shard_map/pallas_call | solution.py:728
  84.6 5.3 %collective-permute-done.30 = bf16[2,128,768]{2,1,0:T(8,128)(2,1)} collective-permute-done((bf16[2,128,768]{2,1,0:T(8,128)(2,1)}, bf16[2,128,768]{2,1,0:T(8,128)(2,1)}, u32[]{:S(2)}, u32[]{:S(2)}) %collective-permute-start.30) | collective-permute-done | bytes 393248 | tf_op jit(solution)/shard_map/ppermute | solution.py:338
  94.8 5.6 %shard_map.274 = (bf16[32,24,768]{2,1,0:T(8,128)(2,1)}, bf16[32,24,3072]{2,1,0:T(8,128)(2,1)}) custom-call(s32[1]{0:T(128)} %bitcast.12.me_ref, bf16[4,24,1920]{2,1,0:T(8,128)(2,1)} %get-tuple-element.241.refs_0_, bf16[4,24,1920]{2,1,0:T(8,128)(2,1)} %collective-permute-done.10.refs_1_, bf16[4,24,1920]{2,1,0:T(8,128)(2,1)} %copy-done.10, ...), custom_call_target="tpu_custom_call" | custom-call | flops 1024 | bytes 1024 | tf_op jit(solution)/shard_map/pallas_call | solution.py:496
  103.6 6.7 %shard_map.275 = (bf16[512,3072]{1,0:T(8,128)(2,1)S(1)}, bf16[512,3072]{1,0:T(8,128)(2,1)S(1)}) custom-call(bf16[512,768]{1,0:T(8,128)(2,1)S(1)} %add_convert_fusion.1.normed_ref, bf16[768,3072]{1,0:T(8,128)(2,1)} %bitcast.106, f32[1,3072]{1,0:T(1,128)S(1)} %reshape_squeeze.3.bias_ref), custom_call_target="tpu_custom_call" | custom-call | flops 1024 | bytes 1024 | tf_op jit(solution)/shard_map/pallas_call | solution.py:825
  110.4 3.1 %shard_map.276 = (bf16[16,96,768]{2,1,0:T(8,128)(2,1)S(1)}, bf16[16,96,768]{2,1,0:T(8,128)(2,1)S(1)}) custom-call(s32[1]{0:T(128)} %bitcast.12.me_ref, bf16[512,3072]{1,0:T(8,128)(2,1)S(1)} %get-tuple-element.306.hidden_ref, bf16[512,768]{1,0:T(8,128)(2,1)S(1)} %bitcast.114), custom_call_target="tpu_custom_call" | custom-call | flops 1024 | bytes 1024 | tf_op jit(solution)/shard_map/pallas_call | solution.py:550
  113.5 4.4 %collective-permute-done.32.refs_2_ = bf16[4,96,768]{2,1,0:T(8,128)(2,1)S(1)} collective-permute-done((bf16[4,96,768]{2,1,0:T(8,128)(2,1)S(1)}, bf16[4,96,768]{2,1,0:T(8,128)(2,1)S(1)}, u32[]{:S(2)}, u32[]{:S(2)}) %collective-permute-start.32) | collective-permute-done | bytes 589856 | tf_op jit(solution)/shard_map/ppermute | solution.py:338
  118.9 4.3 %collective-permute-done.35.refs_4_ = bf16[4,96,768]{2,1,0:T(8,128)(2,1)S(1)} collective-permute-done((bf16[4,96,768]{2,1,0:T(8,128)(2,1)S(1)}, bf16[4,96,768]{2,1,0:T(8,128)(2,1)S(1)}, u32[]{:S(2)}, u32[]{:S(2)}) %collective-permute-start.35) | collective-permute-done | bytes 589856 | tf_op jit(solution)/shard_map/ppermute | solution.py:338
  128.9 4.4 %shard_map.278 = (bf16[512,3072]{1,0:T(8,128)(2,1)S(1)}, f32[1,3072]{1,0:T(1,128)S(1)}) custom-call(bf16[512,768]{1,0:T(8,128)(2,1)S(1)} %bitcast.115, bf16[3072,768]{1,0:T(8,128)(2,1)S(1)} %bitcast.110, bf16[512,3072]{1,0:T(8,128)(2,1)S(1)} %get-tuple-element.283.slope_ref), custom_call_target="tpu_custom_call" | custom-call | flops 1024 | bytes 1024 | tf_op jit(solution)/shard_map/pallas_call | solution.py:852
  133.3 5.5 %shard_map.279 = (f32[512,768]{1,0:T(8,128)S(1)}, bf16[512,768]{1,0:T(8,128)(2,1)S(1)}, bf16[512,768]{1,0:T(8,128)(2,1)S(1)}, f32[8,768]{1,0:T(8,128)S(1)}) custom-call(bf16[512,3072]{1,0:T(8,128)(2,1)S(1)} %get-tuple-element.294.pre_ref, bf16[768,3072]{1,0:T(8,128)(2,1)S(1)} %bitcast.109, f32[512,768]{1,0:T(8,128)S(1)} %get-tuple-element.464.resid_ref, ...), custom_call_target="tpu_custom_call" | custom-call | flops 1024 | bytes 1024 | tf_op jit(solution)/shard_map/pallas_call | solution.py:896
  138.9 3.0 %collective-permute-done.41 = bf16[8,96,384]{2,1,0:T(8,128)(2,1)S(1)} collective-permute-done((bf16[8,96,384]{2,1,0:T(8,128)(2,1)S(1)}, bf16[8,96,384]{2,1,0:T(8,128)(2,1)S(1)}, u32[]{:S(2)}, u32[]{:S(2)}) %collective-permute-start.41) | collective-permute-done | bytes 589856 | tf_op jit(solution)/shard_map/ppermute | solution.py:338
  145.0 4.0 %shard_map.280 = (bf16[16,24,3840]{2,1,0:T(8,128)(2,1)S(1)}, bf16[16,24,3840]{2,1,0:T(8,128)(2,1)S(1)}) custom-call(s32[1]{0:T(128)} %bitcast.12.me_ref, bf16[512,768]{1,0:T(8,128)(2,1)S(1)} %copy-done.8, bf16[512,768]{1,0:T(8,128)(2,1)S(1)} %get-tuple-element.293.branch_ref, bf16[512,768]{1,0:T(8,128)(2,1)S(1)} %add_convert_fusion.1.normed_ref, ...), custom_call_target="tpu_custom_call" | custom-call | flops 1024 | bytes 1024 | tf_op jit(solution)/shard_map/pallas_call | solution.py:550
  154.3 2.7 %collective-permute-done.44 = bf16[16,24,3840]{2,1,0:T(8,128)(2,1)S(1)} collective-permute-done((bf16[16,24,3840]{2,1,0:T(8,128)(2,1)S(1)}, bf16[16,24,3840]{2,1,0:T(8,128)(2,1)S(1)}, u32[]{:S(2)}, u32[]{:S(2)}) %collective-permute-start.44) | collective-permute-done | bytes 2949152 | tf_op jit(solution)/shard_map/ppermute | solution.py:338
  161.1 11.6 %shard_map.281 = (bf16[512,768]{1,0:T(8,128)(2,1)S(1)}, bf16[512,768]{1,0:T(8,128)(2,1)S(1)}, bf16[512,768]{1,0:T(8,128)(2,1)S(1)}) custom-call(bf16[512,2304]{1,0:T(8,128)(2,1)S(1)} %shard_map.272.query_ref.key_ref.value_ref, bf16[512,2304]{1,0:T(8,128)(2,1)S(1)} %shard_map.272.query_ref.key_ref.value_ref, ...), custom_call_target="tpu_custom_call" | custom-call | flops 1024 | bytes 1024 | tf_op jit(solution)/shard_map/pallas_call | solution.py:751
  172.8 3.5 %collective-permute-done.47 = bf16[8,24,1920]{2,1,0:T(8,128)(2,1)S(1)} collective-permute-done((bf16[8,24,1920]{2,1,0:T(8,128)(2,1)S(1)}, bf16[8,24,1920]{2,1,0:T(8,128)(2,1)S(1)}, u32[]{:S(2)}, u32[]{:S(2)}) %collective-permute-start.47) | collective-permute-done | bytes 737312 | tf_op jit(solution)/shard_map/ppermute | solution.py:338
  181.1 3.1 %shard_map.282 = (bf16[512,768]{1,0:T(8,128)(2,1)S(1)}, f32[8,768]{1,0:T(8,128)S(1)}) custom-call(bf16[512,768]{1,0:T(8,128)(2,1)S(1)} %get-tuple-element.324.query_ref, bf16[512,768]{1,0:T(8,128)(2,1)S(1)} %get-tuple-element.325.key_ref, bf16[512,768]{1,0:T(8,128)(2,1)S(1)} %get-tuple-element.326.value_ref, bf16[768,2304]{1,0:T(8,128)(2,1)S(1)} %bitcast.113, ...), custom_call_target="tpu_custom_call" | custom-call | flops 1024 | bytes 1024 | tf_op jit(solution)/shard_map/pallas_call | solution.py:950
  184.2 3.8 %shard_map.283 = (bf16[16,24,2432]{2,1,0:T(8,128)(2,1)S(1)}, bf16[16,24,2432]{2,1,0:T(8,128)(2,1)}) custom-call(s32[1]{0:T(128)} %bitcast.12.me_ref, bf16[512,768]{1,0:T(8,128)(2,1)S(1)} %copy-done.4, bf16[512,768]{1,0:T(8,128)(2,1)S(1)} %get-tuple-element.324.query_ref, bf16[512,768]{1,0:T(8,128)(2,1)S(1)} %get-tuple-element.325.key_ref, ...), custom_call_target="tpu_custom_call" | custom-call | flops 1024 | bytes 1024 | tf_op jit(solution)/shard_map/pallas_call | solution.py:550
  199.1 8.9 %collective-permute-done.56 = bf16[2,24,3840]{2,1,0:T(8,128)(2,1)S(1)} collective-permute-done((bf16[2,24,3840]{2,1,0:T(8,128)(2,1)S(1)}, bf16[2,24,3840]{2,1,0:T(8,128)(2,1)S(1)}, u32[]{:S(2)}, u32[]{:S(2)}) %collective-permute-start.56) | collective-permute-done | bytes 368672 | tf_op jit(solution)/shard_map/ppermute | solution.py:338
  216.3 6.4 %collective-permute-done.59.refs_1_ = bf16[1,24,3840]{2,1,0:T(8,128)(2,1)S(1)} collective-permute-done((bf16[1,24,3840]{2,1,0:T(8,128)(2,1)S(1)}, bf16[1,24,3840]{2,1,0:T(8,128)(2,1)S(1)}, u32[]{:S(2)}, u32[]{:S(2)}) %collective-permute-start.59) | collective-permute-done | bytes 184352 | tf_op jit(solution)/shard_map/ppermute | solution.py:338
  225.8 2.9 %collective-permute-start.63 = (bf16[1,24,2432]{2,1,0:T(8,128)(2,1)S(1)}, bf16[1,24,2432]{2,1,0:T(8,128)(2,1)S(1)}, u32[]{:S(2)}, u32[]{:S(2)}) collective-permute-start(bf16[1,24,2432]{2,1,0:T(8,128)(2,1)S(1)} %get-tuple-element.419), channel_id=1, source_target_pairs={{0,24},{1,25},{2,26},{3,27},{4,28},{5,29},{6,30},{7,31},{8,16},{9,... | collective-permute-start | bytes 350216 | tf_op jit(solution)/shard_map/ppermute | solution.py:338
  (256 shorter events, 112.1 us)
Async XLA Ops:
  19.5 14.6 %collective-permute-start.6 = (bf16[4,24,2432]{2,1,0:T(8,128)(2,1)S(1)}, bf16[4,24,2432]{2,1,0:T(8,128)(2,1)S(1)}, u32[]{:S(2)}, u32[]{:S(2)}) collective-permute-start(bf16[4,24,2432]{2,1,0:T(8,128)(2,1)S(1)} %pad_maximum_fusion.8.refs_0_), channel_id=1, source_target_pairs={{0,6},{1,7},{2,4},{3,5},{4,2},{5,3},{6,0},{7,1},{8,14},{9,15},{10,... | collective-permute-start | bytes 1400840 | tf_op jit(solution)/shard_map/ppermute | solution.py:338
  22.0 19.4 %collective-permute-start.5 = (bf16[4,24,2432]{2,1,0:T(8,128)(2,1)S(1)}, bf16[4,24,2432]{2,1,0:T(8,128)(2,1)S(1)}, u32[]{:S(2)}, u32[]{:S(2)}) collective-permute-start(bf16[4,24,2432]{2,1,0:T(8,128)(2,1)S(1)} %pad_maximum_fusion.8.refs_0_), channel_id=1, source_target_pairs={{0,4},{1,5},{2,6},{3,7},{4,0},{5,1},{6,2},{7,3},{8,12},{9,13},{10,... | collective-permute-start | bytes 1400840 | tf_op jit(solution)/shard_map/ppermute | solution.py:338
  22.5 18.9 %collective-permute-start.4 = (bf16[4,24,2432]{2,1,0:T(8,128)(2,1)S(1)}, bf16[4,24,2432]{2,1,0:T(8,128)(2,1)S(1)}, u32[]{:S(2)}, u32[]{:S(2)}) collective-permute-start(bf16[4,24,2432]{2,1,0:T(8,128)(2,1)S(1)} %pad_maximum_fusion.8.refs_0_), channel_id=1, source_target_pairs={{0,2},{1,3},{2,0},{3,1},{4,6},{5,7},{6,4},{7,5},{8,10},{9,11},{10,... | collective-permute-start | bytes 1400840 | tf_op jit(solution)/shard_map/ppermute | solution.py:338
  41.5 15.4 %collective-permute-start.12 = (bf16[1,96,768]{2,1,0:T(8,128)(2,1)}, bf16[1,96,768]{2,1,0:T(8,128)(2,1)}, u32[]{:S(2)}, u32[]{:S(2)}) collective-permute-start(bf16[1,96,768]{2,1,0:T(8,128)(2,1)} %bitcast.4), channel_id=1, source_target_pairs={{0,16},{1,17},{2,18},{3,19},{4,20},{5,21},{6,22},{7,23},{8,24},{9,... | collective-permute-start | bytes 442376 | tf_op jit(solution)/shard_map/ppermute | solution.py:338
  57.9 19.5 %collective-permute-start.17 = (bf16[4,24,1920]{2,1,0:T(8,128)(2,1)}, bf16[4,24,1920]{2,1,0:T(8,128)(2,1)}, u32[]{:S(2)}, u32[]{:S(2)}) collective-permute-start(bf16[4,24,1920]{2,1,0:T(8,128)(2,1)} %get-tuple-element.241.refs_0_), channel_id=1, source_target_pairs={{0,4},{1,5},{2,6},{3,7},{4,0},{5,1},{6,2},{7,3},{8,12},{9,13},{10,... | collective-permute-start | bytes 1105928 | tf_op jit(solution)/shard_map/ppermute | solution.py:338
  58.8 18.5 %collective-permute-start.18 = (bf16[4,24,1920]{2,1,0:T(8,128)(2,1)}, bf16[4,24,1920]{2,1,0:T(8,128)(2,1)}, u32[]{:S(2)}, u32[]{:S(2)}) collective-permute-start(bf16[4,24,1920]{2,1,0:T(8,128)(2,1)} %collective-permute-done.10.refs_1_), channel_id=1, source_target_pairs={{0,4},{1,5},{2,6},{3,7},{4,0},{5,1},{6,2},{7,3},{8,12},{9,13},{10,... | collective-permute-start | bytes 1105928 | tf_op jit(solution)/shard_map/ppermute | solution.py:338
  59.9 17.4 %collective-permute-start.19 = (bf16[4,24,1920]{2,1,0:T(8,128)(2,1)S(1)}, bf16[4,24,1920]{2,1,0:T(8,128)(2,1)}, u32[]{:S(2)}, u32[]{:S(2)}) collective-permute-start(bf16[4,24,1920]{2,1,0:T(8,128)(2,1)S(1)} %get-tuple-element.243.refs_2_), channel_id=1, source_target_pairs={{0,2},{1,3},{2,0},{3,1},{4,6},{5,7},{6,4},{7,5},{8,10},{9,11},{10,... | collective-permute-start | bytes 1105928 | tf_op jit(solution)/shard_map/ppermute | solution.py:338
  60.9 16.4 %collective-permute-start.20 = (bf16[4,24,1920]{2,1,0:T(8,128)(2,1)}, bf16[4,24,1920]{2,1,0:T(8,128)(2,1)}, u32[]{:S(2)}, u32[]{:S(2)}) collective-permute-start(bf16[4,24,1920]{2,1,0:T(8,128)(2,1)} %collective-permute-done.11.refs_3_), channel_id=1, source_target_pairs={{0,2},{1,3},{2,0},{3,1},{4,6},{5,7},{6,4},{7,5},{8,10},{9,11},{10,... | collective-permute-start | bytes 1105928 | tf_op jit(solution)/shard_map/ppermute | solution.py:338
  63.0 14.4 %collective-permute-start.21 = (bf16[2,96,768]{2,1,0:T(8,128)(2,1)S(1)}, bf16[2,96,768]{2,1,0:T(8,128)(2,1)}, u32[]{:S(2)}, u32[]{:S(2)}) collective-permute-start(bf16[2,96,768]{2,1,0:T(8,128)(2,1)S(1)} %pad_maximum_fusion.11), channel_id=1, source_target_pairs={{0,8},{1,9},{2,10},{3,11},{4,12},{5,13},{6,14},{7,15},{8,0},{9,1},... | collective-permute-start | bytes 884744 | tf_op jit(solution)/shard_map/ppermute | solution.py:338
  89.9 23.6 %collective-permute-start.33 = (bf16[4,96,768]{2,1,0:T(8,128)(2,1)S(1)}, bf16[4,96,768]{2,1,0:T(8,128)(2,1)S(1)}, u32[]{:S(2)}, u32[]{:S(2)}) collective-permute-start(bf16[4,96,768]{2,1,0:T(8,128)(2,1)S(1)} %pad_maximum_fusion.5.refs_0_), channel_id=1, source_target_pairs={{0,6},{1,7},{2,4},{3,5},{4,2},{5,3},{6,0},{7,1},{8,14},{9,15},{10,... | collective-permute-start | bytes 1769480 | tf_op jit(solution)/shard_map/ppermute | solution.py:338
  91.4 26.5 %collective-permute-start.32 = (bf16[4,96,768]{2,1,0:T(8,128)(2,1)S(1)}, bf16[4,96,768]{2,1,0:T(8,128)(2,1)S(1)}, u32[]{:S(2)}, u32[]{:S(2)}) collective-permute-start(bf16[4,96,768]{2,1,0:T(8,128)(2,1)S(1)} %pad_maximum_fusion.5.refs_0_), channel_id=1, source_target_pairs={{0,4},{1,5},{2,6},{3,7},{4,0},{5,1},{6,2},{7,3},{8,12},{9,13},{10,... | collective-permute-start | bytes 1769480 | tf_op jit(solution)/shard_map/ppermute | solution.py:338
  92.4 25.5 %collective-permute-start.31 = (bf16[4,96,768]{2,1,0:T(8,128)(2,1)S(1)}, bf16[4,96,768]{2,1,0:T(8,128)(2,1)S(1)}, u32[]{:S(2)}, u32[]{:S(2)}) collective-permute-start(bf16[4,96,768]{2,1,0:T(8,128)(2,1)S(1)} %pad_maximum_fusion.5.refs_0_), channel_id=1, source_target_pairs={{0,2},{1,3},{2,0},{3,1},{4,6},{5,7},{6,4},{7,5},{8,10},{9,11},{10,... | collective-permute-start | bytes 1769480 | tf_op jit(solution)/shard_map/ppermute | solution.py:338
  94.7 15.6 %collective-permute-start.34 = (bf16[2,128,768]{2,1,0:T(8,128)(2,1)S(1)}, bf16[2,128,768]{2,1,0:T(8,128)(2,1)S(1)}, u32[]{:S(2)}, u32[]{:S(2)}) collective-permute-start(bf16[2,128,768]{2,1,0:T(8,128)(2,1)S(1)} %get-tuple-element.434), channel_id=1, source_target_pairs={{0,1},{1,0},{2,3},{3,2},{4,5},{5,4},{6,7},{7,6},{8,9},{9,8},{10,11... | collective-permute-start | bytes 1179656 | tf_op jit(solution)/shard_map/ppermute | solution.py:338
  126.4 15.4 %collective-permute-start.41 = (bf16[8,96,384]{2,1,0:T(8,128)(2,1)S(1)}, bf16[8,96,384]{2,1,0:T(8,128)(2,1)S(1)}, u32[]{:S(2)}, u32[]{:S(2)}) collective-permute-start(bf16[8,96,384]{2,1,0:T(8,128)(2,1)S(1)} %get-tuple-element.397), channel_id=1, source_target_pairs={{0,2},{1,3},{2,0},{3,1},{4,6},{5,7},{6,4},{7,5},{8,10},{9,11},{10,... | collective-permute-start | bytes 1769480 | tf_op jit(solution)/shard_map/ppermute | solution.py:338
  127.6 15.1 %collective-permute-start.40 = (bf16[8,96,384]{2,1,0:T(8,128)(2,1)S(1)}, bf16[8,96,384]{2,1,0:T(8,128)(2,1)S(1)}, u32[]{:S(2)}, u32[]{:S(2)}) collective-permute-start(bf16[8,96,384]{2,1,0:T(8,128)(2,1)S(1)} %get-tuple-element.398), channel_id=1, source_target_pairs={{0,4},{1,5},{2,6},{3,7},{4,0},{5,1},{6,2},{7,3},{8,12},{9,13},{10,... | collective-permute-start | bytes 1769480 | tf_op jit(solution)/shard_map/ppermute | solution.py:338
  157.7 18.6 %collective-permute-start.47 = (bf16[8,24,1920]{2,1,0:T(8,128)(2,1)S(1)}, bf16[8,24,1920]{2,1,0:T(8,128)(2,1)S(1)}, u32[]{:S(2)}, u32[]{:S(2)}) collective-permute-start(bf16[8,24,1920]{2,1,0:T(8,128)(2,1)S(1)} %get-tuple-element.393), channel_id=1, source_target_pairs={{0,2},{1,3},{2,0},{3,1},{4,6},{5,7},{6,4},{7,5},{8,10},{9,11},{10,... | collective-permute-start | bytes 2211848 | tf_op jit(solution)/shard_map/ppermute | solution.py:338
  158.9 18.2 %collective-permute-start.46 = (bf16[8,24,1920]{2,1,0:T(8,128)(2,1)S(1)}, bf16[8,24,1920]{2,1,0:T(8,128)(2,1)S(1)}, u32[]{:S(2)}, u32[]{:S(2)}) collective-permute-start(bf16[8,24,1920]{2,1,0:T(8,128)(2,1)S(1)} %get-tuple-element.394), channel_id=1, source_target_pairs={{0,4},{1,5},{2,6},{3,7},{4,0},{5,1},{6,2},{7,3},{8,12},{9,13},{10,... | collective-permute-start | bytes 2211848 | tf_op jit(solution)/shard_map/ppermute | solution.py:338
  159.9 12.9 %collective-permute-start.48 = (bf16[2,128,768]{2,1,0:T(8,128)(2,1)S(1)}, bf16[2,128,768]{2,1,0:T(8,128)(2,1)S(1)}, u32[]{:S(2)}, u32[]{:S(2)}) collective-permute-start(bf16[2,128,768]{2,1,0:T(8,128)(2,1)S(1)} %bitcast.134), channel_id=1, source_target_pairs={{0,1},{1,0},{2,3},{3,2},{4,5},{5,4},{6,7},{7,6},{8,9},{9,8},{10,11... | collective-permute-start | bytes 1179656 | tf_op jit(solution)/shard_map/ppermute | solution.py:338
  160.1 12.6 %collective-permute-start.45 = (bf16[2,96,768]{2,1,0:T(8,128)(2,1)S(1)}, bf16[2,96,768]{2,1,0:T(8,128)(2,1)S(1)}, u32[]{:S(2)}, u32[]{:S(2)}) collective-permute-start(bf16[2,96,768]{2,1,0:T(8,128)(2,1)S(1)} %get-tuple-element.411), channel_id=1, source_target_pairs={{0,8},{1,9},{2,10},{3,11},{4,12},{5,13},{6,14},{7,15},{8,0},{9,1},... | collective-permute-start | bytes 884744 | tf_op jit(solution)/shard_map/ppermute | solution.py:338
  195.6 12.5 %collective-permute-start.54 = (bf16[8,24,1152]{2,1,0:T(8,128)(2,1)S(1)}, bf16[8,24,1152]{2,1,0:T(8,128)(2,1)S(1)}, u32[]{:S(2)}, u32[]{:S(2)}) collective-permute-start(bf16[8,24,1152]{2,1,0:T(8,128)(2,1)S(1)} %get-tuple-element.403), channel_id=1, source_target_pairs={{0,4},{1,5},{2,6},{3,7},{4,0},{5,1},{6,2},{7,3},{8,12},{9,13},{10,... | collective-permute-start | bytes 1327112 | tf_op jit(solution)/shard_map/ppermute | solution.py:338
  196.6 13.0 %collective-permute-start.55 = (bf16[8,24,1280]{2,1,0:T(8,128)(2,1)S(1)}, bf16[8,24,1280]{2,1,0:T(8,128)(2,1)S(1)}, u32[]{:S(2)}, u32[]{:S(2)}) collective-permute-start(bf16[8,24,1280]{2,1,0:T(8,128)(2,1)S(1)} %get-tuple-element.401), channel_id=1, source_target_pairs={{0,2},{1,3},{2,0},{3,1},{4,6},{5,7},{6,4},{7,5},{8,10},{9,11},{10,... | collective-permute-start | bytes 1474568 | tf_op jit(solution)/shard_map/ppermute | solution.py:338
  209.7 13.1 %collective-permute-start.57 = (bf16[4,24,1152]{2,1,0:T(8,128)(2,1)S(1)}, bf16[4,24,1152]{2,1,0:T(8,128)(2,1)S(1)}, u32[]{:S(2)}, u32[]{:S(2)}) collective-permute-start(bf16[4,24,1152]{2,1,0:T(8,128)(2,1)S(1)} %get-tuple-element.423), channel_id=1, source_target_pairs={{0,2},{1,3},{2,0},{3,1},{4,6},{5,7},{6,4},{7,5},{8,10},{9,11},{10,... | collective-permute-start | bytes 663560 | tf_op jit(solution)/shard_map/ppermute | solution.py:338
  210.9 13.6 %collective-permute-start.60 = (bf16[2,128,768]{2,1,0:T(8,128)(2,1)S(1)}, bf16[2,128,768]{2,1,0:T(8,128)(2,1)S(1)}, u32[]{:S(2)}, u32[]{:S(2)}) collective-permute-start(bf16[2,128,768]{2,1,0:T(8,128)(2,1)S(1)} %get-tuple-element.363), channel_id=1, source_target_pairs={{0,2},{1,3},{2,0},{3,1},{4,6},{5,7},{6,4},{7,5},{8,10},{9,11},{10,... | collective-permute-start | bytes 1179656 | tf_op jit(solution)/shard_map/ppermute | solution.py:338
  224.5 14.5 %collective-permute-start.64 = (bf16[2,128,768]{2,1,0:T(8,128)(2,1)S(1)}, bf16[2,128,768]{2,1,0:T(8,128)(2,1)S(1)}, u32[]{:S(2)}, u32[]{:S(2)}) collective-permute-start(bf16[2,128,768]{2,1,0:T(8,128)(2,1)S(1)} %get-tuple-element.377), channel_id=1, source_target_pairs={{0,2},{1,3},{2,0},{3,1},{4,6},{5,7},{6,4},{7,5},{8,10},{9,11},{10,... | collective-permute-start | bytes 1179656 | tf_op jit(solution)/shard_map/ppermute | solution.py:338
  (67 other events, 414.5 us)

commit v4 on v3

--- a/solution.py
+++ b/solution.py
@@ -435,10 +435,14 @@
         self.kept = sum(term[0].astype(jnp.float32) for term in terms)
         self.got = [swap(one, mask) for one, mask in zip(ones, LINE[1:])]
 
-    def plane_one(self):
+    def plane_one(self, more=None):
         kept, sent = [], []
         for low, high in halves_of(self.kept.shape[2]):
             pairs = [(one[..., low:high]) for one in (self.kept, self.got)]
+            if more and low:
+                pairs = [
+                    jnp.concatenate(pair, -1) for pair in zip(pairs, (more.kept, more.got))
+                ]
             kept.append(sum_low(*(one[:8] for one in pairs)))
             sent.append(sum_low(*(one[8:] for one in pairs)))
         self.kept, self.got = kept, [swap(one, bit) for one, bit in zip(sent, (Y, X))]
@@ -596,20 +600,14 @@
 
 
 def first_parts_kernel(
-    me_ref,
-    normed_ref,
-    query_ref,
-    key_ref,
-    value_ref,
-    one_ref,
-    two_ref,
-    bias_ref,
-    kept_ref,
-    sent_ref,
-    sum_ref,
+    me_ref, normed_ref, query_ref, key_ref, value_ref, kept_ref, sent_ref, sum_ref
 ):
-    me, outs = me_ref[0], (kept_ref, sent_ref)
-    low = multiply_rows(me, normed_ref, [query_ref, key_ref, value_ref], sum_ref, outs, 0)
+    rights = [query_ref, key_ref, value_ref]
+    multiply_rows(me_ref[0], normed_ref, rights, sum_ref, (kept_ref, sent_ref), 0)
+
+
+def vector_parts_kernel(me_ref, one_ref, two_ref, bias_ref, kept_ref, sent_ref, sum_ref):
+    me, outs, low = me_ref[0], (kept_ref, sent_ref), 0
     rows = kept_ref.shape[1]
     vectors = jnp.concatenate([one_ref[:4], two_ref[:4]], 0)
     width, bias = vectors.shape[1], jnp.broadcast_to(bias_ref[...], (8, bias_ref.shape[1]))
@@ -1194,6 +1192,17 @@
     down_sum.near()
     out_kept, out_got = from_micro_c(result)
     grad_query, grad_key, grad_value = attend_back(project, probs, grad_mixed)
+    qkv_sum = Scatter(
+        parts_call(
+            first_parts_kernel,
+            [normed_one, grad_query, grad_key, grad_value],
+            rows,
+            wide,
+            (width, width),
+            13,
+            me,
+        )
+    )
     (
         down_sum.kept,
         down_sum.got,
@@ -1202,6 +1211,8 @@
         grad_query,
         grad_key,
         grad_value,
+        qkv_sum.kept,
+        qkv_sum.sent,
         out_kept,
         out_got,
     ) = fence(
@@ -1212,31 +1223,20 @@
         grad_query,
         grad_key,
         grad_value,
+        qkv_sum.kept,
+        qkv_sum.sent,
         out_kept,
         out_got,
     )
     up_sum.plane_two()
+    qkv_sum.cores()
     down_sum.far()
     in_grad, sums_one = first_back(
         grad_query, grad_key, grad_value, qkv_full, tokens, gain_one, grad_mid
     )
-    qkv_sum = Scatter(
+    vector_sum = Scatter(
         parts_call(
-            first_parts_kernel,
-            [
-                normed_one,
-                grad_query,
-                grad_key,
-                grad_value,
-                sums_one,
-                sums_two,
-                grad_bias_up,
-            ],
-            rows,
-            wide + 128,
-            (width, width),
-            16,
-            me,
+            vector_parts_kernel, [sums_one, sums_two, grad_bias_up], rows, 128, (8, 128), 8, me
         )
     )
     (
@@ -1245,7 +1245,9 @@
         up_sum.kept,
         up_sum.got,
         qkv_sum.kept,
-        qkv_sum.sent,
+        qkv_sum.got,
+        vector_sum.kept,
+        vector_sum.sent,
         in_grad,
         out_kept,
         out_got,
@@ -1255,14 +1257,16 @@
         up_sum.kept,
         up_sum.got,
         qkv_sum.kept,
-        qkv_sum.sent,
+        qkv_sum.got,
+        vector_sum.kept,
+        vector_sum.sent,
         in_grad,
         out_kept,
         out_got,
     )
 
     up_sum.plane_end()
-    qkv_sum.cores()
+    vector_sum.cores()
     in_kept, in_got = from_micro_c(in_grad)
     out_kept, out_sent = from_micro_pick(out_kept, out_got, core)
     (
@@ -1270,6 +1274,8 @@
         up_sum.got,
         qkv_sum.kept,
         qkv_sum.got,
+        vector_sum.kept,
+        vector_sum.got,
         in_kept,
         in_got,
         out_kept,
@@ -1279,13 +1285,15 @@
         up_sum.got,
         qkv_sum.kept,
         qkv_sum.got,
+        vector_sum.kept,
+        vector_sum.got,
         in_kept,
         in_got,
         out_kept,
         out_sent,
     )
 
-    qkv_sum.plane_one()
+    qkv_sum.plane_one(vector_sum)
     up_sum.near()
     in_kept, in_sent = from_micro_pick(in_kept, in_got, core)
     (

time: 241 us -> 247 us (1.025)
  local copies, waits for them, and re-layouts: 9.91 us -> 13.1 us
    convert_element_type x15, other arithmetic: 5.59 us -> 9.28 us  [sum_low(): return total.astype(jnp.bfloat16)]
    ppermute x65 -> x66, starting transfers between devices: 57.9 us -> 58.6 us  [swap(): return lax.ppermute(values, AXES, pairs)]
    ppermute x65 -> x66, waiting for transfers between devices: 78.6 us -> 78 us  [swap(): return lax.ppermute(values, AXES, pairs)]
    pallas_call x3 -> x4, Pallas kernels: 10.9 us -> 11.2 us  [parts_call(): pl.pallas_call(kernel, grid=(1,), out_shape=[jax.ShapeDtypeStruct(half, j...]
  transfers between devices with their start and end apart: 65 -> 66, of which waited for: 30 -> 30; matrix products, arithmetic and copies ran while one was open for 10% -> 10% of each run, Pallas kernels for 28% -> 28%
where the time goes in v4:
time: 247 us; the launch traced here: 246 us
  waiting for transfers between devices  78 us (32%)
  Pallas kernels  69.1 us (28%)
  starting transfers between devices  58.6 us (24%)
  other arithmetic  21.4 us (9%)
  local copies, waits for them, and re-layouts  13.1 us (5%)
  matrix products  4.77 us (2%)
    ppermute x66, waiting for transfers between devices, swap(): return lax.ppermute(values, AXES, pairs)  78 us
    ppermute x66, starting transfers between devices, swap(): return lax.ppermute(values, AXES, pairs)  58.6 us
    pallas_call x1, Pallas kernels, attend_back(): pl.pallas_call(attend_back_kernel, grid=(pairs,), out_shape=[shape] * 3,...  11.9 us
    pallas_call x4, Pallas kernels, parts_call(): pl.pallas_call(kernel, grid=(1,), out_shape=[jax.ShapeDtypeStruct(half, j...  11.2 us
    pallas_call x1, Pallas kernels, attend(): pl.pallas_call(attend_kernel, grid=(pairs,), out_shape=[jax.ShapeDtypeStr...  11 us
    convert_element_type x15, other arithmetic, sum_low(): return total.astype(jnp.bfloat16)  9.28 us
    pallas_call x3, Pallas kernels, shuffle(): pl.pallas_call(functools.partial(shuffle_kernel, moves, len(arrays)), gri...  8.04 us
    pallas_call x1, Pallas kernels, up_forward(): pl.pallas_call(up_kernel, grid=(inner // tile,), out_shape=[shape, shape]...  6.68 us
  transfers between devices with their start and end apart: 66, of which 30 were waited for; matrix products, arithmetic and copies ran while one was open for 10% of the time, Pallas kernels for 28%

profile of v4, /device:TPU:0, one launch (start us, length us, event | category | flops | bytes accessed | tf_op | source)
XLA Modules:
  0.0 246.5 jit_solution(14685398945170586857)
XLA Ops:
  3.3 5.1 %collective-permute-start.2 = (bf16[1,24,2432]{2,1,0:T(8,128)(2,1)S(1)}, bf16[1,24,2432]{2,1,0:T(8,128)(2,1)S(1)}, u32[]{:S(2)}, u32[]{:S(2)}) collective-permute-start(bf16[1,24,2432]{2,1,0:T(8,128)(2,1)S(1)} %maximum_bitcast_fusion.1), channel_id=1, source_target_pairs={{0,24},{1,25},{2,26},{3,27},{4,28},{5,29},{6,30},{7,31},{8,16},{9,... | collective-permute-start | bytes 350216 | tf_op jit(solution)/shard_map/ppermute | solution.py:338
  12.5 2.7 %collective-permute-done.1 = bf16[1,24,2432]{2,1,0:T(8,128)(2,1)S(1)} collective-permute-done((bf16[1,24,2432]{2,1,0:T(8,128)(2,1)S(1)}, bf16[1,24,2432]{2,1,0:T(8,128)(2,1)S(1)}, u32[]{:S(2)}, u32[]{:S(2)}) %collective-permute-start.1) | collective-permute-done | bytes 116768 | tf_op jit(solution)/shard_map/ppermute | solution.py:338
  15.2 3.1 %collective-permute-done = bf16[1,24,2432]{2,1,0:T(8,128)(2,1)S(1)} collective-permute-done((bf16[1,24,2432]{2,1,0:T(8,128)(2,1)S(1)}, bf16[1,24,2432]{2,1,0:T(8,128)(2,1)S(1)}, u32[]{:S(2)}, u32[]{:S(2)}) %collective-permute-start) | collective-permute-done | bytes 116768 | tf_op jit(solution)/shard_map/ppermute | solution.py:338
  25.6 6.5 %collective-permute-done.7 = bf16[1,24,3840]{2,1,0:T(8,128)(2,1)S(1)} collective-permute-done((bf16[1,24,3840]{2,1,0:T(8,128)(2,1)S(1)}, bf16[1,24,3840]{2,1,0:T(8,128)(2,1)S(1)}, u32[]{:S(2)}, u32[]{:S(2)}) %collective-permute-start.7) | collective-permute-done | bytes 184352 | tf_op jit(solution)/shard_map/ppermute | solution.py:338
  34.2 7.3 %collective-permute-done.5.refs_2_ = bf16[4,24,2432]{2,1,0:T(8,128)(2,1)S(1)} collective-permute-done((bf16[4,24,2432]{2,1,0:T(8,128)(2,1)S(1)}, bf16[4,24,2432]{2,1,0:T(8,128)(2,1)S(1)}, u32[]{:S(2)}, u32[]{:S(2)}) %collective-permute-start.5) | collective-permute-done | bytes 466976 | tf_op jit(solution)/shard_map/ppermute | solution.py:338
  52.1 4.8 %shard_map.272.query_ref.key_ref.value_ref = bf16[512,2304]{1,0:T(8,128)(2,1)S(1)} custom-call(bf16[512,768]{1,0:T(8,128)(2,1)S(1)} %add_convert_fusion.2.normed_ref, bf16[768,2304]{1,0:T(8,128)(2,1)} %bitcast.112, f32[1,2304]{1,0:T(1,128)S(1)} %fusion.14.bias_ref), custom_call_target="tpu_custom_call" | custom-call | flops 1024 | bytes 1024 | tf_op jit(solution)/shard_map/pallas_call | solution.py:789
  65.5 11.0 %shard_map.273 = (bf16[512,768]{1,0:T(8,128)(2,1)S(1)}, bf16[12,512,512]{2,1,0:T(8,128)(2,1)}) custom-call(s32[1,512]{1,0:T(1,128)S(1)} %bitcast.121, bf16[512,2304]{1,0:T(8,128)(2,1)S(1)} %shard_map.272.query_ref.key_ref.value_ref, bf16[512,2304]{1,0:T(8,128)(2,1)S(1)} %shard_map.272.query_ref.key_ref.value_ref, ...), custom_call_target="tpu_custom_call" | custom-call | flops 1024 | bytes 1024 | tf_op jit(solution)/shard_map/pallas_call | solution.py:726
  84.6 5.3 %collective-permute-done.30 = bf16[2,128,768]{2,1,0:T(8,128)(2,1)} collective-permute-done((bf16[2,128,768]{2,1,0:T(8,128)(2,1)}, bf16[2,128,768]{2,1,0:T(8,128)(2,1)}, u32[]{:S(2)}, u32[]{:S(2)}) %collective-permute-start.30) | collective-permute-done | bytes 393248 | tf_op jit(solution)/shard_map/ppermute | solution.py:338
  94.8 5.6 %shard_map.274 = (bf16[32,24,768]{2,1,0:T(8,128)(2,1)}, bf16[32,24,3072]{2,1,0:T(8,128)(2,1)}) custom-call(s32[1]{0:T(128)} %bitcast.12.me_ref, bf16[4,24,1920]{2,1,0:T(8,128)(2,1)} %get-tuple-element.249.refs_0_, bf16[4,24,1920]{2,1,0:T(8,128)(2,1)} %collective-permute-done.10.refs_1_, bf16[4,24,1920]{2,1,0:T(8,128)(2,1)} %copy-done.18, ...), custom_call_target="tpu_custom_call" | custom-call | flops 1024 | bytes 1024 | tf_op jit(solution)/shard_map/pallas_call | solution.py:500
  103.6 6.7 %shard_map.275 = (bf16[512,3072]{1,0:T(8,128)(2,1)S(1)}, bf16[512,3072]{1,0:T(8,128)(2,1)S(1)}) custom-call(bf16[512,768]{1,0:T(8,128)(2,1)S(1)} %add_convert_fusion.1.normed_ref, bf16[768,3072]{1,0:T(8,128)(2,1)} %bitcast.106, f32[1,3072]{1,0:T(1,128)S(1)} %reshape_squeeze.3.bias_ref), custom_call_target="tpu_custom_call" | custom-call | flops 1024 | bytes 1024 | tf_op jit(solution)/shard_map/pallas_call | solution.py:823
  110.4 3.1 %shard_map.276 = (bf16[16,96,768]{2,1,0:T(8,128)(2,1)S(1)}, bf16[16,96,768]{2,1,0:T(8,128)(2,1)S(1)}) custom-call(s32[1]{0:T(128)} %bitcast.12.me_ref, bf16[512,3072]{1,0:T(8,128)(2,1)S(1)} %get-tuple-element.314.hidden_ref, bf16[512,768]{1,0:T(8,128)(2,1)S(1)} %bitcast.114), custom_call_target="tpu_custom_call" | custom-call | flops 1024 | bytes 1024 | tf_op jit(solution)/shard_map/pallas_call | solution.py:554
  113.6 4.4 %collective-permute-done.32.refs_2_ = bf16[4,96,768]{2,1,0:T(8,128)(2,1)S(1)} collective-permute-done((bf16[4,96,768]{2,1,0:T(8,128)(2,1)S(1)}, bf16[4,96,768]{2,1,0:T(8,128)(2,1)S(1)}, u32[]{:S(2)}, u32[]{:S(2)}) %collective-permute-start.32) | collective-permute-done | bytes 589856 | tf_op jit(solution)/shard_map/ppermute | solution.py:338
  119.0 4.3 %collective-permute-done.35.refs_4_ = bf16[4,96,768]{2,1,0:T(8,128)(2,1)S(1)} collective-permute-done((bf16[4,96,768]{2,1,0:T(8,128)(2,1)S(1)}, bf16[4,96,768]{2,1,0:T(8,128)(2,1)S(1)}, u32[]{:S(2)}, u32[]{:S(2)}) %collective-permute-start.35) | collective-permute-done | bytes 589856 | tf_op jit(solution)/shard_map/ppermute | solution.py:338
  129.0 4.6 %shard_map.278 = (bf16[512,3072]{1,0:T(8,128)(2,1)S(1)}, f32[1,3072]{1,0:T(1,128)S(1)}) custom-call(bf16[512,768]{1,0:T(8,128)(2,1)S(1)} %bitcast.115, bf16[3072,768]{1,0:T(8,128)(2,1)S(1)} %bitcast.110, bf16[512,3072]{1,0:T(8,128)(2,1)S(1)} %get-tuple-element.291.slope_ref), custom_call_target="tpu_custom_call" | custom-call | flops 1024 | bytes 1024 | tf_op jit(solution)/shard_map/pallas_call | solution.py:850
  133.7 5.4 %shard_map.279 = (f32[512,768]{1,0:T(8,128)S(1)}, bf16[512,768]{1,0:T(8,128)(2,1)S(1)}, bf16[512,768]{1,0:T(8,128)(2,1)S(1)}, f32[8,768]{1,0:T(8,128)S(1)}) custom-call(bf16[512,3072]{1,0:T(8,128)(2,1)S(1)} %get-tuple-element.302.pre_ref, bf16[768,3072]{1,0:T(8,128)(2,1)S(1)} %bitcast.109, f32[512,768]{1,0:T(8,128)S(1)} %get-tuple-element.480.resid_ref, ...), custom_call_target="tpu_custom_call" | custom-call | flops 1024 | bytes 1024 | tf_op jit(solution)/shard_map/pallas_call | solution.py:894
  139.1 2.9 %collective-permute-done.41 = bf16[8,96,384]{2,1,0:T(8,128)(2,1)S(1)} collective-permute-done((bf16[8,96,384]{2,1,0:T(8,128)(2,1)S(1)}, bf16[8,96,384]{2,1,0:T(8,128)(2,1)S(1)}, u32[]{:S(2)}, u32[]{:S(2)}) %collective-permute-start.41) | collective-permute-done | bytes 589856 | tf_op jit(solution)/shard_map/ppermute | solution.py:338
  145.1 4.0 %shard_map.280 = (bf16[16,24,3840]{2,1,0:T(8,128)(2,1)S(1)}, bf16[16,24,3840]{2,1,0:T(8,128)(2,1)S(1)}) custom-call(s32[1]{0:T(128)} %bitcast.12.me_ref, bf16[512,768]{1,0:T(8,128)(2,1)S(1)} %copy-done.15, bf16[512,768]{1,0:T(8,128)(2,1)S(1)} %get-tuple-element.301.branch_ref, bf16[512,768]{1,0:T(8,128)(2,1)S(1)} %add_convert_fusion.1.normed_ref, ...), custom_call_target="tpu_custom_call" | custom-call | flops 1024 | bytes 1024 | tf_op jit(solution)/shard_map/pallas_call | solution.py:554
  154.5 2.7 %collective-permute-done.44 = bf16[16,24,3840]{2,1,0:T(8,128)(2,1)S(1)} collective-permute-done((bf16[16,24,3840]{2,1,0:T(8,128)(2,1)S(1)}, bf16[16,24,3840]{2,1,0:T(8,128)(2,1)S(1)}, u32[]{:S(2)}, u32[]{:S(2)}) %collective-permute-start.44) | collective-permute-done | bytes 2949152 | tf_op jit(solution)/shard_map/ppermute | solution.py:338
  163.0 11.9 %shard_map.281 = (bf16[512,768]{1,0:T(8,128)(2,1)S(1)}, bf16[512,768]{1,0:T(8,128)(2,1)S(1)}, bf16[512,768]{1,0:T(8,128)(2,1)S(1)}) custom-call(bf16[512,2304]{1,0:T(8,128)(2,1)S(1)} %shard_map.272.query_ref.key_ref.value_ref, bf16[512,2304]{1,0:T(8,128)(2,1)S(1)} %shard_map.272.query_ref.key_ref.value_ref, ...), custom_call_target="tpu_custom_call" | custom-call | flops 1024 | bytes 1024 | tf_op jit(solution)/shard_map/pallas_call | solution.py:749
  175.0 3.5 %shard_map.282 = (bf16[16,24,2304]{2,1,0:T(8,128)(2,1)S(1)}, bf16[16,24,2304]{2,1,0:T(8,128)(2,1)}) custom-call(s32[1]{0:T(128)} %bitcast.12.me_ref, bf16[512,768]{1,0:T(8,128)(2,1)S(1)} %copy-done.4, bf16[512,768]{1,0:T(8,128)(2,1)S(1)} %get-tuple-element.336.query_ref, bf16[512,768]{1,0:T(8,128)(2,1)S(1)} %get-tuple-element.337.key_ref, ...), custom_call_target="tpu_custom_call" | custom-call | flops 1024 | bytes 1024 | tf_op jit(solution)/shard_map/pallas_call | solution.py:554
  188.1 3.2 %shard_map.283 = (bf16[512,768]{1,0:T(8,128)(2,1)S(1)}, f32[8,768]{1,0:T(8,128)S(1)}) custom-call(bf16[512,768]{1,0:T(8,128)(2,1)S(1)} %copy-done.6, bf16[512,768]{1,0:T(8,128)(2,1)S(1)} %copy-done.8, bf16[512,768]{1,0:T(8,128)(2,1)S(1)} %copy-done.10, bf16[768,2304]{1,0:T(8,128)(2,1)S(1)} %bitcast.113, bf16[512,768]{1,0:T(8,128)(2,1)S(1)} %bitcast.118, ...), custom_call_target="tpu_custom_call" | custom-call | flops 1024 | bytes 1024 | tf_op jit(solution)/shard_map/pallas_call | solution.py:948
  204.5 9.1 %collective-permute-done.57 = bf16[2,24,3840]{2,1,0:T(8,128)(2,1)S(1)} collective-permute-done((bf16[2,24,3840]{2,1,0:T(8,128)(2,1)S(1)}, bf16[2,24,3840]{2,1,0:T(8,128)(2,1)S(1)}, u32[]{:S(2)}, u32[]{:S(2)}) %collective-permute-start.57) | collective-permute-done | bytes 368672 | tf_op jit(solution)/shard_map/ppermute | solution.py:338
  221.9 6.6 %collective-permute-done.60.refs_1_ = bf16[1,24,3840]{2,1,0:T(8,128)(2,1)S(1)} collective-permute-done((bf16[1,24,3840]{2,1,0:T(8,128)(2,1)S(1)}, bf16[1,24,3840]{2,1,0:T(8,128)(2,1)S(1)}, u32[]{:S(2)}, u32[]{:S(2)}) %collective-permute-start.60) | collective-permute-done | bytes 184352 | tf_op jit(solution)/shard_map/ppermute | solution.py:338
  231.5 2.9 %collective-permute-start.64 = (bf16[1,24,2432]{2,1,0:T(8,128)(2,1)S(1)}, bf16[1,24,2432]{2,1,0:T(8,128)(2,1)S(1)}, u32[]{:S(2)}, u32[]{:S(2)}) collective-permute-start(bf16[1,24,2432]{2,1,0:T(8,128)(2,1)S(1)} %get-tuple-element.435), channel_id=1, source_target_pairs={{0,24},{1,25},{2,26},{3,27},{4,28},{5,29},{6,30},{7,31},{8,16},{9,... | collective-permute-start | bytes 350216 | tf_op jit(solution)/shard_map/ppermute | solution.py:338
  (281 shorter events, 118.3 us)
Async XLA Ops:
  19.5 14.6 %collective-permute-start.6 = (bf16[4,24,2432]{2,1,0:T(8,128)(2,1)S(1)}, bf16[4,24,2432]{2,1,0:T(8,128)(2,1)S(1)}, u32[]{:S(2)}, u32[]{:S(2)}) collective-permute-start(bf16[4,24,2432]{2,1,0:T(8,128)(2,1)S(1)} %pad_maximum_fusion.10.refs_0_), channel_id=1, source_target_pairs={{0,6},{1,7},{2,4},{3,5},{4,2},{5,3},{6,0},{7,1},{8,14},{9,15},{10,... | collective-permute-start | bytes 1400840 | tf_op jit(solution)/shard_map/ppermute | solution.py:338
  22.0 19.4 %collective-permute-start.5 = (bf16[4,24,2432]{2,1,0:T(8,128)(2,1)S(1)}, bf16[4,24,2432]{2,1,0:T(8,128)(2,1)S(1)}, u32[]{:S(2)}, u32[]{:S(2)}) collective-permute-start(bf16[4,24,2432]{2,1,0:T(8,128)(2,1)S(1)} %pad_maximum_fusion.10.refs_0_), channel_id=1, source_target_pairs={{0,4},{1,5},{2,6},{3,7},{4,0},{5,1},{6,2},{7,3},{8,12},{9,13},{10,... | collective-permute-start | bytes 1400840 | tf_op jit(solution)/shard_map/ppermute | solution.py:338
  22.5 18.9 %collective-permute-start.4 = (bf16[4,24,2432]{2,1,0:T(8,128)(2,1)S(1)}, bf16[4,24,2432]{2,1,0:T(8,128)(2,1)S(1)}, u32[]{:S(2)}, u32[]{:S(2)}) collective-permute-start(bf16[4,24,2432]{2,1,0:T(8,128)(2,1)S(1)} %pad_maximum_fusion.10.refs_0_), channel_id=1, source_target_pairs={{0,2},{1,3},{2,0},{3,1},{4,6},{5,7},{6,4},{7,5},{8,10},{9,11},{10,... | collective-permute-start | bytes 1400840 | tf_op jit(solution)/shard_map/ppermute | solution.py:338
  41.5 15.4 %collective-permute-start.12 = (bf16[1,96,768]{2,1,0:T(8,128)(2,1)}, bf16[1,96,768]{2,1,0:T(8,128)(2,1)}, u32[]{:S(2)}, u32[]{:S(2)}) collective-permute-start(bf16[1,96,768]{2,1,0:T(8,128)(2,1)} %bitcast.4), channel_id=1, source_target_pairs={{0,16},{1,17},{2,18},{3,19},{4,20},{5,21},{6,22},{7,23},{8,24},{9,... | collective-permute-start | bytes 442376 | tf_op jit(solution)/shard_map/ppermute | solution.py:338
  57.9 19.5 %collective-permute-start.17 = (bf16[4,24,1920]{2,1,0:T(8,128)(2,1)}, bf16[4,24,1920]{2,1,0:T(8,128)(2,1)}, u32[]{:S(2)}, u32[]{:S(2)}) collective-permute-start(bf16[4,24,1920]{2,1,0:T(8,128)(2,1)} %get-tuple-element.249.refs_0_), channel_id=1, source_target_pairs={{0,4},{1,5},{2,6},{3,7},{4,0},{5,1},{6,2},{7,3},{8,12},{9,13},{10,... | collective-permute-start | bytes 1105928 | tf_op jit(solution)/shard_map/ppermute | solution.py:338
  58.8 18.5 %collective-permute-start.18 = (bf16[4,24,1920]{2,1,0:T(8,128)(2,1)}, bf16[4,24,1920]{2,1,0:T(8,128)(2,1)}, u32[]{:S(2)}, u32[]{:S(2)}) collective-permute-start(bf16[4,24,1920]{2,1,0:T(8,128)(2,1)} %collective-permute-done.10.refs_1_), channel_id=1, source_target_pairs={{0,4},{1,5},{2,6},{3,7},{4,0},{5,1},{6,2},{7,3},{8,12},{9,13},{10,... | collective-permute-start | bytes 1105928 | tf_op jit(solution)/shard_map/ppermute | solution.py:338
  59.9 17.5 %collective-permute-start.19 = (bf16[4,24,1920]{2,1,0:T(8,128)(2,1)S(1)}, bf16[4,24,1920]{2,1,0:T(8,128)(2,1)}, u32[]{:S(2)}, u32[]{:S(2)}) collective-permute-start(bf16[4,24,1920]{2,1,0:T(8,128)(2,1)S(1)} %get-tuple-element.251.refs_2_), channel_id=1, source_target_pairs={{0,2},{1,3},{2,0},{3,1},{4,6},{5,7},{6,4},{7,5},{8,10},{9,11},{10,... | collective-permute-start | bytes 1105928 | tf_op jit(solution)/shard_map/ppermute | solution.py:338
  60.9 16.5 %collective-permute-start.20 = (bf16[4,24,1920]{2,1,0:T(8,128)(2,1)}, bf16[4,24,1920]{2,1,0:T(8,128)(2,1)}, u32[]{:S(2)}, u32[]{:S(2)}) collective-permute-start(bf16[4,24,1920]{2,1,0:T(8,128)(2,1)} %collective-permute-done.11.refs_3_), channel_id=1, source_target_pairs={{0,2},{1,3},{2,0},{3,1},{4,6},{5,7},{6,4},{7,5},{8,10},{9,11},{10,... | collective-permute-start | bytes 1105928 | tf_op jit(solution)/shard_map/ppermute | solution.py:338
  63.0 14.4 %collective-permute-start.21 = (bf16[2,96,768]{2,1,0:T(8,128)(2,1)S(1)}, bf16[2,96,768]{2,1,0:T(8,128)(2,1)S(1)}, u32[]{:S(2)}, u32[]{:S(2)}) collective-permute-start(bf16[2,96,768]{2,1,0:T(8,128)(2,1)S(1)} %pad_maximum_fusion.13), channel_id=1, source_target_pairs={{0,8},{1,9},{2,10},{3,11},{4,12},{5,13},{6,14},{7,15},{8,0},{9,1},... | collective-permute-start | bytes 884744 | tf_op jit(solution)/shard_map/ppermute | solution.py:338
  89.9 23.6 %collective-permute-start.33 = (bf16[4,96,768]{2,1,0:T(8,128)(2,1)S(1)}, bf16[4,96,768]{2,1,0:T(8,128)(2,1)S(1)}, u32[]{:S(2)}, u32[]{:S(2)}) collective-permute-start(bf16[4,96,768]{2,1,0:T(8,128)(2,1)S(1)} %pad_maximum_fusion.5.refs_0_), channel_id=1, source_target_pairs={{0,6},{1,7},{2,4},{3,5},{4,2},{5,3},{6,0},{7,1},{8,14},{9,15},{10,... | collective-permute-start | bytes 1769480 | tf_op jit(solution)/shard_map/ppermute | solution.py:338
  91.5 26.5 %collective-permute-start.32 = (bf16[4,96,768]{2,1,0:T(8,128)(2,1)S(1)}, bf16[4,96,768]{2,1,0:T(8,128)(2,1)S(1)}, u32[]{:S(2)}, u32[]{:S(2)}) collective-permute-start(bf16[4,96,768]{2,1,0:T(8,128)(2,1)S(1)} %pad_maximum_fusion.5.refs_0_), channel_id=1, source_target_pairs={{0,4},{1,5},{2,6},{3,7},{4,0},{5,1},{6,2},{7,3},{8,12},{9,13},{10,... | collective-permute-start | bytes 1769480 | tf_op jit(solution)/shard_map/ppermute | solution.py:338
  92.5 25.5 %collective-permute-start.31 = (bf16[4,96,768]{2,1,0:T(8,128)(2,1)S(1)}, bf16[4,96,768]{2,1,0:T(8,128)(2,1)S(1)}, u32[]{:S(2)}, u32[]{:S(2)}) collective-permute-start(bf16[4,96,768]{2,1,0:T(8,128)(2,1)S(1)} %pad_maximum_fusion.5.refs_0_), channel_id=1, source_target_pairs={{0,2},{1,3},{2,0},{3,1},{4,6},{5,7},{6,4},{7,5},{8,10},{9,11},{10,... | collective-permute-start | bytes 1769480 | tf_op jit(solution)/shard_map/ppermute | solution.py:338
  94.7 15.6 %collective-permute-start.34 = (bf16[2,128,768]{2,1,0:T(8,128)(2,1)S(1)}, bf16[2,128,768]{2,1,0:T(8,128)(2,1)S(1)}, u32[]{:S(2)}, u32[]{:S(2)}) collective-permute-start(bf16[2,128,768]{2,1,0:T(8,128)(2,1)S(1)} %get-tuple-element.450), channel_id=1, source_target_pairs={{0,1},{1,0},{2,3},{3,2},{4,5},{5,4},{6,7},{7,6},{8,9},{9,8},{10,11... | collective-permute-start | bytes 1179656 | tf_op jit(solution)/shard_map/ppermute | solution.py:338
  126.5 15.4 %collective-permute-start.41 = (bf16[8,96,384]{2,1,0:T(8,128)(2,1)S(1)}, bf16[8,96,384]{2,1,0:T(8,128)(2,1)S(1)}, u32[]{:S(2)}, u32[]{:S(2)}) collective-permute-start(bf16[8,96,384]{2,1,0:T(8,128)(2,1)S(1)} %get-tuple-element.413), channel_id=1, source_target_pairs={{0,2},{1,3},{2,0},{3,1},{4,6},{5,7},{6,4},{7,5},{8,10},{9,11},{10,... | collective-permute-start | bytes 1769480 | tf_op jit(solution)/shard_map/ppermute | solution.py:338
  127.7 15.1 %collective-permute-start.40 = (bf16[8,96,384]{2,1,0:T(8,128)(2,1)S(1)}, bf16[8,96,384]{2,1,0:T(8,128)(2,1)S(1)}, u32[]{:S(2)}, u32[]{:S(2)}) collective-permute-start(bf16[8,96,384]{2,1,0:T(8,128)(2,1)S(1)} %get-tuple-element.414), channel_id=1, source_target_pairs={{0,4},{1,5},{2,6},{3,7},{4,0},{5,1},{6,2},{7,3},{8,12},{9,13},{10,... | collective-permute-start | bytes 1769480 | tf_op jit(solution)/shard_map/ppermute | solution.py:338
  159.0 19.5 %collective-permute-start.47 = (bf16[8,24,1920]{2,1,0:T(8,128)(2,1)S(1)}, bf16[8,24,1920]{2,1,0:T(8,128)(2,1)}, u32[]{:S(2)}, u32[]{:S(2)}) collective-permute-start(bf16[8,24,1920]{2,1,0:T(8,128)(2,1)S(1)} %get-tuple-element.409), channel_id=1, source_target_pairs={{0,2},{1,3},{2,0},{3,1},{4,6},{5,7},{6,4},{7,5},{8,10},{9,11},{10,... | collective-permute-start | bytes 2211848 | tf_op jit(solution)/shard_map/ppermute | solution.py:338
  160.1 18.5 %collective-permute-start.46 = (bf16[8,24,1920]{2,1,0:T(8,128)(2,1)S(1)}, bf16[8,24,1920]{2,1,0:T(8,128)(2,1)}, u32[]{:S(2)}, u32[]{:S(2)}) collective-permute-start(bf16[8,24,1920]{2,1,0:T(8,128)(2,1)S(1)} %get-tuple-element.410), channel_id=1, source_target_pairs={{0,4},{1,5},{2,6},{3,7},{4,0},{5,1},{6,2},{7,3},{8,12},{9,13},{10,... | collective-permute-start | bytes 2211848 | tf_op jit(solution)/shard_map/ppermute | solution.py:338
  161.9 16.6 %collective-permute-start.48 = (bf16[2,128,768]{2,1,0:T(8,128)(2,1)S(1)}, bf16[2,128,768]{2,1,0:T(8,128)(2,1)S(1)}, u32[]{:S(2)}, u32[]{:S(2)}) collective-permute-start(bf16[2,128,768]{2,1,0:T(8,128)(2,1)S(1)} %bitcast.134), channel_id=1, source_target_pairs={{0,1},{1,0},{2,3},{3,2},{4,5},{5,4},{6,7},{7,6},{8,9},{9,8},{10,11... | collective-permute-start | bytes 1179656 | tf_op jit(solution)/shard_map/ppermute | solution.py:338
  162.1 16.5 %collective-permute-start.45 = (bf16[2,96,768]{2,1,0:T(8,128)(2,1)S(1)}, bf16[2,96,768]{2,1,0:T(8,128)(2,1)S(1)}, u32[]{:S(2)}, u32[]{:S(2)}) collective-permute-start(bf16[2,96,768]{2,1,0:T(8,128)(2,1)S(1)} %get-tuple-element.427), channel_id=1, source_target_pairs={{0,8},{1,9},{2,10},{3,11},{4,12},{5,13},{6,14},{7,15},{8,0},{9,1},... | collective-permute-start | bytes 884744 | tf_op jit(solution)/shard_map/ppermute | solution.py:338
  179.4 16.4 %collective-permute-start.52 = (bf16[16,24,2304]{2,1,0:T(8,128)(2,1)}, bf16[16,24,2304]{2,1,0:T(8,128)(2,1)}, u32[]{:S(2)}, u32[]{:S(2)}) collective-permute-start(bf16[16,24,2304]{2,1,0:T(8,128)(2,1)} %get-tuple-element.335), channel_id=1, source_target_pairs={{0,1},{1,0},{2,3},{3,2},{4,5},{5,4},{6,7},{7,6},{8,9},{9,8},{10,11... | collective-permute-start | bytes 5308424 | tf_op jit(solution)/shard_map/ppermute | solution.py:338
  201.7 13.3 %collective-permute-start.56 = (bf16[8,24,1280]{2,1,0:T(8,128)(2,1)S(1)}, bf16[8,24,1280]{2,1,0:T(8,128)(2,1)S(1)}, u32[]{:S(2)}, u32[]{:S(2)}) collective-permute-start(bf16[8,24,1280]{2,1,0:T(8,128)(2,1)S(1)} %get-tuple-element.419), channel_id=1, source_target_pairs={{0,2},{1,3},{2,0},{3,1},{4,6},{5,7},{6,4},{7,5},{8,10},{9,11},{10,... | collective-permute-start | bytes 1474568 | tf_op jit(solution)/shard_map/ppermute | solution.py:338
  215.1 13.4 %collective-permute-start.58 = (bf16[4,24,1152]{2,1,0:T(8,128)(2,1)S(1)}, bf16[4,24,1152]{2,1,0:T(8,128)(2,1)S(1)}, u32[]{:S(2)}, u32[]{:S(2)}) collective-permute-start(bf16[4,24,1152]{2,1,0:T(8,128)(2,1)S(1)} %get-tuple-element.439), channel_id=1, source_target_pairs={{0,2},{1,3},{2,0},{3,1},{4,6},{5,7},{6,4},{7,5},{8,10},{9,11},{10,... | collective-permute-start | bytes 663560 | tf_op jit(solution)/shard_map/ppermute | solution.py:338
  216.4 13.8 %collective-permute-start.61 = (bf16[2,128,768]{2,1,0:T(8,128)(2,1)S(1)}, bf16[2,128,768]{2,1,0:T(8,128)(2,1)S(1)}, u32[]{:S(2)}, u32[]{:S(2)}) collective-permute-start(bf16[2,128,768]{2,1,0:T(8,128)(2,1)S(1)} %get-tuple-element.379), channel_id=1, source_target_pairs={{0,2},{1,3},{2,0},{3,1},{4,6},{5,7},{6,4},{7,5},{8,10},{9,11},{10,... | collective-permute-start | bytes 1179656 | tf_op jit(solution)/shard_map/ppermute | solution.py:338
  230.2 14.8 %collective-permute-start.65 = (bf16[2,128,768]{2,1,0:T(8,128)(2,1)S(1)}, bf16[2,128,768]{2,1,0:T(8,128)(2,1)S(1)}, u32[]{:S(2)}, u32[]{:S(2)}) collective-permute-start(bf16[2,128,768]{2,1,0:T(8,128)(2,1)S(1)} %get-tuple-element.393), channel_id=1, source_target_pairs={{0,2},{1,3},{2,0},{3,1},{4,6},{5,7},{6,4},{7,5},{8,10},{9,11},{10,... | collective-permute-start | bytes 1179656 | tf_op jit(solution)/shard_map/ppermute | solution.py:338
  (78 other events, 477.2 us)
